TPU v7x, 32 devices: a whole 2x2x4 slice. The times are simulated.
32 devices in a mesh: wide: 8 (over z, x), narrow: 4 (over y, core).
Axes of the slice: x: 2, y: 2, z: 4, core: 2. Of those that a mesh axis runs over, the one named last changes fastest.
Arguments:
- tokens: bfloat16 [2048, 128, 256], P(('wide', 'narrow')), may hold values from -6 to 6
- visible_index: int32 [2048, 112], P(('wide', 'narrow')), may hold values from 0 to 127, as said below
- visible_count: int32 [2048], P(('wide', 'narrow')), may hold values from 8 to 112, as said below
- ln1_gain: bfloat16 [256], replicated, may hold values from 0.5 to 1.5
- ln1_bias: bfloat16 [256], replicated, may hold values from -1.1953125 to 1.1953125
- qkv_weight: bfloat16 [256, 768], replicated, may hold values from -0.375 to 0.375
- query_bias: bfloat16 [256], replicated, may hold values from -1.796875 to 1.796875
- value_bias: bfloat16 [256], replicated, may hold values from -1.796875 to 1.796875
- out_weight: bfloat16 [256, 256], replicated, may hold values from -1.5 to 1.5
- out_bias: bfloat16 [256], replicated, may hold values from -1.1953125 to 1.1953125
- ln2_gain: bfloat16 [256], replicated, may hold values from 0.5 to 1.5
- ln2_bias: bfloat16 [256], replicated, may hold values from -1.1953125 to 1.1953125
- up_weight: bfloat16 [256, 1024], replicated, may hold values from -0.375 to 0.375
- up_bias: bfloat16 [1024], replicated, may hold values from -1.796875 to 1.796875
- down_weight: bfloat16 [1024, 256], replicated, may hold values from -0.375 to 0.375
- down_bias: bfloat16 [256], replicated, may hold values from -1.1953125 to 1.1953125
- out_grad: bfloat16 [2048, 112, 256], P(('wide', 'narrow')), may hold values from -6 to 6
Outputs:
- layer_out: bfloat16 [2048, 112, 256], P(('wide', 'narrow'))
- tokens_grad: bfloat16 [2048, 128, 256], P(('wide', 'narrow'))
- ln1_gain_grad: float32 [256], replicated
- ln1_bias_grad: float32 [256], replicated
- qkv_weight_grad: float32 [256, 768], replicated
- query_bias_grad: float32 [256], replicated
- value_bias_grad: float32 [256], replicated
- out_weight_grad: float32 [256, 256], replicated
- out_bias_grad: float32 [256], replicated
- ln2_gain_grad: float32 [256], replicated
- ln2_bias_grad: float32 [256], replicated
- up_weight_grad: float32 [256, 1024], replicated
- up_bias_grad: float32 [1024], replicated
- down_weight_grad: float32 [1024, 256], replicated
- down_bias_grad: float32 [256], replicated
Inputs may be any that keep to these rules, and one draw needn't show every extreme that they name: `visible_index`: the entries of a row are distinct positions; entries at or beyond the row's visible count are not used. `visible_count`: in every block of 64 trajectories (those of one device) one trajectory has exactly 112.
All inputs are finite; a program needn't handle non-finite values.
Results may differ from a plain program's by a relative error of at most 0.012.
Values sent between devices are 32-bit elements; how exact they have to be, the bound alone decides.
No kernel may reach another device: no remote copies, remote signals or barrier semaphores. Data moves between devices by JAX's collectives and lax.ppermute only.
A program may use at most 256 MiB of HBM per device.

v0:
```python
from functools import partial

import jax
import jax.numpy as jnp
from jax import lax
from jax.sharding import PartitionSpec as P

HEADS = 4


def normalize(rows):
    centered = rows - jnp.mean(rows, axis=-1, keepdims=True)
    spread = jnp.mean(centered * centered, axis=-1, keepdims=True)
    return centered * lax.rsqrt(spread + 1e-05)


def norm_affine(rows, gain_f, bias_f):
    return normalize(rows) * gain_f + bias_f


def total_grads(grads):
    inner = lax.psum(grads, "narrow")
    return lax.psum(inner, "wide")


def attention_probs(queries, key_rows, key_usable, score_scale, top_score, total_mass):
    scores = (
        jnp.einsum("thqe,thke->thqk", queries, key_rows, preferred_element_type=jnp.float32)
        * score_scale
    )
    scores = jnp.where(key_usable, scores, -1e30)
    return jnp.exp(scores - top_score) / total_mass


def body(
    tokens,
    visible_index,
    visible_count,
    ln1_gain,
    ln1_bias,
    qkv_weight,
    query_bias,
    value_bias,
    out_weight,
    out_bias,
    ln2_gain,
    ln2_bias,
    up_weight,
    up_bias,
    down_weight,
    down_bias,
    out_grad,
):
    traj_count, slots = visible_index.shape
    seq_len = tokens.shape[1]
    width = tokens.shape[2]
    head_size = width // HEADS
    score_scale = head_size ** (-0.5)
    row_count = traj_count * slots
    usable = (
        lax.broadcasted_iota(jnp.int32, (traj_count, slots), 1) < visible_count[:, None]
    ).astype(jnp.float32)
    row_usable = usable.reshape(row_count, 1)
    token_selector = (
        visible_index[:, :, None]
        == lax.broadcasted_iota(jnp.int32, (traj_count, slots, seq_len), 2)
    ) & (usable[:, :, None] > 0)
    gathered = jnp.einsum(
        "ago,aow->agw",
        token_selector.astype(jnp.bfloat16),
        tokens,
        preferred_element_type=jnp.float32,
    ).reshape(row_count, width)
    first_f, first_pull = jax.vjp(
        norm_affine, gathered, ln1_gain.astype(jnp.float32), ln1_bias.astype(jnp.float32)
    )
    first_in = first_f.astype(jnp.bfloat16)
    bias_row = jnp.concatenate(
        [
            query_bias.astype(jnp.float32),
            jnp.zeros((width,), jnp.float32),
            value_bias.astype(jnp.float32),
        ]
    )
    qkv_low = (jnp.dot(first_in, qkv_weight, preferred_element_type=jnp.float32) + bias_row).astype(
        jnp.bfloat16
    )
    split_qkv = qkv_low.reshape(traj_count, slots, 3, HEADS, head_size).transpose(2, 0, 3, 1, 4)
    queries, key_rows, values = (split_qkv[0], split_qkv[1], split_qkv[2])
    key_usable = usable[:, None, None, :] > 0
    scores = (
        jnp.einsum("thqe,thke->thqk", queries, key_rows, preferred_element_type=jnp.float32)
        * score_scale
    )
    scores = jnp.where(key_usable, scores, -1e30)
    top_score = jnp.max(scores, axis=-1, keepdims=True)
    raised = jnp.exp(scores - top_score)
    total_mass = jnp.sum(raised, axis=-1, keepdims=True)
    probs_low = (raised / total_mass).astype(jnp.bfloat16)
    attended = jnp.einsum(
        "thqk,thke->thqe", probs_low, values, preferred_element_type=jnp.float32
    ).astype(jnp.bfloat16)
    attended = attended.transpose(0, 2, 1, 3).reshape(row_count, width)
    hidden_layer_rows = (
        gathered
        + jnp.dot(attended, out_weight, preferred_element_type=jnp.float32)
        + out_bias.astype(jnp.float32)
    )
    second_f, second_pull = jax.vjp(
        norm_affine, hidden_layer_rows, ln2_gain.astype(jnp.float32), ln2_bias.astype(jnp.float32)
    )
    second_in = second_f.astype(jnp.bfloat16)
    pre_act = jnp.dot(second_in, up_weight, preferred_element_type=jnp.float32) + up_bias.astype(
        jnp.float32
    )
    act_f, gelu_pull = jax.vjp(partial(jax.nn.gelu, approximate=True), pre_act)
    activated = act_f.astype(jnp.bfloat16)
    mlp_rows = jnp.dot(
        activated, down_weight, preferred_element_type=jnp.float32
    ) + down_bias.astype(jnp.float32)
    layer_out = (
        ((hidden_layer_rows + mlp_rows) * row_usable)
        .reshape(traj_count, slots, width)
        .astype(jnp.bfloat16)
    )
    incoming_output_gradient = out_grad.astype(jnp.float32).reshape(row_count, width) * row_usable
    grad_mlp = incoming_output_gradient.astype(jnp.bfloat16)
    down_w_grad = jnp.einsum("rf,rd->fd", activated, grad_mlp, preferred_element_type=jnp.float32)
    down_b_grad = jnp.sum(grad_mlp.astype(jnp.float32), axis=0)
    grad_act = jnp.einsum("rd,fd->rf", grad_mlp, down_weight, preferred_element_type=jnp.float32)
    preactivation_gradient = gelu_pull(grad_act)[0].astype(jnp.bfloat16)
    up_w_grad = jnp.einsum(
        "rd,rf->df", second_in, preactivation_gradient, preferred_element_type=jnp.float32
    )
    up_b_grad = jnp.sum(preactivation_gradient.astype(jnp.float32), axis=0)
    grad_second = jnp.einsum(
        "rf,df->rd", preactivation_gradient, up_weight, preferred_element_type=jnp.float32
    )
    grad_mid_norm, ln2_g_grad, ln2_c_grad = second_pull(grad_second)
    grad_mid = incoming_output_gradient + grad_mid_norm
    grad_branch = grad_mid.astype(jnp.bfloat16)
    out_w_grad = jnp.einsum("rc,rd->cd", attended, grad_branch, preferred_element_type=jnp.float32)
    out_b_grad = jnp.sum(grad_branch.astype(jnp.float32), axis=0)
    bucket_late = (
        ln2_g_grad,
        ln2_c_grad,
        up_w_grad,
        up_b_grad,
        down_w_grad,
        down_b_grad,
        out_w_grad,
        out_b_grad,
    )
    grad_att = jnp.einsum(
        "rd,cd->rc", grad_branch, out_weight, preferred_element_type=jnp.float32
    ).astype(jnp.bfloat16)
    grad_att = grad_att.reshape(traj_count, slots, HEADS, head_size).transpose(0, 2, 1, 3)
    probs_again = attention_probs(queries, key_rows, key_usable, score_scale, top_score, total_mass)
    probs_low = probs_again.astype(jnp.bfloat16)
    probability_gradient = jnp.einsum(
        "thqe,thke->thqk", grad_att, values, preferred_element_type=jnp.float32
    )
    value_grad = jnp.einsum(
        "thqk,thqe->thke", probs_low, grad_att, preferred_element_type=jnp.float32
    )
    row_delta = jnp.sum(probs_again * probability_gradient, axis=-1, keepdims=True)
    grad_scores = (probs_again * (probability_gradient - row_delta)).astype(jnp.bfloat16)
    query_grad = (
        jnp.einsum("thqk,thke->thqe", grad_scores, key_rows, preferred_element_type=jnp.float32)
        * score_scale
    )
    key_grad = (
        jnp.einsum("thqk,thqe->thke", grad_scores, queries, preferred_element_type=jnp.float32)
        * score_scale
    )
    grad_qkv = jnp.stack((query_grad, key_grad, value_grad), axis=0).transpose(1, 3, 0, 2, 4)
    grad_qkv = grad_qkv.reshape(row_count, 3 * width).astype(jnp.bfloat16)
    qkv_w_grad = jnp.einsum("rd,rk->dk", first_in, grad_qkv, preferred_element_type=jnp.float32)
    qkv_b_grad = jnp.sum(grad_qkv.astype(jnp.float32), axis=0)
    grad_first = jnp.einsum("rk,dk->rd", grad_qkv, qkv_weight, preferred_element_type=jnp.float32)
    grad_gather_norm, ln1_g_grad, ln1_c_grad = first_pull(grad_first)
    gathered_token_gradient = ((grad_mid + grad_gather_norm) * row_usable).reshape(
        traj_count, slots, width
    )
    tokens_grad = jnp.einsum(
        "gjo,gjy->goy",
        token_selector.astype(jnp.float32),
        gathered_token_gradient,
        precision=lax.Precision.HIGHEST,
        preferred_element_type=jnp.float32,
    ).astype(jnp.bfloat16)
    bucket_first = (ln1_g_grad, ln1_c_grad, qkv_w_grad, qkv_b_grad[:width], qkv_b_grad[2 * width :])
    summed_late = total_grads(bucket_late)
    summed_first = total_grads(bucket_first)
    return (
        layer_out,
        tokens_grad,
        summed_first[0],
        summed_first[1],
        summed_first[2],
        summed_first[3],
        summed_first[4],
        summed_late[6],
        summed_late[7],
        summed_late[0],
        summed_late[1],
        summed_late[2],
        summed_late[3],
        summed_late[4],
        summed_late[5],
    )


def solution(mesh):
    placed = (
        P(("wide", "narrow"), None, None),
        P(("wide", "narrow"), None),
        P(("wide", "narrow")),
        P(),
        P(),
        P(),
        P(),
        P(),
        P(),
        P(),
        P(),
        P(),
        P(),
        P(),
        P(),
        P(),
        P(("wide", "narrow"), None, None),
    )
    return jax.shard_map(
        body,
        mesh=mesh,
        in_specs=placed,
        out_specs=(
            P(("wide", "narrow"), None, None),
            P(("wide", "narrow"), None, None),
            P(),
            P(),
            P(),
            P(),
            P(),
            P(),
            P(),
            P(),
            P(),
            P(),
            P(),
            P(),
            P(),
        ),
        check_vma=False,
    )
```

profile of v0, /device:TPU:0, one launch (start us, length us, event | category | flops | bytes accessed | tf_op | source)
XLA Modules:
  0.0 619.4 jit_solution(15957954562696982090)
XLA Ops:
  7.2 0.8 fusion.51
  8.0 7.0 %fusion.65 = (f32[64,112]{1,0:T(8,128)S(1)}, f32[64,112,256]{2,1,0:T(8,128)}) fusion(bf16[64,128,256]{2,1,0:T(8,128)(2,1)} %param.17, s32[64,112]{1,0:T(8,128)} %param.18, pred[64,112]{1,0:T(8,128)(4,1)S(1)} %get-tuple-element.62), kind=kOutput, calls=%fused_computation.103 | convolution fusion | flops 473424896 | bytes 11598848 | tf_op jit(solution)/shard_map/ago,aow->agw/dot_general | solution.py:68
  15.1 0.1 div.51
  15.2 4.3 multiply_reduce_fusion.6
  19.5 0.6 fusion.55
  20.1 0.1 add.149
  20.3 5.1 bitcast_subtract_fusion
  25.5 2.8 copy-done.4
  28.3 0.1 copy-done.32
  28.4 7.6 %add_convert_fusion = bf16[7168,768]{1,0:T(8,128)(2,1)} fusion(bf16[256,768]{1,0:T(8,128)(2,1)S(1)} %copy-done.19, f32[768]{0:T(1024)S(1)} %pad_maximum_fusion, f32[7168,256]{1,0:T(8,128)S(1)} %bitcast_subtract_fusion, f32[256]{0:T(256)S(1)} %convert_element_type.136, f32[256]{0:T(256)S(1)} %convert_element_type.135, f32[7168]{0:T(1024)S(1)} %rsqrt.23), kind=kOutput, calls=%fused_computation.14 | convolution fusion | flops 2836922368 | bytes 18777088 | tf_op jit(solution)/shard_map/dot_general | solution.py:85
  36.0 31.8 %reshape.234 = bf16[64,112,3,4,64]{4,3,2,1,0:T(4,128)(2,1)} reshape(bf16[7168,768]{1,0:T(8,128)(2,1)} %add_convert_fusion) | data formatting | bytes 22020096 | tf_op jit(solution)/shard_map/reshape | solution.py:88
  67.8 29.5 %copy.39 = bf16[64,112,3,4,64]{1,4,3,0,2:T(8,128)(2,1)} copy(bf16[64,112,3,4,64]{4,3,2,1,0:T(4,128)(2,1)} %reshape.234) | data formatting | bytes 22020096 | tf_op jit(solution)/shard_map/reshape | solution.py:88
  97.2 10.7 %fusion.22 = f32[64,4,112,112]{2,3,1,0:T(8,128)} fusion(bf16[3,64,4,112,64]{3,4,2,1,0:T(8,128)(2,1)} %bitcast.87), kind=kOutput, calls=%fused_computation.61 | convolution fusion | flops 411041792 | bytes 21233664 | tf_op jit(solution)/shard_map/thqe,thke->thqk/dot_general | solution.py:92
  108.0 11.2 %fusion.66 = (f32[64,4,112]{2,1,0:T(4,128)S(1)}, f32[64,4,112,112]{2,3,1,0:T(8,128)}) fusion(f32[64,4,112,112]{2,3,1,0:T(8,128)} %fusion.22, pred[64,112]{1,0:T(8,128)(4,1)S(1)} %get-tuple-element.62), kind=kOutput, calls=%fused_computation.104 | output fusion | flops 12845167 | bytes 25811968 | tf_op jit(solution)/shard_map/sub | solution.py:97
  119.2 11.7 %convert_bitcast_fusion = bf16[64,112,4,64]{1,3,2,0:T(8,128)(2,1)} fusion(bf16[3,64,4,112,64]{3,4,2,1,0:T(8,128)(2,1)} %bitcast.88, f32[64,4,112]{2,1,0:T(4,128)S(1)} %get-tuple-element.65, f32[64,4,112,112]{2,3,1,0:T(8,128)} %fusion.22, pred[64,112]{1,0:T(8,128)(4,1)S(1)} %get-tuple-element.62), kind=kOutput, calls=%fused_computation.57 | convolution fusion | flops 428961888 | bytes 22666240 | tf_op jit(solution)/shard_map/thqk,thke->thqe/dot_general | solution.py:100
  130.9 6.9 %copy.41 = bf16[64,112,4,64]{1,0,3,2:T(8,128)(2,1)} copy(bf16[64,112,4,64]{1,3,2,0:T(8,128)(2,1)} %convert_bitcast_fusion) | data formatting | bytes 7340032 | tf_op jit(solution)/shard_map/convert_element_type | solution.py:102
  137.8 9.0 %reshape.229 = bf16[7168,256]{0,1:T(8,128)(2,1)} reshape(bf16[64,112,4,64]{1,0,3,2:T(8,128)(2,1)} %copy.41) | data formatting | bytes 7340032 | tf_op jit(solution)/shard_map/reshape | solution.py:103
  146.8 6.4 %fusion.67 = (f32[7168]{0:T(1024)S(1)}, f32[7168,256]{1,0:T(8,128)S(1)}) fusion(f32[256]{0:T(256)S(1)} %convert_element_type.144, f32[7168,256]{1,0:T(8,128)} %bitcast.86, bf16[7168,256]{0,1:T(8,128)(2,1)} %reshape.229, bf16[256,256]{1,0:T(8,128)(2,1)S(1)} %copy-done.17), kind=kOutput, calls=%fused_computation.105 | convolution fusion | flops 945021952 | bytes 18510848 | tf_op jit(solution)/shard_map/dot_general | solution.py:106
  153.3 2.9 copy-done.1
  156.2 4.3 multiply_reduce_fusion.5
  160.6 0.1 reshape.233
  160.7 4.6 fusion.17
  165.4 11.6 %fusion.58 = f32[7168,1024]{1,0:T(8,128)} fusion(bf16[256,1024]{1,0:T(8,128)(2,1)S(1)} %copy-done.14, f32[7168,256]{1,0:T(8,128)S(1)} %copy-done.2, f32[256]{0:T(256)S(1)} %convert_element_type.146, f32[256]{0:T(256)S(1)} %convert_element_type.145, f32[7168]{0:T(1024)S(1)} %fusion.52, f32[7168]{0:T(1024)S(1)} %broadcast_multiply_fusion.1), kind=kOutput, calls=%fused_computation.99 | convolution fusion | flops 3767271424 | bytes 37283840 | tf_op jit(solution)/shard_map/dot_general | solution.py:113
  177.0 30.4 %convert_reduce_fusion = (f32[1024]{0:T(1024)}, bf16[7168,1024]{1,0:T(8,128)(2,1)}, bf16[7168,1024]{1,0:T(8,128)(2,1)}) fusion(f32[7168,1024]{1,0:T(8,128)} %fusion.58, f32[1024]{0:T(1024)S(1)} %convert_element_type.148, bf16[7168,256]{1,0:T(8,128)(2,1)S(1)} %fusion.17, bf16[1024,256]{1,0:T(8,128)(2,1)S(1)} %copy-done), kind=kOutput, calls=%fused_computation.10 | convolution fusion | flops 3941596160 | bytes 62922752 | tf_op jit(solution)/shard_map/rd,fd->rf/dot_general | solution.py:130
  207.4 11.6 %fusion.57 = f32[256,1024]{1,0:T(8,128)} fusion(bf16[7168,1024]{1,0:T(8,128)(2,1)} %get-tuple-element.49, f32[7168,256]{1,0:T(8,128)S(1)} %copy-done.2, f32[256]{0:T(256)S(1)} %convert_element_type.146, f32[256]{0:T(256)S(1)} %convert_element_type.145, f32[7168]{0:T(1024)S(1)} %fusion.52, f32[7168]{0:T(1024)S(1)} %broadcast_multiply_fusion.1), kind=kOutput, calls=%fused_computation.98 | convolution fusion | flops 3767271424 | bytes 23128064 | tf_op jit(solution)/shard_map/rd,rf->df/dot_general | solution.py:132
  219.0 13.8 %multiply_reduce_fusion.1 = (f32[256]{0:T(256)S(1)}, f32[7168]{0:T(1024)S(1)}, f32[256]{0:T(256)S(1)}, f32[7168,256]{1,0:T(8,128)}) fusion(f32[7168,256]{1,0:T(8,128)S(1)} %copy-done.2, f32[7168]{0:T(1024)S(1)} %fusion.52, f32[7168]{0:T(1024)S(1)} %broadcast_multiply_fusion.1, f32[256]{0:T(256)S(1)} %convert_element_type.145, ...), kind=kOutput, calls=%fused_computation.36 | convolution fusion | flops 3772768768 | bytes 29973504 | tf_op jit(solution)/shard_map/rf,df->rd/dot_general | solution.py:136
  232.8 8.7 %fusion.63 = (f32[7168]{0:T(1024)S(1)}, f32[7168,256]{1,0:T(8,128)S(1)}) fusion(f32[7168]{0:T(1024)S(1)} %multiply_multiply_fusion.3, f32[7168,256]{1,0:T(8,128)S(1)} %copy-done.2, f32[7168]{0:T(1024)S(1)} %broadcast_multiply_fusion.1, f32[7168]{0:T(1024)S(1)} %fusion.52, f32[7168,256]{1,0:T(8,128)} %get-tuple-element.69, f32[256]{0:T(256)S(1)} %convert_element_type.145), kind=kLoop, calls=%fused_computation.101 | loop fusion | flops 12837888 | bytes 22135808 | tf_op jit(solution)/shard_map/transpose(jvp())/reduce_sum | solution.py:12
  241.6 3.7 convert_reduce_fusion.3
  245.3 1.8 copy-done.8
  247.1 3.0 convolution_convert_fusion
  250.1 6.0 copy.42
  256.1 8.9 %reshape.231 = bf16[64,112,4,64]{1,0,3,2:T(8,128)(2,1)} reshape(bf16[7168,256]{0,1:T(8,128)(2,1)} %copy.42) | data formatting | bytes 7340032 | tf_op jit(solution)/shard_map/reshape | solution.py:157
  265.0 22.5 %multiply_reduce_fusion = (f32[64,4,112]{2,1,0:T(4,128)S(1)}, f32[64,4,112,112]{2,3,1,0:T(8,128)}) fusion(f32[64,4,112,112]{2,3,1,0:T(8,128)} %get-tuple-element.66, f32[64,4,112]{2,1,0:T(4,128)S(1)} %get-tuple-element.65, bf16[3,64,4,112,64]{3,4,2,1,0:T(8,128)(2,1)} %bitcast.89, bf16[64,4,112,64]{2,0,3,1:T(8,128)(2,1)} %bitcast.95), kind=kOutput, calls=%fused_computation.16 | convolution fusion | flops 420646912 | bytes 36143104 | tf_op jit(solution)/shard_map/thqe,thke->thqk/dot_general | solution.py:160
  287.6 10.8 %multiply_convert_fusion.1 = bf16[64,4,112,112]{2,3,1,0:T(8,128)(2,1)S(1)} fusion(f32[64,4,112,112]{2,3,1,0:T(8,128)} %get-tuple-element.71, f32[64,4,112]{2,1,0:T(4,128)S(1)} %get-tuple-element.70, f32[64,4,112,112]{2,3,1,0:T(8,128)} %get-tuple-element.66, f32[64,4,112]{2,1,0:T(4,128)S(1)} %get-tuple-element.65), kind=kLoop, calls=%fused_computation.15 | loop fusion | flops 12845056 | bytes 32342016 | tf_op jit(solution)/shard_map/convert_element_type | solution.py:167
  298.4 3.0 copy-done.6
  301.4 6.2 %multiply_bitcast_fusion.1 = bf16[1,64,4,112,64]{3,4,2,1,0:T(8,128)(2,1)} fusion(bf16[64,4,112,112]{2,3,1,0:T(8,128)(2,1)S(1)} %multiply_convert_fusion.1, bf16[3,64,4,112,64]{3,4,2,1,0:T(8,128)(2,1)} %bitcast.90), kind=kOutput, calls=%fused_computation.31 | convolution fusion | flops 414711808 | bytes 14286848 | tf_op jit(solution)/shard_map/thqk,thke->thqe/dot_general | solution.py:169
  307.6 11.0 %multiply_bitcast_fusion = bf16[1,64,4,112,64]{3,4,2,1,0:T(8,128)(2,1)} fusion(bf16[64,4,112,112]{2,3,1,0:T(8,128)(2,1)} %copy-done.6, bf16[3,64,4,112,64]{3,4,2,1,0:T(8,128)(2,1)} %bitcast.91), kind=kOutput, calls=%fused_computation.30 | convolution fusion | flops 414711808 | bytes 15204352 | tf_op jit(solution)/shard_map/thqk,thqe->thke/dot_general | solution.py:173
  318.6 12.6 %fusion.37 = bf16[1,64,4,112,64]{3,4,2,1,0:T(8,128)(2,1)} fusion(bf16[64,4,112,64]{2,0,3,1:T(8,128)(2,1)} %bitcast.96, f32[64,4,112]{2,1,0:T(4,128)S(1)} %get-tuple-element.65, f32[64,4,112,112]{2,3,1,0:T(8,128)} %fusion.22, pred[64,112]{1,0:T(8,128)(4,1)S(1)} %copy-done.24), kind=kOutput, calls=%fused_computation.75 | convolution fusion | flops 427126880 | bytes 20306944 | tf_op jit(solution)/shard_map/thqk,thqe->thke/dot_general | solution.py:163
  331.2 5.1 fusion.69
  336.3 0.6 copy-done.12
  336.9 1.2 copy-done.13
  338.1 7.3 %convert_reduce_fusion.1 = (f32[3,4,64]{2,1,0:T(4,128)S(1)}, bf16[64,112,3,4,64]{1,4,3,0,2:T(8,128)(2,1)S(1)}) fusion(bf16[1,64,4,112,64]{3,4,2,1,0:T(8,128)(2,1)S(1)} %copy-done.13, bf16[1,64,4,112,64]{3,4,2,1,0:T(8,128)(2,1)S(1)} %copy-done.12, bf16[1,64,4,112,64]{3,4,2,1,0:T(8,128)(2,1)S(1)} %copy-done.11), kind=kLoop, calls=%fused_computation.13 | loop fusion | flops 22019328 | bytes 22023168 | tf_op jit(solution)/shard_map/reduce_sum | solution.py:179
  345.4 9.0 %copy.48 = bf16[64,112,3,4,64]{1,0,4,3,2:T(8,128)(2,1)} copy(bf16[64,112,3,4,64]{1,4,3,0,2:T(8,128)(2,1)S(1)} %get-tuple-element.53) | data formatting | bytes 22020096 | tf_op jit(solution)/shard_map/convert_element_type | solution.py:177
  354.4 24.5 %convert_element_type.163 = bf16[7168,768]{0,1:T(8,128)(2,1)} reshape(bf16[64,112,3,4,64]{1,0,4,3,2:T(8,128)(2,1)} %copy.48) | data formatting | bytes 22020096 | tf_op jit(solution)/shard_map/convert_element_type | solution.py:177
  378.9 5.6 add_convert_fusion.1
  384.6 8.5 %fusion.70 = f32[1024,256]{1,0:T(8,128)} fusion(bf16[7168,1024]{1,0:T(8,128)(2,1)} %get-tuple-element.56, bf16[7168,256]{1,0:T(8,128)(2,1)S(1)} %copy-done.10), kind=kOutput, calls=%fused_computation.108 | convolution fusion | flops 3758096384 | bytes 19398656 | tf_op jit(solution)/shard_map/rf,rd->fd/dot_general | solution.py:128
  393.1 3.9 fusion.68
  397.1 0.0 all-reduce.7.cloned.1.call-start
  397.2 10.7 %fusion.59 = (f32[256]{0:T(256)S(1)}, f32[7168]{0:T(1024)S(1)}, f32[7168,256]{1,0:T(8,128)S(1)}) fusion(f32[7168,256]{1,0:T(8,128)} %copy-done.4, f32[256]{0:T(256)S(1)} %copy-done.33, bf16[7168,768]{0,1:T(8,128)(2,1)} %convert_element_type.163, bf16[256,768]{1,0:T(8,128)(2,1)S(1)} %copy-done.20), kind=kOutput, calls=%fused_computation.100 | convolution fusion | flops 2825904896 | bytes 26114048 | tf_op jit(solution)/shard_map/rk,dk->rd/dot_general | solution.py:180
  408.0 8.7 %multiply_reduce_fusion.2 = (f32[256]{0:T(256)S(1)}, f32[7168]{0:T(1024)S(1)}) fusion(f32[7168,256]{1,0:T(8,128)S(1)} %get-tuple-element.72, f32[7168,256]{1,0:T(8,128)} %copy-done.4, f32[7168]{0:T(1024)S(1)} %copy-done.26, f32[7168]{0:T(1024)S(1)} %multiply_multiply_fusion.2, f32[256]{0:T(256)S(1)} %copy-done.33), kind=kLoop, calls=%fused_computation.39 | loop fusion | flops 16507648 | bytes 14768128 | tf_op jit(solution)/shard_map/transpose(jvp())/reduce_sum | solution.py:18
  416.8 52.2 %all-reduce.9.cloned.1.call-done = (f32[256,768]{1,0:T(8,128)}, f32[256,256]{1,0:T(8,128)}, f32[256,1024]{1,0:T(8,128)}, f32[1024,256]{1,0:T(8,128)}) async-done(((f32[256,768]{1,0:T(8,128)}, f32[256,256]{1,0:T(8,128)}, f32[256,1024]{1,0:T(8,128)}, f32[1024,256]{1,0:T(8,128)}), (f32[256,768]{1,0:T(8,128)}, f32[256,256]{1,0:T(8,128)}, f32[256,1024]{1,0:T(8,128)}, ...) | async-done | bytes 3145744 | tf_op jit(solution)/shard_map/psum | solution.py:22
  469.1 12.9 %add_multiply_fusion = f32[7168,256]{1,0:T(8,128)} fusion(f32[7168,256]{1,0:T(8,128)} %copy-done.5, bf16[64,112,256]{2,1,0:T(8,128)(2,1)} %param.33, f32[7168]{0:T(1024)S(1)} %negate_multiply_fusion, f32[7168]{0:T(1024)S(1)} %negate_multiply_fusion.1, f32[7168]{0:T(1024)S(1)} %reshape.233, f32[7168]{0:T(1024)S(1)} %multiply_multiply_fusion.2, ...), kind=kLoop, calls=%fused_computation.40 | loop fusion | flops 23855104 | bytes 33203200 | tf_op jit(solution)/shard_map/mul | solution.py:182
  482.0 0.1 slice.25
  482.0 0.1 slice.27
  482.1 2.6 convert_reduce_fusion.2
  484.8 10.9 %all-reduce.2 = (f32[256]{0:T(256)S(1)}, f32[256]{0:T(256)S(1)}, f32[256]{0:T(256)S(1)}, f32[256]{0:T(256)S(1)}, f32[256]{0:T(256)S(1)}, /*index=5*/f32[256]{0:T...) all-reduce(f32[256]{0:T(256)S(1)} %get-tuple-element.17, ...), channel_id=1, replica_groups=mesh['wide'=8,'narrow'=4] {'narrow'}, use_global_device_ids=true, to_apply=%region_12.13 | all-reduce | flops 3072 | bytes 24576 | tf_op jit(solution)/shard_map/psum | solution.py:22
  495.7 38.2 %all-reduce = (f32[256]{0:T(256)}, f32[256]{0:T(256)}, f32[256]{0:T(256)}, f32[256]{0:T(256)}, f32[256]{0:T(256)}, /*index=5*/f32[256]{0:T(256)}, f32[256]{0:T(256)}, f32[1024]{0:T(1024)}, f32[256]{0:T(256)}) all-reduce(f32[256]{0:T(256)S(1)} %get-tuple-element.35, ...), channel_id=1, replica_groups=mesh['wide'=8,'narrow'=4] {'wide'}, use_global_device_ids=true, to_apply=%region_13.14 | all-reduce | flops 3072 | bytes 24576 | tf_op jit(solution)/shard_map/psum | solution.py:23
  533.9 9.3 %fusion.42 = bf16[64,128,256]{2,1,0:T(8,128)(2,1)} fusion(f32[64,112,256]{2,1,0:T(8,128)} %bitcast.92, s32[64,112]{1,0:T(8,128)S(1)} %copy-done.18, pred[64,112]{1,0:T(8,128)(4,1)S(1)} %copy-done.24), kind=kOutput, calls=%fused_computation.76 | convolution fusion | flops 2822504448 | bytes 11570176 | tf_op jit(solution)/shard_map/gjo,gjy->goy/dot_general | solution.py:185
  543.2 11.4 %fusion.13 = bf16[7168,256]{1,0:T(8,128)(2,1)} fusion(f32[7168,256]{1,0:T(8,128)} %copy-done.1, bf16[7168,1024]{1,0:T(8,128)(2,1)} %get-tuple-element.56, bf16[1024,256]{1,0:T(8,128)(2,1)S(1)} %copy-done, f32[7168]{0:T(1024)S(1)} %reshape.233, f32[256]{0:T(256)S(1)} %convert_element_type.150), kind=kOutput, calls=%fused_computation.29 | convolution fusion | flops 3765436416 | bytes 26244096 | tf_op jit(solution)/shard_map/dot_general | solution.py:118
  554.6 49.2 %all-reduce.7.cloned.1.call-done = (f32[256,768]{1,0:T(8,128)}, f32[256,256]{1,0:T(8,128)}, f32[256,1024]{1,0:T(8,128)}, f32[1024,256]{1,0:T(8,128)}) async-done(((f32[256,768]{1,0:T(8,128)}, f32[256,256]{1,0:T(8,128)}, f32[256,1024]{1,0:T(8,128)}, f32[1024,256]{1,0:T(8,128)}), (f32[256,768]{1,0:T(8,128)}, f32[256,256]{1,0:T(8,128)}, f32[256,1024]{1,0:T(8,128)}, ...) | async-done | bytes 3145744 | tf_op jit(solution)/shard_map/psum | solution.py:23
  603.8 2.1 copy.71
  605.9 1.7 copy.72
  607.5 2.3 copy.73
  609.8 2.3 copy.74
  (115 shorter events, 0.4 us)
Async XLA Ops:
  7.2 169.8 %copy-start = (bf16[1024,256]{1,0:T(8,128)(2,1)S(1)}, bf16[1024,256]{1,0:T(8,128)(2,1)}, u32[]{:S(2)}) copy-start(bf16[1024,256]{1,0:T(8,128)(2,1)} %param.31) | copy-start | bytes 1572868
  7.2 461.8 %all-reduce.9.cloned.1.call-start = ((), (), s32[]{:S(2)}) async-start(), calls=%async_computation.1 | async-start | bytes 6291456 | tf_op jit(solution)/shard_map/psum | solution.py:22
  8.0 111.2 %copy-start.23 = (pred[64,112]{1,0:T(8,128)(4,1)}, pred[64,112]{1,0:T(8,128)(4,1)S(1)}, u32[]{:S(2)}) copy-start(pred[64,112]{1,0:T(8,128)(4,1)S(1)} %get-tuple-element.62) | copy-start | bytes 21508
  8.0 152.6 %copy-start.21 = (f32[64,112]{1,0:T(8,128)}, f32[64,112]{1,0:T(8,128)S(1)}, u32[]{:S(2)}) copy-start(f32[64,112]{1,0:T(8,128)S(1)} %get-tuple-element.61) | copy-start | bytes 86020
  15.1 10.3 %copy-start.15 = (f32[64,112]{1,0:T(8,128)}, f32[64,112]{1,0:T(8,128)S(1)}, u32[]{:S(2)}) copy-start(f32[64,112]{1,0:T(8,128)S(1)} %broadcast_multiply_fusion) | copy-start | bytes 86020
  15.2 10.2 %copy-start.27 = (f32[7168]{0:T(1024)}, f32[7168]{0:T(1024)S(1)}, u32[]{:S(2)}) copy-start(f32[7168]{0:T(1024)S(1)} %div.51) | copy-start | bytes 86020
  20.2 5.2 copy-start.29
  20.2 5.3 copy-start.25
  20.2 5.2 copy-start.38
  20.2 5.2 copy-start.39
  20.3 5.2 copy-start.40
  20.3 5.2 copy-start.41
  20.3 8.1 %copy-start.19 = (bf16[256,768]{1,0:T(8,128)(2,1)S(1)}, bf16[256,768]{1,0:T(8,128)(2,1)}, u32[]{:S(2)}) copy-start(bf16[256,768]{1,0:T(8,128)(2,1)} %param.22) | copy-start | bytes 1179652
  25.4 2.9 copy-start.4
  25.4 2.9 copy-start.32
  25.5 2.9 copy-start.36
  130.9 15.9 %copy-start.42 = (bf16[256]{0:T(256)(128)(2,1)S(1)}, bf16[256]{0:T(256)(128)(2,1)}, u32[]{:S(2)}) copy-start(bf16[256]{0:T(256)(128)(2,1)} %param.26) | copy-start | bytes 1540
  130.9 15.9 %copy-start.17 = (bf16[256,256]{1,0:T(8,128)(2,1)S(1)}, bf16[256,256]{1,0:T(8,128)(2,1)}, u32[]{:S(2)}) copy-start(bf16[256,256]{1,0:T(8,128)(2,1)} %param.25) | copy-start | bytes 393220
  153.2 3.0 copy-start.1
  153.2 7.3 %copy-start.43 = (bf16[256]{0:T(256)(128)(2,1)S(1)}, bf16[256]{0:T(256)(128)(2,1)}, u32[]{:S(2)}) copy-start(bf16[256]{0:T(256)(128)(2,1)} %param.27) | copy-start | bytes 1540
  153.2 7.4 %copy-start.44 = (bf16[256]{0:T(256)(128)(2,1)S(1)}, bf16[256]{0:T(256)(128)(2,1)}, u32[]{:S(2)}) copy-start(bf16[256]{0:T(256)(128)(2,1)} %param.28) | copy-start | bytes 1540
  153.2 7.5 %copy-start.35 = (bf16[1024]{0:T(1024)(128)(2,1)S(1)}, bf16[1024]{0:T(1024)(128)(2,1)}, u32[]{:S(2)}) copy-start(bf16[1024]{0:T(1024)(128)(2,1)} %param.30) | copy-start | bytes 6148
  156.2 9.2 %copy-start.14 = (bf16[256,1024]{1,0:T(8,128)(2,1)S(1)}, bf16[256,1024]{1,0:T(8,128)(2,1)}, u32[]{:S(2)}) copy-start(bf16[256,1024]{1,0:T(8,128)(2,1)} %param.29) | copy-start | bytes 1572868
  160.7 4.7 copy-start.2
  165.4 11.6 %copy-start.9 = (bf16[7168,256]{1,0:T(8,128)(2,1)}, bf16[7168,256]{1,0:T(8,128)(2,1)S(1)}, u32[]{:S(2)}) copy-start(bf16[7168,256]{1,0:T(8,128)(2,1)S(1)} %fusion.17) | copy-start | bytes 11010052
  232.8 8.7 %copy-start.7 = (bf16[64,112,256]{2,1,0:T(8,128)(2,1)S(1)}, bf16[64,112,256]{2,1,0:T(8,128)(2,1)}, u32[]{:S(2)}) copy-start(bf16[64,112,256]{2,1,0:T(8,128)(2,1)} %param.33) | copy-start | bytes 11010052
  241.6 3.8 copy-start.5
  245.3 1.8 copy-start.8
  298.4 3.0 copy-start.6
  307.6 11.0 %copy-start.24 = (pred[64,112]{1,0:T(8,128)(4,1)S(1)}, pred[64,112]{1,0:T(8,128)(4,1)}, u32[]{:S(2)}) copy-start(pred[64,112]{1,0:T(8,128)(4,1)} %copy-done.23) | copy-start | bytes 21508
  331.1 5.1 copy-start.11
  331.2 5.7 copy-start.12
  331.2 6.9 %copy-start.13 = (bf16[1,64,4,112,64]{3,4,2,1,0:T(8,128)(2,1)S(1)}, bf16[1,64,4,112,64]{3,4,2,1,0:T(8,128)(2,1)}, u32[]{:S(2)}) copy-start(bf16[1,64,4,112,64]{3,4,2,1,0:T(8,128)(2,1)} %fusion.37) | copy-start | bytes 11010052
  354.4 24.5 %copy-start.16 = (f32[64,112]{1,0:T(8,128)S(1)}, f32[64,112]{1,0:T(8,128)}, u32[]{:S(2)}) copy-start(f32[64,112]{1,0:T(8,128)} %copy-done.15) | copy-start | bytes 86020
  354.4 24.5 %copy-start.31 = (f32[64,112]{1,0:T(8,128)S(1)}, f32[64,112]{1,0:T(8,128)}, u32[]{:S(2)}) copy-start(f32[64,112]{1,0:T(8,128)} %get-tuple-element.57) | copy-start | bytes 86020
  354.4 24.5 %copy-start.33 = (f32[256]{0:T(256)S(1)}, f32[256]{0:T(256)}, u32[]{:S(2)}) copy-start(f32[256]{0:T(256)} %copy-done.32) | copy-start | bytes 3076
  354.4 24.5 %copy-start.37 = (f32[256]{0:T(256)S(1)}, f32[256]{0:T(256)}, u32[]{:S(2)}) copy-start(f32[256]{0:T(256)} %copy-done.36) | copy-start | bytes 3076
  378.9 5.6 copy-start.10
  378.9 14.2 %slice-start = ((s8[11010048]{0:T(1024)(128)(4,1)}), s8[4194304]{0:T(1024)(128)(4,1)S(1)}, s32[]{:S(2)}) async-start(s8[11010048]{0:T(1024)(128)(4,1)} %bitcast.93), calls=%async_computation.2 | async-start | bytes 8388608
  384.6 8.6 %slice-start.1 = ((s8[11010048]{0:T(1024)(128)(4,1)}), s8[4194304]{0:T(1024)(128)(4,1)S(1)}, s32[]{:S(2)}) async-start(s8[11010048]{0:T(1024)(128)(4,1)} %bitcast.93), calls=%async_computation.3 | async-start | bytes 8388608
  384.6 8.5 %slice-start.2 = ((s8[11010048]{0:T(1024)(128)(4,1)}), s8[2621440]{0:T(1024)(128)(4,1)S(1)}, s32[]{:S(2)}) async-start(s8[11010048]{0:T(1024)(128)(4,1)} %bitcast.93), calls=%async_computation.4 | async-start | bytes 5242880
  393.1 4.1 copy-start.20
  397.1 10.8 %copy-start.30 = (f32[7168]{0:T(1024)S(1)}, f32[7168]{0:T(1024)}, u32[]{:S(2)}) copy-start(f32[7168]{0:T(1024)} %copy-done.29) | copy-start | bytes 86020
  397.1 10.9 %copy-start.26 = (f32[7168]{0:T(1024)S(1)}, f32[7168]{0:T(1024)}, u32[]{:S(2)}) copy-start(f32[7168]{0:T(1024)} %copy-done.25) | copy-start | bytes 86020
  397.1 206.7 %all-reduce.7.cloned.1.call-start = ((), (), s32[]{:S(2)}) async-start(), calls=%async_computation | async-start | bytes 6291456 | tf_op jit(solution)/shard_map/psum | solution.py:23
  407.9 8.8 %copy-start.3 = (f32[7168,256]{1,0:T(8,128)}, f32[7168,256]{1,0:T(8,128)S(1)}, u32[]{:S(2)}) copy-start(f32[7168,256]{1,0:T(8,128)S(1)} %get-tuple-element.72) | copy-start | bytes 22020100
  408.0 61.0 %copy-start.28 = (f32[7168]{0:T(1024)S(1)}, f32[7168]{0:T(1024)}, u32[]{:S(2)}) copy-start(f32[7168]{0:T(1024)} %copy-done.27) | copy-start | bytes 86020
  469.0 13.1 %copy-start.45 = (bf16[256]{0:T(256)(128)(2,1)S(1)}, bf16[256]{0:T(256)(128)(2,1)}, u32[]{:S(2)}) copy-start(bf16[256]{0:T(256)(128)(2,1)} %param.32) | copy-start | bytes 1540
  469.0 13.1 %copy-start.22 = (f32[64,112]{1,0:T(8,128)S(1)}, f32[64,112]{1,0:T(8,128)}, u32[]{:S(2)}) copy-start(f32[64,112]{1,0:T(8,128)} %copy-done.21) | copy-start | bytes 86020
  469.0 15.7 %copy-start.34 = (f32[1024]{0:T(1024)S(1)}, f32[1024]{0:T(1024)}, u32[]{:S(2)}) copy-start(f32[1024]{0:T(1024)} %get-tuple-element.48) | copy-start | bytes 12292
  469.0 64.9 %copy-start.18 = (s32[64,112]{1,0:T(8,128)S(1)}, s32[64,112]{1,0:T(8,128)}, u32[]{:S(2)}) copy-start(s32[64,112]{1,0:T(8,128)} %param.18) | copy-start | bytes 86020
Sparse Core Ops, SparseCore 0:
  397.2 71.6 all-reduce.8
  472.8 130.8 all-reduce.6
where the time goes:
time: 630 us; the launch traced here: 619 us
  matrix products  215 us (34%)
  local copies, waits for them, and re-layouts  147 us (23%)
  waiting for transfers between devices  101 us (16%)
  other arithmetic  91.5 us (15%)
  blocking collectives  49.1 us (8%)
  between operations  15.3 us (2%)
    reshape x2, local copies, waits for them, and re-layouts, body(): qkv_low.reshape(traj_count, slots, 3, HEADS, head_size)  61.3 us
    psum x1, waiting for transfers between devices, total_grads(): inner = lax.psum(grads, 'narrow')  52.2 us
    psum x1, waiting for transfers between devices, total_grads(): return lax.psum(inner, 'wide')  49.2 us
    psum x1, blocking collectives, total_grads(): return lax.psum(inner, 'wide')  38.2 us
    convert_element_type x2, local copies, waits for them, and re-layouts, body(): grad_qkv = grad_qkv.reshape(row_count, 3 * width).astype(jnp.bfloat16)  33.5 us
    dot_general x1, matrix products, body(): jnp.einsum('rd,fd->rf', grad_mlp, down_weight, preferred_element_type=jnp...  30.4 us
    dot_general x1, matrix products, body(): jnp.einsum('thqe,thke->thqk', grad_att, values, preferred_element_type=jn...  22.5 us
    unnamed x102, local copies, waits for them, and re-layouts  20.8 us
  transfers between devices with their start and end apart: 2, of which 2 were waited for; matrix products, arithmetic and copies ran while one was open for 9% of the time, Pallas kernels for 0%

commit v1 on v0

v1 whole, which is shorter than its diff:
```python
import jax
import jax.numpy as jnp
from jax import lax
from jax.experimental import pallas as pl
from jax.experimental.pallas import tpu as pltpu
from jax.sharding import Mesh, PartitionSpec as P

AXES = ("wide", "square", "core")
HEADS = 4
EPS = 1e-05
BIN = 128
PAIR = 2 * BIN
BINS = 4
TILE = BINS * BIN
BINS_A = 8
TILE_A = BINS_A * BIN
F32 = jnp.float32
BF16 = jnp.bfloat16
GELU_A = 0.7978845608028654
GELU_B = 0.044715 * GELU_A

NN = (((1,), (0,)), ((), ()))
NT = (((1,), (1,)), ((), ()))
TN = (((0,), (0,)), ((), ()))

MIB = 1024 * 1024
HBM = pl.BlockSpec(memory_space=pl.ANY)


def mm(left, right, dims=NN):
    return lax.dot_general(left, right, dims, preferred_element_type=F32)


class Meta:
    def __init__(self, ref, traj):
        self.ref = ref
        self.width = traj + 8

    @staticmethod
    def size(traj):
        return 4 * (traj + 8) + 16

    def bin(self, b):
        return tuple(self.ref[j * self.width + b] for j in range(4))

    def put(self, b, *values):
        for j, value in enumerate(values):
            self.ref[j * self.width + b] = value

    @property
    def tiles_at(self):
        return 4 * self.width

    def tiles(self):
        return self.ref[self.tiles_at]

    def bit(self, b):
        return self.ref[self.tiles_at + 1 + b]


def plan_kernel(count_ref, rank_ref, meta_ref, first_ref, order_ref):
    traj = count_ref.shape[0]
    top = first_ref.shape[0]
    meta = Meta(meta_ref, traj)

    def clear(v, carry):
        first_ref[v] = 0
        return carry

    lax.fori_loop(0, top, clear, 0, unroll=16)

    def tally(t, carry):
        c = count_ref[t]
        first_ref[c] = first_ref[c] + 1
        return carry

    lax.fori_loop(0, traj, tally, 0, unroll=8)

    def starts(i, run):
        v = top - 1 - i
        n = first_ref[v]
        first_ref[v] = run
        return run + n

    lax.fori_loop(0, top, starts, 0, unroll=16)

    def place(t, carry):
        c = count_ref[t]
        at = first_ref[c]
        order_ref[at] = t
        first_ref[c] = at + 1
        return carry

    lax.fori_loop(0, traj, place, 0, unroll=8)

    def pair(carry):
        hi, lo, n = carry
        t_hi = order_ref[hi]
        t_lo = order_ref[lo]
        c_hi = count_ref[t_hi]
        c_lo = count_ref[t_lo]
        fits = jnp.logical_and(hi < lo, c_hi + c_lo <= BIN)
        meta.put(n, t_hi, jnp.where(fits, t_lo, t_hi), c_hi, jnp.where(fits, c_lo, 0))
        return hi + 1, jnp.where(fits, lo - 1, lo), n + 1

    _, _, n = lax.while_loop(lambda c: c[0] <= c[1], pair, (jnp.int32(0), jnp.int32(traj - 1), jnp.int32(0)))
    last = meta_ref[n - 1]
    for j in range(BINS_A - 1):
        meta.put(n + j, last, last, 0, 0)
    meta_ref[meta.tiles_at] = lax.shift_right_logical(n + BINS - 1, BINS.bit_length() - 1)
    for b in range(15):
        meta_ref[meta.tiles_at + 1 + b] = jnp.bitwise_and(lax.shift_right_logical(rank_ref[0], b), 1)


def make_plan(counts, rank, slots):
    traj = counts.shape[0]
    smem = pl.BlockSpec(memory_space=pltpu.SMEM)
    return pl.pallas_call(
        plan_kernel,
        in_specs=[smem, smem],
        out_specs=smem,
        out_shape=jax.ShapeDtypeStruct((Meta.size(traj),), jnp.int32),
        scratch_shapes=[pltpu.SMEM((-(-(slots + 1) // 16) * 16,), jnp.int32), pltpu.SMEM((traj,), jnp.int32)],
        name="plan",
    )(counts, rank)


def bin_onehot(idx_ref, ta, tb, ca, cb, seq):
    lane = lax.broadcasted_iota(jnp.int32, (8, BIN), 1)
    ia = jnp.broadcast_to(idx_ref[pl.ds(ta, 1), :], (8, BIN))
    ib = jnp.broadcast_to(idx_ref[pl.ds(tb, 1), :], (8, BIN))
    ib = pltpu.roll(ib, ca, 1)
    code = jnp.where(lane < ca, ia, jnp.where(lane < ca + cb, ib + seq, -1))[0:1, :]
    pos = lax.broadcasted_iota(jnp.int32, (2 * seq, BIN), 0)
    return jnp.where(pos == code, 1.0, 0.0).astype(BF16)


def bin_slots(ca, cb):
    row = lax.broadcasted_iota(jnp.int32, (BIN, BIN), 0)
    lane = lax.broadcasted_iota(jnp.int32, (BIN, BIN), 1)
    first = jnp.logical_and(lane == row, row < ca)
    second = jnp.logical_and(lane == row + ca, row < cb)
    return jnp.concatenate([jnp.where(x, 1.0, 0.0).astype(BF16) for x in (first, second)], axis=0)


def bin_mask(ca, cb):
    row = lax.broadcasted_iota(jnp.int32, (BIN, BIN), 0)
    lane = lax.broadcasted_iota(jnp.int32, (BIN, BIN), 1)
    key = jnp.where(row < ca, 0, jnp.where(row < ca + cb, 1, 2))
    query = jnp.where(lane < ca, 0, jnp.where(lane < ca + cb, 1, 3))
    return jnp.where(key == query, 0.0, -1e30)


def center(x):
    mean = jnp.mean(x, axis=0, keepdims=True)
    xc = x - mean
    var = jnp.mean(xc * xc, axis=0, keepdims=True)
    rstd = lax.rsqrt(var + EPS)
    return xc * rstd, rstd


def lanes_into_rows(acc):
    return jnp.sum(acc.T, axis=0, keepdims=True)


def two(x):
    return jnp.concatenate([x, x], axis=1)


def bin_lanes(b):
    return slice(b * BIN, (b + 1) * BIN)


def pair_lanes(t):
    return slice(t * PAIR, (t + 1) * PAIR)


def departures(meta, tile, rows_s, slot, to_ref, rows, sems, act):
    half = rows_s.shape[2] // 2
    for b in range(BINS):
        ta, tb, ca, cb = meta.bin(tile * BINS + b)
        for part, (t, c) in enumerate(((ta, ca), (tb, cb))):

            @pl.when(c > 0)
            def _():
                act(
                    pltpu.make_async_copy(
                        rows_s.at[slot, b, pl.ds(part * half, rows)], to_ref.at[t], sems.at[slot, b, part]
                    )
                )


class Share:
    def __init__(self, first, last):
        self.first, self.last = first, last

    def start(self, tiles):
        return lax.shift_right_logical(tiles * self.first, 4)

    def stop(self, tiles):
        return lax.shift_right_logical(tiles * self.last, 4)

    def most(self, fewest, most):
        return max((n * self.last >> 4) - (n * self.first >> 4) for n in range(fewest, most + 1))

    def block(self, tiles_at):
        return lambda i, meta: jnp.minimum(self.start(meta[tiles_at]) + i, self.stop(meta[tiles_at]) - 1)


def shares(*cuts):
    return [Share(a, b) for a, b in zip(cuts[:-1], cuts[1:])]


def keep_half(meta, acc_s, keep_ref, send_ref):
    half = keep_ref.shape[0]
    core = meta.bit(CORE)
    keep_ref[...] = acc_s[pl.ds(pl.multiple_of(core * half, 8), half), :]
    send_ref[...] = acc_s[pl.ds(pl.multiple_of((1 - core) * half, 8), half), :]


def late_kernel(
    meta_ref,
    idx_ref,
    tok_ref,
    og_ref,
    g1_ref,
    c1_ref,
    bq_ref,
    bv_ref,
    bo_ref,
    g2_ref,
    c2_ref,
    bup_ref,
    wqkv_ref,
    wo_ref,
    wup_ref,
    wdn_ref,
    wdnt_s,
    nhat1_ref,
    rstd1_ref,
    qkv_ref,
    prob_ref,
    gatt_ref,
    gmid_ref,
    act_ref,
    mid_ref,
    keep_ref,
    send_ref,
    dvec_ref,
    tok_s,
    og_s,
    in_sem,
    idx_s,
    vec_s,
    col_s,
    wqkvt_s,
    wot_s,
    wupt_s,
    gath_s,
    first_s,
    bd_s,
    score_s,
    att_s,
    nhat_s,
    sec_s,
    gm_s,
    u_s,
    ga_s,
    gp_s,
    gb_s,
    gs_s,
    acc_s,
    bacc_s,
):
    step = pl.program_id(0)
    traj, seq, d = tok_ref.shape
    slots = og_ref.shape[1]
    ff = wup_ref.shape[1]
    hs = d // HEADS
    scale = hs**-0.5
    meta = Meta(meta_ref, traj)
    steps = lax.shift_right_logical(meta.tiles() + 1, 1)

    def arrivals(i, act):
        slot = jnp.bitwise_and(i, 1)
        for b in range(BINS_A):
            for part, t in enumerate(meta.bin(i * BINS_A + b)[0:2]):
                sems = in_sem.at[slot, b, part]
                act(pltpu.make_async_copy(tok_ref.at[t], tok_s.at[slot, b, pl.ds(part * seq, seq)], sems.at[0]))
                act(pltpu.make_async_copy(og_ref.at[t], og_s.at[slot, b, pl.ds(part * BIN, slots)], sems.at[1]))

    @pl.when(step == 0)
    def _():
        for part in range(2):
            og_s[:, :, part * BIN + slots : (part + 1) * BIN, :] = jnp.zeros((2, BINS_A, BIN - slots, d), BF16)
        arrivals(0, lambda c: c.start())
        idx_s[...] = jnp.zeros_like(idx_s)
        idx_s[:, 0:slots] = idx_ref[...]
        vec_s[...] = jnp.zeros_like(vec_s)
        rows = [(0, g1_ref), (1, c1_ref), (2, bq_ref), (4, bv_ref), (5, bo_ref), (6, g2_ref), (7, c2_ref)]
        for j, ref in rows:
            vec_s[j : j + 1, :] = ref[...].astype(F32).reshape(1, d)
        for j in range(ff // d):
            vec_s[8 + j : 9 + j, :] = bup_ref[j * d : (j + 1) * d].astype(F32).reshape(1, d)
        vec_s[2:3, :] = vec_s[2:3, :] * scale
        cols = vec_s[...].T
        for j in range(12):
            col_s[j * d : (j + 1) * d, :] = jnp.broadcast_to(cols[:, j : j + 1], (d, BIN))
        wqkvt_s[...] = wqkv_ref[...].T
        wqkvt_s[0:d, :] = (wqkvt_s[0:d, :].astype(F32) * scale).astype(BF16)
        wot_s[...] = wo_ref[...].T
        wupt_s[...] = wup_ref[...].T
        wdnt_s[...] = wdn_ref[...].T
        bd_s[...] = jnp.zeros_like(bd_s)
        bacc_s[...] = jnp.zeros_like(bacc_s)
        acc_s[...] = jnp.zeros_like(acc_s)

    def col(j, n=1):
        return col_s[j * d : (j + n) * d, :]

    @pl.when(step < steps)
    def _():
        slot = jnp.bitwise_and(step, 1)
        arrivals(step, lambda c: c.wait())

        @pl.when(step + 1 < steps)
        def _():
            arrivals(step + 1, lambda c: c.start())

        metas = [meta.bin(step * BINS_A + b) for b in range(BINS_A)]
        rstds = {}

        def gather(b):
            lanes = bin_lanes(b)
            gath_s[:, lanes] = mm(tok_s[slot, b], bin_onehot(idx_s, *metas[b], seq), TN)

        def first_norm(b):
            lanes = bin_lanes(b)
            nhat, rstd = center(gath_s[:, lanes])
            nhat1_ref[0, :, lanes] = nhat.astype(BF16)
            rstd1_ref[0, :, lanes] = jnp.broadcast_to(rstd, (8, BIN))
            first_s[:, lanes] = (nhat * col(0) + col(1)).astype(BF16)

        def cotangent(b):
            gm_s[:, bin_lanes(b)] = mm(og_s[slot, b], bin_slots(*metas[b][2:]), TN).astype(BF16)

        def project(t):
            lanes = pair_lanes(t)
            qkv_ref[0, :, lanes] = (mm(wqkvt_s[...], first_s[:, lanes]) + two(col(2, 3))).astype(BF16)

        def scores(b, p):
            lanes = bin_lanes(b)
            f0 = p * 2 * hs
            at = b * (HEADS // 2) + p
            bd_s[at, 0:hs, 0:BIN] = qkv_ref[0, f0 : f0 + hs, lanes]
            bd_s[at, hs : 2 * hs, BIN:PAIR] = qkv_ref[0, f0 + hs : f0 + 2 * hs, lanes]
            score_s[at] = mm(qkv_ref[0, d + f0 : d + f0 + 2 * hs, lanes], bd_s[at], TN)

        def softmax(b):
            mask = two(bin_mask(*metas[b][2:]))
            for p in range(HEADS // 2):
                s = score_s[b * (HEADS // 2) + p] + mask
                e = jnp.exp(s - jnp.max(s, axis=0, keepdims=True))
                prob_ref[0, b, :, pair_lanes(p)] = (e * (1.0 / jnp.sum(e, axis=0, keepdims=True))).astype(BF16)

        def attend(b, p):
            lanes = bin_lanes(b)
            f0 = p * 2 * hs
            both = mm(qkv_ref[0, 2 * d + f0 : 2 * d + f0 + 2 * hs, lanes], prob_ref[0, b, :, pair_lanes(p)])
            for h in range(2):
                att_s[f0 + h * hs : f0 + (h + 1) * hs, lanes] = both[h * hs : (h + 1) * hs, bin_lanes(h)].astype(BF16)

        def residual(t):
            lanes = pair_lanes(t)
            mid_ref[0, :, lanes] = mm(wot_s[...], att_s[:, lanes])

        def second_norm(b):
            lanes = bin_lanes(b)
            mid = mid_ref[0, :, lanes] + gath_s[:, lanes] + col(5)
            mid_ref[0, :, lanes] = mid
            nhat, rstds[b] = center(mid)
            nhat_s[:, lanes] = nhat
            sec_s[:, lanes] = (nhat * col(6) + col(7)).astype(BF16)

        def up(t):
            lanes = pair_lanes(t)
            u_s[:, lanes] = mm(wupt_s[...], sec_s[:, lanes])
            ga_s[:, lanes] = mm(wdn_ref[...], gm_s[:, lanes])

        def gelu(t, rows):
            lanes = pair_lanes(t)
            u = u_s[rows, lanes] + two(col_s[8 * d + rows.start : 8 * d + rows.stop, :])
            q = u * u * GELU_B + GELU_A
            sg = 0.5 * jnp.tanh(u * q) + 0.5
            act = u * sg
            gp = (act * (1.0 - sg) * (6.0 * q - 4.0 * GELU_A) + sg) * ga_s[rows, lanes]
            act_ref[0, rows, lanes] = act.astype(BF16)
            gp_s[rows, lanes] = gp.astype(BF16)
            bacc_s[d + rows.start : d + rows.stop, :] += gp[:, 0:BIN] + gp[:, BIN:PAIR]

        def down(t):
            lanes = pair_lanes(t)
            gs_s[:, lanes] = mm(wup_ref[...], gp_s[:, lanes])

        def second_norm_back(b):
            lanes = bin_lanes(b)
            gs = gs_s[:, lanes]
            nhat = nhat_s[:, lanes]
            bacc_s[0:d, :] += gs * nhat
            a = gs * col(6)
            m1 = jnp.mean(a, axis=0, keepdims=True)
            m2 = jnp.mean(a * nhat, axis=0, keepdims=True)
            gm = gm_s[:, lanes].astype(F32)
            gmid = gm + rstds[b] * (a - m1 - nhat * m2)
            gmid_ref[0, :, lanes] = gmid
            gb_s[:, lanes] = gmid.astype(BF16)
            bacc_s[d + ff : 2 * d + ff, :] += gm
            bacc_s[2 * d + ff : 3 * d + ff, :] += gmid

        def grad_attended(t):
            lanes = pair_lanes(t)
            gatt_ref[0, :, lanes] = mm(wo_ref[...], gb_s[:, lanes]).astype(BF16)

        def work(count):
            bins, tiles, chunk, lanes = range(count), range(count // 2), 32, slice(0, count * BIN)
            for b in bins:
                gather(b)
            for b in bins:
                cotangent(b)
            for b in bins:
                first_norm(b)
            for t in tiles:
                project(t)
            pairs = [(b, p) for b in bins for p in range(HEADS // 2)]
            for b, p in pairs:
                scores(b, p)
            for b in bins:
                softmax(b)
            for b, p in pairs:
                attend(b, p)
            for t in tiles:
                residual(t)
            for b in bins:
                second_norm(b)
            for t in tiles:
                up(t)
            for t in tiles:
                for j in range(ff // chunk):
                    gelu(t, slice(j * chunk, (j + 1) * chunk))
            acc_s[0:ff, :] += mm(act_ref[0, :, lanes], gm_s[:, lanes], NT)
            acc_s[ff : 2 * ff, :] += mm(gp_s[:, lanes], sec_s[:, lanes], NT)
            for t in tiles:
                down(t)
            for b in bins:
                second_norm_back(b)
            acc_s[2 * ff : 2 * ff + d, :] += mm(att_s[:, lanes], gb_s[:, lanes], NT)
            for t in tiles:
                grad_attended(t)

        full = 2 * step + 1 < meta.tiles()

        @pl.when(full)
        def _():
            work(BINS_A)

        @pl.when(jnp.logical_not(full))
        def _():
            work(BINS)

        @pl.when(step == steps - 1)
        def _():
            dvec_ref[...] = jnp.zeros_like(dvec_ref)
            keep_half(meta, acc_s, keep_ref, send_ref)
            for j in range(7):
                dvec_ref[j : j + 1, :] = lanes_into_rows(bacc_s[j * d : (j + 1) * d, :])


def attention_kernel(
    traj,
    meta_ref,
    nhat1_ref,
    qkv_ref,
    prob_ref,
    gatt_ref,
    dvec_ref,
    gq_ref,
    keep_ref,
    send_ref,
    bd_s,
    bdq_s,
    dp_s,
    ds_s,
    bacc_s,
    acc_s,
):
    step = pl.program_id(0)
    d = nhat1_ref.shape[1]
    hs = d // HEADS
    scale = hs**-0.5
    meta = Meta(meta_ref, traj)

    @pl.when(step == 0)
    def _():
        bd_s[...] = jnp.zeros_like(bd_s)
        bdq_s[...] = jnp.zeros_like(bdq_s)
        bacc_s[...] = jnp.zeros_like(bacc_s)
        acc_s[...] = jnp.zeros_like(acc_s)

    def work(count):
        pairs = [(b, p * 2 * hs, b * (HEADS // 2) + p, p) for b in range(count) for p in range(HEADS // 2)]
        for b, f0, at, _ in pairs:
            lanes = bin_lanes(b)
            bd_s[at, 0:hs, 0:BIN] = gatt_ref[0, f0 : f0 + hs, lanes]
            bd_s[at, hs : 2 * hs, BIN:PAIR] = gatt_ref[0, f0 + hs : f0 + 2 * hs, lanes]
            bdq_s[at, 0:hs, 0:BIN] = qkv_ref[0, f0 : f0 + hs, lanes]
            bdq_s[at, hs : 2 * hs, BIN:PAIR] = qkv_ref[0, f0 + hs : f0 + 2 * hs, lanes]
        for b, f0, at, _ in pairs:
            dp_s[at] = mm(qkv_ref[0, 2 * d + f0 : 2 * d + f0 + 2 * hs, bin_lanes(b)], bd_s[at], TN)
        for b, f0, at, p in pairs:
            pr = prob_ref[0, b, :, pair_lanes(p)].astype(F32)
            t = pr * dp_s[at]
            ds_s[at] = (t - pr * jnp.sum(t, axis=0, keepdims=True)).astype(BF16)

        def put(b, row, part):
            gq_ref[0, row : row + 2 * hs, bin_lanes(b)] = part.astype(BF16)
            bacc_s[row : row + 2 * hs, :] += part

        for b, f0, at, _ in pairs:
            both = mm(qkv_ref[0, d + f0 : d + f0 + 2 * hs, bin_lanes(b)], ds_s[at]) * scale
            put(b, f0, jnp.concatenate([both[0:hs, 0:BIN], both[hs : 2 * hs, BIN:PAIR]], axis=0))
        for b, f0, at, _ in pairs:
            put(b, d + f0, mm(bdq_s[at], ds_s[at], NT))
        for b, f0, at, p in pairs:
            put(b, 2 * d + f0, mm(bd_s[at], prob_ref[0, b, :, pair_lanes(p)], NT))
        lanes = slice(0, count * BIN)
        acc_s[0 : 3 * d, :] += mm(gq_ref[0, :, lanes], nhat1_ref[0, :, lanes], NT)

    @pl.when(2 * step + 1 < meta.tiles())
    def _():
        work(BINS_A)

    @pl.when(2 * step + 1 == meta.tiles())
    def _():
        work(BINS)

    @pl.when(step == pl.num_programs(0) - 1)
    def _():
        for j in range(3):
            acc_s[3 * d + j : 3 * d + j + 1, :] = lanes_into_rows(bacc_s[j * d : (j + 1) * d, :])
        acc_s[3 * d + 3 : 3 * d + 11, :] = dvec_ref[...]
        keep_half(meta, acc_s, keep_ref, send_ref)


def token_kernel(share, meta_ref, idx_ref, g1_ref, wqkv_ref, nhat1_ref, rstd1_ref, gq_ref, gmid_ref, *refs):
    tg_ref, idx_s, col_s, gg_s, rows_s, sems = refs[-6:]
    step = pl.program_id(0)
    traj, slots = idx_ref.shape
    seq, d = tg_ref.shape[1:]
    meta = Meta(meta_ref, traj)

    @pl.when(step == 0)
    def _():
        idx_s[...] = jnp.zeros_like(idx_s)
        idx_s[:, 0:slots] = idx_ref[...]
        row = jnp.broadcast_to(g1_ref[...].astype(F32).reshape(1, d), (8, d))
        col_s[...] = jnp.broadcast_to(row.T[:, 0:1], (d, BIN))

    def rows_of(tile, slot):
        gfs = [mm(wqkv_ref[...], gq_ref[0, :, pair_lanes(t)]) for t in range(BINS // 2)]
        for b in range(BINS):
            lanes = bin_lanes(b)
            nhat = nhat1_ref[0, :, lanes].astype(F32)
            a = gfs[b // 2][:, bin_lanes(b % 2)] * col_s[...]
            m1 = jnp.mean(a, axis=0, keepdims=True)
            m2 = jnp.mean(a * nhat, axis=0, keepdims=True)
            rstd = rstd1_ref[0, 0:1, lanes]
            gg_s[:, lanes] = (gmid_ref[0, :, lanes] + rstd * (a - m1 - nhat * m2)).astype(BF16)
        for b in range(BINS):
            onehot = bin_onehot(idx_s, *meta.bin(tile * BINS + b), seq)
            rows_s[slot, b] = mm(onehot, gg_s[:, bin_lanes(b)], NT).astype(BF16)

    store_tiles(share, meta, step, rows_of, rows_s, tg_ref, seq, sems)


def store_tiles(share, meta, step, rows_of, rows_s, to_ref, rows, sems):
    first, stop = share.start(meta.tiles()), share.stop(meta.tiles())
    tile = first + step
    slot = jnp.bitwise_and(step, 1)

    def leave(tile, slot, act):
        departures(meta, tile, rows_s, slot, to_ref, rows, sems, act)

    @pl.when(tile < stop)
    def _():
        @pl.when(step >= 2)
        def _():
            leave(tile - 2, slot, lambda c: c.wait())

        rows_of(tile, slot)
        leave(tile, slot, lambda c: c.start())

    @pl.when(step == pl.num_programs(0) - 1)
    def _():
        done = stop - first

        @pl.when(done >= 2)
        def _():
            leave(stop - 2, jnp.bitwise_and(done, 1), lambda c: c.wait())

        leave(stop - 1, jnp.bitwise_and(done - 1, 1), lambda c: c.wait())


def output_kernel(share, traj, meta_ref, bdn_ref, wdnt_ref, act_ref, mid_ref, *refs):
    lay_ref, col_s, y_s, rows_s, sems = refs[-5:]
    step = pl.program_id(0)
    slots, d = lay_ref.shape[1:]
    meta = Meta(meta_ref, traj)

    @pl.when(step == 0)
    def _():
        row = jnp.broadcast_to(bdn_ref[...].astype(F32).reshape(1, d), (8, d))
        col_s[...] = jnp.broadcast_to(row.T[:, 0:1], (d, BIN))

    def rows_of(tile, slot):
        for t in range(BINS // 2):
            lanes = pair_lanes(t)
            mlp = mm(wdnt_ref[...], act_ref[0, :, lanes])
            y_s[:, lanes] = (mlp + mid_ref[0, :, lanes] + two(col_s[...])).astype(BF16)
        for b in range(BINS):
            _, _, ca, cb = meta.bin(tile * BINS + b)
            rows_s[slot, b] = mm(bin_slots(ca, cb), y_s[:, bin_lanes(b)], NT).astype(BF16)

    store_tiles(share, meta, step, rows_of, rows_s, lay_ref, slots, sems)


CORE, Y, X, Z = 0, 1, 2, 3


def row_at(const=0, **bits):
    return const, tuple(({"core": CORE, "y": Y, "x": X, "z": Z}[name], coef) for name, coef in bits.items())


def mine(bit, rows, base=0):
    return base, ((bit, rows),)


def other(bit, rows, base=0):
    return base + rows, ((bit, -rows),)


class Step:
    def __init__(self, inputs, out_rows, parts, sends=()):
        self.inputs, self.out_rows, self.parts, self.sends = list(inputs), list(out_rows), list(parts), dict(sends)


def combine_kernel(step, bits_at, meta_ref, *refs):
    ins, outs = refs[: len(step.inputs)], refs[len(step.inputs) :]

    def row(start):
        if isinstance(start, int):
            return start
        const, bits = start
        for bit, coef in bits:
            const = const + meta_ref[bits_at + bit] * coef
        return const

    def rows(start, n):
        return pl.ds(start if isinstance(start, int) else pl.multiple_of(start, 8), n)

    for n, terms, goes in step.parts:
        for out, start, first, count in goes:
            total = None
            for ref, at in terms:
                term = ins[ref][rows(row(at) + row(first), count), :]
                total = term if total is None else total + term
            outs[out][rows(row(start), count), :] = total


def combine(step, meta, bits_at, width):
    vmem = pl.BlockSpec(memory_space=pltpu.VMEM)
    return pl.pallas_call(
        lambda *refs: combine_kernel(step, bits_at, *refs),
        in_specs=[pl.BlockSpec(memory_space=pltpu.SMEM)] + [vmem] * len(step.inputs),
        out_specs=[vmem] * len(step.out_rows),
        out_shape=[jax.ShapeDtypeStruct((n, width), F32) for n in step.out_rows],
        compiler_params=pltpu.CompilerParams(vmem_limit_bytes=2 * MIB),
        name="combine",
    )(meta, *step.inputs)


def bucket_sum(bits, keep, send, half, halve_z):
    q, e, f = half // 4, half // 8, half // 16
    _, (got,) = yield Step([send], [], [], {0: CORE})
    (k0, k1, _, _), (g0, g1) = yield Step(
        [keep, got],
        [q, q, q, q],
        [
            (2 * q, [(0, row_at()), (1, row_at())], [(0, row_at(), mine(X, q), q), (2, row_at(), other(X, q), q)]),
            (
                2 * q,
                [(0, row_at(2 * q)), (1, row_at(2 * q))],
                [(1, row_at(), mine(Y, q), q), (3, row_at(), other(Y, q), q)],
            ),
        ],
        {2: X, 3: Y},
    )
    (a0, a1, _, _), (g0, g1) = yield Step(
        [k0, k1, g0, g1],
        [e, e, e, e],
        [
            (q, [(0, row_at()), (2, row_at())], [(0, row_at(), mine(Y, e), e), (2, row_at(), other(Y, e), e)]),
            (q, [(1, row_at()), (3, row_at())], [(1, row_at(), mine(X, e), e), (3, row_at(), other(X, e), e)]),
        ],
        {2: Y, 3: X},
    )
    if halve_z:
        (z, _), (got,) = yield Step(
            [a0, a1, g0, g1],
            [e, e],
            [
                (
                    e,
                    [(c, row_at()), (2 + c, row_at())],
                    [(0, row_at(c * f), mine(Z, f), f), (1, row_at(c * f), other(Z, f), f)],
                )
                for c in range(2)
            ],
            {1: Z},
        )
        for bit in [*range(Z + 1, bits), Z]:
            (z,), (got,) = yield Step([z, got], [e], [(e, [(0, row_at()), (1, row_at())], [(0, row_at(), 0, e)])], {0: bit})
        (e0, e1), (g0, g1) = yield Step(
            [z, got],
            [e, e],
            [
                (f, [(ref, row_at(c * f))], [(c, side(Z, f), 0, f)])
                for ref, side in enumerate((mine, other))
                for c in range(2)
            ],
            {0: Y, 1: X},
        )
    else:
        (z,), (got,) = yield Step(
            [a0, a1, g0, g1],
            [2 * e],
            [(e, [(c, row_at()), (2 + c, row_at())], [(0, row_at(c * e), 0, e)]) for c in range(2)],
            {0: bits - 1},
        )
        for bit in range(bits - 2, Z - 1, -1):
            (z,), (got,) = yield Step(
                [z, got], [2 * e], [(2 * e, [(0, row_at()), (1, row_at())], [(0, row_at(), 0, 2 * e)])], {0: bit}
            )
        (e0, e1), (g0, g1) = yield Step(
            [z, got],
            [e, e],
            [(2 * e, [(0, row_at()), (1, row_at())], [(0, row_at(), 0, e), (1, row_at(), e, e)])],
            {0: Y, 1: X},
        )
    (f0, f1), (g0, g1) = yield Step(
        [e0, e1, g0, g1],
        [q, q],
        [
            (e, [(0, row_at())], [(0, mine(Y, e), 0, e)]),
            (e, [(2, row_at())], [(0, other(Y, e), 0, e)]),
            (e, [(1, row_at())], [(1, mine(X, e), 0, e)]),
            (e, [(3, row_at())], [(1, other(X, e), 0, e)]),
        ],
        {0: X, 1: Y},
    )
    (near,), (far,) = yield Step(
        [f0, f1, g0, g1],
        [half],
        [
            (q, [(0, row_at())], [(0, mine(X, q), 0, q)]),
            (q, [(2, row_at())], [(0, other(X, q), 0, q)]),
            (q, [(1, row_at())], [(0, mine(Y, q, 2 * q), 0, q)]),
            (q, [(3, row_at())], [(0, other(Y, q, 2 * q), 0, q)]),
        ],
        {0: CORE},
    )
    return near, far


class Sums:
    def __init__(self, ranks, meta, bits_at, width):
        self.ranks, self.meta, self.bits_at, self.width = ranks, meta, bits_at, width
        self.arrays, self.arrived, self.sent = [], [], []
        self.running, self.results = {}, {}

    def view(self, array):
        self.arrays.append(array)
        return (len(self.arrays) - 1, 0)

    def add(self, name, steps):
        self.running[name] = (steps, next(steps))

    def advance(self, after=None):
        if after is not None and self.arrived:
            tied = lax.optimization_barrier((*[self.arrays[k] for k in self.arrived], after))
            for k, array in zip(self.arrived, tied):
                self.arrays[k] = array
        inputs, out_rows, parts, places, sends = [], [], [], {}, {}
        for name, (_, step) in self.running.items():
            outs = []
            for out, rows in enumerate(step.out_rows):
                bit = step.sends.get(out)
                if bit in sends:
                    at = sends[bit]
                    outs.append((at, out_rows[at]))
                    out_rows[at] += rows
                    continue
                if bit is not None:
                    sends[bit] = len(out_rows)
                outs.append((len(out_rows), 0))
                out_rows.append(rows)
            places[name] = outs
            for rows, terms, goes in step.parts:
                moved = []
                for ref, (const, bits) in terms:
                    k, row = step.inputs[ref]
                    if k not in inputs:
                        inputs.append(k)
                    moved.append((inputs.index(k), (const + row, bits)))
                parts.append(
                    (
                        rows,
                        moved,
                        [(outs[out][0], (const + outs[out][1], bits), *rest) for out, (const, bits), *rest in goes],
                    )
                )
        base = len(self.arrays)
        if out_rows:
            merged = Step([self.arrays[k] for k in inputs], out_rows, parts)
            self.arrays += list(combine(merged, self.meta, self.bits_at, self.width))
        to_send = {bit: base + out for bit, out in sends.items()}
        raw = {name: step for name, (_, step) in self.running.items() if not step.parts}
        for step in raw.values():
            for out, bit in step.sends.items():
                to_send[(bit, id(step))] = step.inputs[out][0]
        self.sent = [self.arrays[k] for k in to_send.values()]
        received = {}
        for key, k in to_send.items():
            bit = key[0] if isinstance(key, tuple) else key
            perm = [(r, r ^ (1 << bit)) for r in range(self.ranks)]
            received[key] = self.view(lax.ppermute(self.arrays[k], AXES, perm))[0]
        self.arrived = list(received.values())
        for name, (steps, step) in list(self.running.items()):
            if name in raw:
                outs = []
                got = [(received[(bit, id(step))], 0) for bit in step.sends.values()]
            else:
                outs = [(base + out, row) for out, row in places[name]]
                got = [(received[bit], places[name][out][1]) for out, bit in step.sends.items()]
            try:
                self.running[name] = (steps, steps.send((outs, got)))
            except StopIteration as stop:
                self.results[name] = stop.value
                del self.running[name]

    def ordered(self, value):
        return lax.optimization_barrier((value, *self.sent))[0]


def finish_kernel(
    bits_at, rows_at, meta_ref, late0_ref, late1_ref, first0_ref, first1_ref, g1_ref, c1_ref, wqkv_ref, wup_ref,
    dwn_ref, dup_ref, dwo_ref, dqkv_ref, dg1_ref, dc1_ref, dbq_ref, dbv_ref, dbo_ref, dg2_ref, dc2_ref, dbup_ref, dbdn_ref,
    late_s, first_s, first_sem, late_sem, out_sem,
):
    ff, d = dwn_ref.shape
    core = meta_ref[bits_at + CORE]
    late_near, late_far, first_near, first_far = rows_at
    first, late = [], []
    for to_s, copies, sems, sides in (
        (late_s, late, late_sem, ((late0_ref, late_near, core), (late1_ref, late_far, 1 - core))),
        (first_s, first, first_sem, ((first0_ref, first_near, core), (first1_ref, first_far, 1 - core))),
    ):
        half = to_s.shape[0] // 2
        for k, (ref, row, side) in enumerate(sides):
            to = to_s.at[pl.ds(pl.multiple_of(side * half, 8), half)]
            copies.append(pltpu.make_async_copy(ref.at[pl.ds(row, half)], to, sems.at[k]))
    for copy in late + first:
        copy.start()
    for copy in late:
        copy.wait()
    copies = [
        pltpu.make_async_copy(late_s.at[pl.ds(0, ff)], dwn_ref, out_sem.at[0]),
        pltpu.make_async_copy(late_s.at[pl.ds(2 * ff, d)], dwo_ref, out_sem.at[1]),
    ]
    for copy in copies:
        copy.start()
    for j in range(ff // d):
        dup_ref[:, j * d : (j + 1) * d] = late_s[ff + j * d : ff + (j + 1) * d, :].T
    for copy in first:
        copy.wait()

    def late_row(j):
        return first_s[3 * d + 3 + j : 3 * d + 4 + j, :].reshape(d)

    dg2_ref[...] = late_row(0)
    for j in range(ff // d):
        dbup_ref[j * d : (j + 1) * d] = late_row(1 + j)
    dbdn_ref[...] = late_row(5)
    dbo_ref[...] = late_row(6)

    def times(weight_ref, row, n):
        total = jnp.zeros((8, d), F32)
        for j in range(n):
            left = jnp.broadcast_to(first_s[row + j : row + j + 1, :], (8, d))
            for _ in range(3):
                low = left.astype(BF16)
                left = left - low.astype(F32)
                total = total + mm(low, weight_ref[:, j * d : (j + 1) * d], NT)
        return total[0:1, :]

    dc2_ref[...] = times(wup_ref, 3 * d + 4, ff // d).reshape(d)
    dc1_ref[...] = times(wqkv_ref, 3 * d, 3).reshape(d)

    gain = jnp.broadcast_to(g1_ref[...].astype(F32).reshape(1, d), (8, d)).T[:, 0:1]
    bias = jnp.broadcast_to(c1_ref[...].astype(F32).reshape(1, d), (8, d)).T[:, 0:1]
    gain_grad = jnp.zeros((d, d), F32)
    for j in range(3):
        block = slice(j * d, (j + 1) * d)
        total = first_s[3 * d + j : 3 * d + j + 1, :]
        product = first_s[block, :].T
        weight = wqkv_ref[:, block].astype(F32)
        dqkv_ref[:, block] = gain * product + bias * total
        gain_grad += weight * product
    dg1_ref[...] = jnp.sum(gain_grad.T, axis=0, keepdims=True).reshape(d)
    dbq_ref[...] = first_s[3 * d : 3 * d + 1, :].reshape(d)
    dbv_ref[...] = first_s[3 * d + 2 : 3 * d + 3, :].reshape(d)
    for copy in copies:
        copy.wait()


def whole(shape):
    zeros = (0,) * len(shape)
    return pl.BlockSpec(shape, lambda i, *_: zeros, pipeline_mode=pl.Buffered(1))


def per_step(shape, at):
    rest = (0,) * len(shape)
    return pl.BlockSpec((1,) + shape, lambda i, meta: (at(i, meta),) + rest)


def per_tile(shape, at):
    axis = 0 if len(shape) == 3 else len(shape) - 1

    def index(i, meta):
        tile = at(i, meta)
        place = [0] * len(shape)
        place[axis] = jnp.bitwise_and(tile, 1)
        return (lax.shift_right_logical(tile, 1), *place)

    return pl.BlockSpec((1,) + shape, index)


def doubled(shape):
    if len(shape) == 3:
        return (2 * shape[0],) + shape[1:]
    return shape[:-1] + (2 * shape[-1],)


SHARES_C = shares(0, 5, 8, 10, 16)
SHARES_D = shares(0, 6, 9, 16)


def strided(first, pieces, tiles_at, halved=0):
    def at(i, meta):
        bits = pieces.bit_length() - 1
        count = lax.shift_right_logical(meta[tiles_at] + halved, halved)
        last = first + lax.shift_left(lax.shift_right_logical(count - 1 - first, bits), bits)
        return jnp.minimum(i * pieces + first, last)

    return at


def body(
    ranks,
    tokens,
    visible_index,
    visible_count,
    ln1_gain,
    ln1_bias,
    qkv_weight,
    query_bias,
    value_bias,
    out_weight,
    out_bias,
    ln2_gain,
    ln2_bias,
    up_weight,
    up_bias,
    down_weight,
    down_bias,
    out_grad,
):
    traj, slots = visible_index.shape
    seq, d = tokens.shape[1:]
    ff = up_weight.shape[1]
    hs = d // HEADS
    steps_a = -(-traj // BINS_A)
    tiles = 2 * steps_a
    tiles_at = Meta.size(traj) - 16
    bits = ranks.bit_length() - 1
    rank = lax.axis_index(AXES).astype(jnp.int32).reshape(1)
    meta = make_plan(visible_count, rank, slots)
    sums = Sums(ranks, meta, tiles_at + 1, d)

    shapes = dict(
        nhat=((d, TILE), BF16),
        rstd=((8, TILE), F32),
        qkv=((3 * d, TILE), BF16),
        prob=((BINS, BIN, HEADS * BIN), BF16),
        gatt=((d, TILE), BF16),
        gmid=((d, TILE), F32),
        act=((ff, TILE), BF16),
        mid=((d, TILE), F32),
    )

    def stored(name):
        shape, kind = shapes[name]
        return jax.ShapeDtypeStruct((steps_a,) + doubled(shape), kind)

    at_a = strided(0, 1, tiles_at, 1)

    def params(mib):
        return pltpu.CompilerParams(dimension_semantics=("arbitrary",), vmem_limit_bytes=mib * MIB)

    late_shape = (2 * ff + d, d)
    vectors = [ln1_gain, ln1_bias, query_bias, value_bias, out_bias, ln2_gain, ln2_bias, up_bias]
    weights = [qkv_weight, out_weight, up_weight, down_weight]
    down_weight_t, nhat, rstd, qkv, prob, gatt, gmid, act, mid, late_keep, late_send, late_vectors = pl.pallas_call(
        late_kernel,
        grid_spec=pltpu.PrefetchScalarGridSpec(
            num_scalar_prefetch=1,
            grid=(steps_a,),
            in_specs=[whole((traj, slots)), HBM, HBM] + [whole(v.shape) for v in vectors + weights],
            out_specs=[whole((d, ff))]
            + [per_step(doubled(shapes[n][0]), at_a) for n in shapes]
            + [whole((late_shape[0] // 2, d))] * 2
            + [whole((8, d))],
            scratch_shapes=[
                pltpu.VMEM((2, BINS_A, 2 * seq, d), BF16),
                pltpu.VMEM((2, BINS_A, 2 * BIN, d), BF16),
                pltpu.SemaphoreType.DMA((2, BINS_A, 2, 2)),
                pltpu.VMEM((traj, BIN), jnp.int32),
                pltpu.VMEM((16, d), F32),
                pltpu.VMEM((12 * d, BIN), F32),
                pltpu.VMEM((3 * d, d), BF16),
                pltpu.VMEM((d, d), BF16),
                pltpu.VMEM((ff, d), BF16),
                pltpu.VMEM((d, TILE_A), F32),
                pltpu.VMEM((d, TILE_A), BF16),
                pltpu.VMEM((BINS_A * HEADS // 2, 2 * hs, PAIR), BF16),
                pltpu.VMEM((BINS_A * HEADS // 2, BIN, PAIR), F32),
                pltpu.VMEM((d, TILE_A), BF16),
                pltpu.VMEM((d, TILE_A), F32),
                pltpu.VMEM((d, TILE_A), BF16),
                pltpu.VMEM((d, TILE_A), BF16),
                pltpu.VMEM((ff, TILE_A), F32),
                pltpu.VMEM((ff, TILE_A), F32),
                pltpu.VMEM((ff, TILE_A), BF16),
                pltpu.VMEM((d, TILE_A), BF16),
                pltpu.VMEM((d, TILE_A), F32),
                pltpu.VMEM(late_shape, F32),
                pltpu.VMEM((3 * d + ff, BIN), F32),
            ],
        ),
        out_shape=[jax.ShapeDtypeStruct((d, ff), BF16)]
        + [stored(n) for n in shapes]
        + [jax.ShapeDtypeStruct(n, F32) for n in ((late_shape[0] // 2, d), (late_shape[0] // 2, d), (8, d))],
        compiler_params=params(56),
        name="forward_mlp",
    )(meta, visible_index, tokens, out_grad, *vectors, *weights)
    late = bucket_sum(bits, sums.view(late_keep), sums.view(late_send), late_shape[0] // 2, True)
    sums.add("late", late)
    sums.advance()

    acc_shape = (-(-(3 * d + 11) // 128) * 128, d)
    send_shape = (acc_shape[0] // 2, d)
    at = strided(0, 1, tiles_at, 1)
    grad_qkv, first_keep, first_send = pl.pallas_call(
        lambda *refs: attention_kernel(traj, *refs),
        grid_spec=pltpu.PrefetchScalarGridSpec(
            num_scalar_prefetch=1,
            grid=(steps_a,),
            in_specs=[per_step(doubled(shapes[n][0]), at) for n in ("nhat", "qkv", "prob", "gatt")] + [whole((8, d))],
            out_specs=[per_step((3 * d, TILE_A), at)] + [whole(send_shape)] * 2,
            scratch_shapes=[pltpu.VMEM((BINS_A * HEADS // 2, 2 * hs, PAIR), BF16)] * 2
            + [
                pltpu.VMEM((BINS_A * HEADS // 2, BIN, PAIR), F32),
                pltpu.VMEM((BINS_A * HEADS // 2, BIN, PAIR), BF16),
                pltpu.VMEM((3 * d, BIN), F32),
                pltpu.VMEM(acc_shape, F32),
            ],
        ),
        out_shape=[jax.ShapeDtypeStruct((steps_a, 3 * d, TILE_A), BF16)] + [jax.ShapeDtypeStruct(send_shape, F32)] * 2,
        compiler_params=params(56),
        cost_estimate=pl.CostEstimate(flops=5 * 10**9, bytes_accessed=16 * 10**6, transcendentals=0),
        name="attention_backward",
    )(sums.ordered(meta), nhat, qkv, prob, gatt, late_vectors)
    first = bucket_sum(bits, sums.view(first_keep), sums.view(first_send), send_shape[0], False)
    sums.add("first", first)
    sums.advance(first_keep)

    fewest = -(-traj // (2 * BINS))

    def stores(kernel, share, name, inputs, in_specs, rows, scratch, earlier):
        given = [] if earlier is None else [earlier]
        return pl.pallas_call(
            kernel,
            grid_spec=pltpu.PrefetchScalarGridSpec(
                num_scalar_prefetch=1,
                grid=(share.most(fewest, tiles),),
                in_specs=in_specs + [HBM] * len(given),
                out_specs=HBM,
                scratch_shapes=scratch
                + [pltpu.VMEM((2, BINS, 2 * BIN, d), BF16), pltpu.SemaphoreType.DMA((2, BINS, 2))],
            ),
            out_shape=jax.ShapeDtypeStruct((traj, rows, d), BF16),
            input_output_aliases={1 + len(inputs): 0} if given else {},
            compiler_params=params(56),
            cost_estimate=pl.CostEstimate(flops=2 * 10**9, bytes_accessed=8 * 10**6, transcendentals=0),
            name=name,
        )(sums.ordered(meta), *inputs, *given)

    tokens_grad = None
    for share in SHARES_C:
        at = share.block(tiles_at)
        tokens_grad = stores(
            lambda *refs, share=share: token_kernel(share, *refs),
            share,
            "tokens_backward",
            [visible_index, ln1_gain, qkv_weight, nhat, rstd, grad_qkv, gmid],
            [whole((traj, slots)), whole((d,)), whole((d, 3 * d))]
            + [per_tile(shapes["nhat"][0], at), per_tile(shapes["rstd"][0], at)]
            + [per_tile((3 * d, TILE), at), per_tile(shapes["gmid"][0], at)],
            seq,
            [pltpu.VMEM((traj, BIN), jnp.int32), pltpu.VMEM((d, BIN), F32), pltpu.VMEM((d, TILE), BF16)],
            tokens_grad,
        )
        sums.advance(tokens_grad)
    layer_out = None
    for share in SHARES_D:
        at = share.block(tiles_at)
        layer_out = stores(
            lambda *refs, share=share: output_kernel(share, traj, *refs),
            share,
            "layer_output",
            [down_bias, down_weight_t, act, mid],
            [whole((d,)), whole((d, ff)), per_tile(shapes["act"][0], at), per_tile(shapes["mid"][0], at)],
            slots,
            [pltpu.VMEM((d, BIN), F32), pltpu.VMEM((d, TILE), BF16)],
            layer_out,
        )
        sums.advance(layer_out)
    while sums.running:
        sums.advance()
    views = sums.results["late"] + sums.results["first"]
    near_far = [sums.arrays[k] for k, _ in views]
    rows_at = tuple(row for _, row in views)

    vmem = pl.BlockSpec(memory_space=pltpu.VMEM)
    vector = jax.ShapeDtypeStruct((d,), F32)
    dwn, dup, dwo, dqkv, dg1, dc1, dbq, dbv, dbo, dg2, dc2, dbup, dbdn = pl.pallas_call(
        lambda *refs: finish_kernel(tiles_at + 1, rows_at, *refs),
        in_specs=[pl.BlockSpec(memory_space=pltpu.SMEM)] + [HBM] * 4 + [vmem] * 4,
        out_specs=[HBM, vmem, HBM] + [vmem] * 10,
        out_shape=[
            jax.ShapeDtypeStruct((ff, d), F32),
            jax.ShapeDtypeStruct((d, ff), F32),
            jax.ShapeDtypeStruct((d, d), F32),
            jax.ShapeDtypeStruct((d, 3 * d), F32),
        ]
        + [vector] * 7
        + [jax.ShapeDtypeStruct((ff,), F32), vector],
        scratch_shapes=[
            pltpu.VMEM(late_shape, F32),
            pltpu.VMEM(acc_shape, F32),
            pltpu.SemaphoreType.DMA((2,)),
            pltpu.SemaphoreType.DMA((2,)),
            pltpu.SemaphoreType.DMA((2,)),
        ],
        compiler_params=pltpu.CompilerParams(vmem_limit_bytes=24 * MIB),
        name="finish",
    )(meta, *near_far, ln1_gain, ln1_bias, qkv_weight, up_weight)
    return layer_out, tokens_grad, dg1, dc1, dqkv, dbq, dbv, dwo, dbo, dg2, dc2, dup, dbup, dwn, dbdn


def solution(mesh):
    devices = mesh.devices
    ranks = devices.size
    mesh = Mesh(devices.reshape(devices.shape[0], devices.shape[1] // 2, 2), AXES)
    rows = P(AXES)
    placed = (rows, rows, rows) + (P(),) * 13 + (rows,)
    return jax.shard_map(
        lambda *args: body(ranks, *args),
        mesh=mesh,
        in_specs=placed,
        out_specs=(rows, rows) + (P(),) * 13,
        check_vma=False,
    )
```

time: 630 us -> 150 us (0.24); the launches traced: 619 us -> 151 us
  matrix products: 215 us -> 0 us
  local copies, waits for them, and re-layouts: 147 us -> 0.06 us
  Pallas kernels: 0 us -> 128 us
  other arithmetic: 91.5 us -> 0 us
  waiting for transfers between devices: 101 us -> 10.5 us
  blocking collectives: 49.1 us -> 0 us
  between operations: 15.3 us -> 1.17 us
  starting transfers between devices: 0.08 us -> 11 us
    dot_general x20 -> x0, matrix products: 215 us -> none  [the longest x1 30.4 us: body(): jnp.einsum('rd,fd->rf', grad_mlp, down_weight, preferred_element_type=jnp...]
    pallas_call x0 -> x19, Pallas kernels: none -> 128 us  [the longest x1 54 us: body(): pl.pallas_call(late_kernel, grid_spec=pltpu.PrefetchScalarGridSpec(num_sc...]
    psum x2 -> x0, waiting for transfers between devices: 101 us -> none  [the longest x1 52.2 us: total_grads(): inner = lax.psum(grads, 'narrow')]
    reshape x4 -> x0, local copies, waits for them, and re-layouts: 79.2 us -> none  [the longest x2 61.3 us: body(): qkv_low.reshape(traj_count, slots, 3, HEADS, head_size)]
    psum x2 -> x0, blocking collectives: 49.1 us -> none  [the longest x1 38.2 us: total_grads(): return lax.psum(inner, 'wide')]
    convert_element_type x5 -> x0, local copies, waits for them, and re-layouts: 46.5 us -> none  [the longest x2 33.5 us: body(): grad_qkv = grad_qkv.reshape(row_count, 3 * width).astype(jnp.bfloat16)]
    reduce_sum x7 -> x0, other arithmetic: 39.7 us -> none  [the longest x1 8.73 us: norm_affine(): return normalize(rows) * gain_f + bias_f]
    convert_element_type x13 -> x0, other arithmetic: 21.9 us -> none  [the longest x1 10.8 us: body(): (probs_again * (probability_gradient - row_delta)).astype(jnp.bfloat16)]
  transfers between devices with their start and end apart: 2 -> 16, of which waited for: 2 -> 6; matrix products, arithmetic and copies ran while one was open for 9% -> 0% of each run, Pallas kernels for 0% -> 41%
where the time goes in v1:
time: 150 us; the launch traced here: 151 us
  Pallas kernels  128 us (85%)
  starting transfers between devices  11 us (7%)
  waiting for transfers between devices  10.5 us (7%)
    pallas_call x1, Pallas kernels, body(): pl.pallas_call(late_kernel, grid_spec=pltpu.PrefetchScalarGridSpec(num_sc...  54 us
    pallas_call x7, Pallas kernels, stores(): pl.pallas_call(kernel, grid_spec=pltpu.PrefetchScalarGridSpec(num_scalar_...  44.8 us
    pallas_call x1, Pallas kernels, body(): pl.pallas_call(lambda *refs: attention_kernel(traj, *refs), grid_spec=plt...  16.9 us
    ppermute x16, starting transfers between devices, advance(): received[key] = self.view(lax.ppermute(self.arrays[k], AXES, perm))[0]  11 us
    ppermute x16, waiting for transfers between devices, advance(): received[key] = self.view(lax.ppermute(self.arrays[k], AXES, perm))[0]  10.5 us
    pallas_call x8, Pallas kernels, combine(): pl.pallas_call(lambda *refs: combine_kernel(step, bits_at, *refs), in_spe...  5.05 us
    pallas_call x1, Pallas kernels, body(): pl.pallas_call(lambda *refs: finish_kernel(tiles_at + 1, rows_at, *refs),...  4.33 us
  transfers between devices with their start and end apart: 16, of which 6 were waited for; matrix products, arithmetic and copies ran while one was open for 0% of the time, Pallas kernels for 41%

profile of v1, /device:TPU:0, one launch (start us, length us, event | category | flops | bytes accessed | tf_op | source)
XLA Modules:
  0.0 150.7 jit_solution(9555071424553869774)
XLA Ops:
  0.7 2.9 %plan.1.meta_ref.refs_0_ = s32[304]{0:T(512)} custom-call(s32[64]{0:T(128)} %count_ref.1, s32[1]{0:T(128)} %bitcast.rank_ref), custom_call_target="tpu_custom_call" | custom-call | tf_op jit(solution)/shard_map/plan/pallas_call | solution.py:118
  3.5 54.0 %forward_mlp.1 = (bf16[256,1024]{1,0:T(8,128)(2,1)}, bf16[8,256,1024]{2,1,0:T(8,128)(2,1)}, f32[8,8,1024]{2,1,0:T(8,128)}, bf16[8,768,1024]{2,1,0:T(8,128)(2,1)}...) custom-call(s32[304]{0:T(512)} %plan.1.meta_ref.refs_0_, ...), custom_call_target="tpu_custom_call" | custom-call | tf_op jit(solution)/shard_map/forward_mlp/pallas_call | solution.py:1032
  57.5 0.1 collective-permute-start
  57.6 0.0 copy-start.2
  57.6 0.0 copy-start.3
  57.6 16.9 %attention_backward.1 = (bf16[8,768,1024]{2,1,0:T(8,128)(2,1)}, f32[448,256]{1,0:T(8,128)}, f32[448,256]{1,0:T(8,128)}) custom-call(s32[304]{0:T(512)} %plan.1.meta_ref.refs_0_, bf16[8,256,1024]{2,1,0:T(8,128)(2,1)} %get-tuple-element.89.refs_1_.refs_4_, bf16[8,768,1024]{2,1,0:T(8,128)(2,1)} %get-tuple-element.90.refs_2_, ...), custom_call_target="tpu_custom_call" | custom-call | flops 5000000000 | bytes 16000000 | tf_op jit(solution)/shard_map/attention_backward/pallas_call | solution.py:1082
  74.6 0.0 collective-permute-start.3
  74.6 0.0 collective-permute-done.refs_2_
  74.6 0.0 copy-done.2
  74.6 0.0 copy-done.3
  74.6 0.7 combine.8
  75.3 0.1 collective-permute-start.1
  75.4 4.2 %collective-permute-start.2 = (f32[288,256]{1,0:T(8,128)S(1)}, f32[288,256]{1,0:T(8,128)S(1)}, u32[]{:S(2)}, u32[]{:S(2)}) collective-permute-start(f32[288,256]{1,0:T(8,128)S(1)} %get-tuple-element.98), channel_id=1, source_target_pairs={{0,2},{1,3},{2,0},{3,1},{4,6},{5,7},{6,4},{7,5},{8,10},{9,11},{10,... | collective-permute-start | bytes 884744 | tf_op jit(solution)/shard_map/ppermute | solution.py:845
  79.6 7.0 %tokens_backward.4.refs_8_ = bf16[64,128,256]{2,1,0:T(8,128)(2,1)} custom-call(s32[304]{0:T(512)} %plan.1.meta_ref.refs_0_, s32[64,112]{1,0:T(8,128)} %refs_1_.10, bf16[256]{0:T(256)(128)(2,1)} %refs_5_.1, bf16[256,768]{1,0:T(8,128)(2,1)} %refs_7_.1, bf16[8,256,1024]{2,1,0:T(8,128)(2,1)} %get-tuple-element.89.refs_1_.refs_4_, ...), custom_call_target="tpu_custom_call" | custom-call | flops 2000000000 | bytes 8000000 | tf_op jit(solution)/shard_map/tokens_backward/pallas_call | solution.py:1110
  86.6 0.0 collective-permute-done.3.refs_6_
  86.6 0.0 collective-permute-done.1.refs_2_
  86.6 0.0 collective-permute-done.2.refs_4_
  86.6 0.0 copy-done.4
  86.6 0.0 copy-done.11
  86.6 0.7 combine.9
  87.3 1.7 %collective-permute-start.4 = (f32[256,256]{1,0:T(8,128)S(1)}, f32[256,256]{1,0:T(8,128)S(1)}, u32[]{:S(2)}, u32[]{:S(2)}) collective-permute-start(f32[256,256]{1,0:T(8,128)S(1)} %get-tuple-element.109), channel_id=1, source_target_pairs={{0,2},{1,3},{2,0},{3,1},{4,6},{5,7},{6,4},{7,5},{8,10},{9,11},{10,... | collective-permute-start | bytes 786440 | tf_op jit(solution)/shard_map/ppermute | solution.py:845
  89.0 0.4 collective-permute-start.5
  89.4 5.3 %tokens_backward.5.refs_8_ = bf16[64,128,256]{2,1,0:T(8,128)(2,1)} custom-call(s32[304]{0:T(512)} %plan.1.meta_ref.refs_0_, s32[64,112]{1,0:T(8,128)} %refs_1_.10, bf16[256]{0:T(256)(128)(2,1)} %refs_5_.1, bf16[256,768]{1,0:T(8,128)(2,1)} %refs_7_.1, bf16[8,256,1024]{2,1,0:T(8,128)(2,1)} %get-tuple-element.89.refs_1_.refs_4_, ...), custom_call_target="tpu_custom_call", output_to_operand_aliasing={{}: (8, {})} | custom-call | flops 2000000000 | bytes 8000000 | tf_op jit(solution)/shard_map/tokens_backward/pallas_call | solution.py:1110
  94.7 0.0 collective-permute-done.4.refs_2_
  94.7 1.1 collective-permute-done.5.refs_4_
  95.8 0.0 copy-done.5
  95.8 0.6 combine.10
  96.4 0.7 collective-permute-start.7
  97.1 0.7 collective-permute-start.8
  97.8 0.0 collective-permute-start.6
  97.8 4.4 %tokens_backward.6.refs_8_ = bf16[64,128,256]{2,1,0:T(8,128)(2,1)} custom-call(s32[304]{0:T(512)} %plan.1.meta_ref.refs_0_, s32[64,112]{1,0:T(8,128)} %refs_1_.10, bf16[256]{0:T(256)(128)(2,1)} %refs_5_.1, bf16[256,768]{1,0:T(8,128)(2,1)} %refs_7_.1, bf16[8,256,1024]{2,1,0:T(8,128)(2,1)} %get-tuple-element.89.refs_1_.refs_4_, ...), custom_call_target="tpu_custom_call", output_to_operand_aliasing={{}: (8, {})} | custom-call | flops 2000000000 | bytes 8000000 | tf_op jit(solution)/shard_map/tokens_backward/pallas_call | solution.py:1110
  102.2 0.0 collective-permute-done.7.refs_4_
  102.2 0.0 collective-permute-done.8.refs_6_
  102.2 0.7 collective-permute-done.6.refs_2_
  102.9 0.6 combine.11.refs_1_
  103.5 0.0 copy-start.7
  103.5 0.1 collective-permute-start.9
  103.6 7.9 %tokens_backward.7 = bf16[64,128,256]{2,1,0:T(8,128)(2,1)} custom-call(s32[304]{0:T(512)} %plan.1.meta_ref.refs_0_, s32[64,112]{1,0:T(8,128)} %refs_1_.10, bf16[256]{0:T(256)(128)(2,1)} %refs_5_.1, bf16[256,768]{1,0:T(8,128)(2,1)} %refs_7_.1, bf16[8,256,1024]{2,1,0:T(8,128)(2,1)} %get-tuple-element.89.refs_1_.refs_4_, ...), custom_call_target="tpu_custom_call", output_to_operand_aliasing={{}: (8, {})} | custom-call | flops 2000000000 | bytes 8000000 | tf_op jit(solution)/shard_map/tokens_backward/pallas_call | solution.py:1110
  111.5 4.0 %collective-permute-done.9.refs_2_ = f32[256,256]{1,0:T(8,128)S(1)} collective-permute-done((f32[256,256]{1,0:T(8,128)S(1)}, f32[256,256]{1,0:T(8,128)S(1)}, u32[]{:S(2)}, u32[]{:S(2)}) %collective-permute-start.9) | collective-permute-done | bytes 262176 | tf_op jit(solution)/shard_map/ppermute | solution.py:845
  115.5 0.0 copy-done.7
  115.5 0.6 combine.12.refs_1_
  116.1 0.1 collective-permute-start.10
  116.1 0.0 copy-start.8
  116.1 6.5 %layer_output.3.refs_5_ = bf16[64,112,256]{2,1,0:T(8,128)(2,1)} custom-call(s32[304]{0:T(512)} %plan.1.meta_ref.refs_0_, bf16[256]{0:T(256)(128)(2,1)} %refs_1_.13, bf16[256,1024]{1,0:T(8,128)(2,1)} %get-tuple-element.130.refs_2_, bf16[8,1024,1024]{2,1,0:T(8,128)(2,1)} %get-tuple-element.131.refs_3_, f32[8,256,1024]{2,1,0:T(8,128)} %get-tuple-element.132.refs_4_), custom_call_target="tpu_custom_call" | custom-call | flops 2000000000 | bytes 8000000 | tf_op jit(solution)/shard_map/layer_output/pallas_call | solution.py:1110
  122.7 0.6 collective-permute-done.10.refs_2_
  123.2 0.0 copy-done.8
  123.2 0.6 combine.13
  123.8 1.4 collective-permute-start.11
  125.2 0.2 collective-permute-start.12
  125.4 4.9 %layer_output.4.refs_5_ = bf16[64,112,256]{2,1,0:T(8,128)(2,1)} custom-call(s32[304]{0:T(512)} %plan.1.meta_ref.refs_0_, bf16[256]{0:T(256)(128)(2,1)} %refs_1_.13, bf16[256,1024]{1,0:T(8,128)(2,1)} %get-tuple-element.130.refs_2_, bf16[8,1024,1024]{2,1,0:T(8,128)(2,1)} %get-tuple-element.131.refs_3_, ...), custom_call_target="tpu_custom_call", output_to_operand_aliasing={{}: (5, {})} | custom-call | flops 2000000000 | bytes 8000000 | tf_op jit(solution)/shard_map/layer_output/pallas_call | solution.py:1110
  130.4 0.0 collective-permute-done.11.refs_2_
  130.4 0.6 collective-permute-done.12.refs_4_
  131.0 0.0 copy-done.9
  131.0 0.6 combine.14
  131.6 1.4 collective-permute-start.13
  133.0 0.0 copy-start.13
  133.0 0.1 collective-permute-start.14
  133.1 8.8 %layer_output.5 = bf16[64,112,256]{2,1,0:T(8,128)(2,1)} custom-call(s32[304]{0:T(512)} %plan.1.meta_ref.refs_0_, bf16[256]{0:T(256)(128)(2,1)} %refs_1_.13, bf16[256,1024]{1,0:T(8,128)(2,1)} %get-tuple-element.130.refs_2_, bf16[8,1024,1024]{2,1,0:T(8,128)(2,1)} %get-tuple-element.131.refs_3_, ...), custom_call_target="tpu_custom_call", output_to_operand_aliasing={{}: (5, {})} | custom-call | flops 2000000000 | bytes 8000000 | tf_op jit(solution)/shard_map/layer_output/pallas_call | solution.py:1110
  141.9 0.0 collective-permute-done.13.refs_2_
  141.9 0.0 collective-permute-done.14.refs_4_
  141.9 0.7 combine.15.refs_1_.refs_3_
  142.6 0.1 collective-permute-start.15
  142.7 3.5 %collective-permute-done.15.refs_2_.refs_4_ = f32[1600,256]{1,0:T(8,128)S(1)} collective-permute-done((f32[1600,256]{1,0:T(8,128)S(1)}, f32[1600,256]{1,0:T(8,128)S(1)}, u32[]{:S(2)}, u32[]{:S(2)}) %collective-permute-start.15) | collective-permute-done | bytes 1638432 | tf_op jit(solution)/shard_map/ppermute | solution.py:845
  146.2 4.3 %finish.1 = (f32[1024,256]{1,0:T(8,128)}, f32[256,1024]{1,0:T(8,128)}, f32[256,256]{1,0:T(8,128)}, f32[256,768]{1,0:T(8,128)}, f32[256]{0:T(256)}, /*index=5*/f3...) custom-call(s32[304]{0:T(512)S(1)} %copy-done.10, ...), custom_call_target="tpu_custom_call" | custom-call | tf_op jit(solution)/shard_map/finish/pallas_call | solution.py:1165
  (15 shorter events, 0.0 us)
Async XLA Ops:
  57.5 17.0 %collective-permute-start = (f32[1152,256]{1,0:T(8,128)}, f32[1152,256]{1,0:T(8,128)S(1)}, u32[]{:S(2)}, u32[]{:S(2)}) collective-permute-start(f32[1152,256]{1,0:T(8,128)} %get-tuple-element.87), channel_id=1, source_target_pairs={{0,1},{1,0},{2,3},{3,2},{4,5},{5,4},{6,7},{7,6},{8,9},{9,8},{10,11... | collective-permute-start | bytes 3538952 | tf_op jit(solution)/shard_map/ppermute | solution.py:845
  57.6 17.0 %copy-start.2 = (f32[1152,256]{1,0:T(8,128)S(1)}, f32[1152,256]{1,0:T(8,128)}, u32[]{:S(2)}) copy-start(f32[1152,256]{1,0:T(8,128)} %get-tuple-element.86.refs_1_) | copy-start | bytes 3538948
  57.6 17.0 %copy-start.3 = (s32[304]{0:T(512)S(1)}, s32[304]{0:T(512)}, u32[]{:S(2)}) copy-start(s32[304]{0:T(512)} %plan.1.meta_ref.refs_0_) | copy-start | bytes 3652
  74.6 12.0 %collective-permute-start.3 = (f32[448,256]{1,0:T(8,128)}, f32[448,256]{1,0:T(8,128)S(1)}, u32[]{:S(2)}, u32[]{:S(2)}) collective-permute-start(f32[448,256]{1,0:T(8,128)} %get-tuple-element.99), channel_id=1, source_target_pairs={{0,1},{1,0},{2,3},{3,2},{4,5},{5,4},{6,7},{7,6},{8,9},{9,8},{10,11... | collective-permute-start | bytes 1376264 | tf_op jit(solution)/shard_map/ppermute | solution.py:845
  75.3 11.3 %collective-permute-start.1 = (f32[288,256]{1,0:T(8,128)S(1)}, f32[288,256]{1,0:T(8,128)S(1)}, u32[]{:S(2)}, u32[]{:S(2)}) collective-permute-start(f32[288,256]{1,0:T(8,128)S(1)} %get-tuple-element.97), channel_id=1, source_target_pairs={{0,4},{1,5},{2,6},{3,7},{4,0},{5,1},{6,2},{7,3},{8,12},{9,13},{10,... | collective-permute-start | bytes 884744 | tf_op jit(solution)/shard_map/ppermute | solution.py:845
  75.4 11.3 %collective-permute-start.2 = (f32[288,256]{1,0:T(8,128)S(1)}, f32[288,256]{1,0:T(8,128)S(1)}, u32[]{:S(2)}, u32[]{:S(2)}) collective-permute-start(f32[288,256]{1,0:T(8,128)S(1)} %get-tuple-element.98), channel_id=1, source_target_pairs={{0,2},{1,3},{2,0},{3,1},{4,6},{5,7},{6,4},{7,5},{8,10},{9,11},{10,... | collective-permute-start | bytes 884744 | tf_op jit(solution)/shard_map/ppermute | solution.py:845
  79.6 7.0 %copy-start.4 = (s32[304]{0:T(512)S(1)}, s32[304]{0:T(512)}, u32[]{:S(2)}) copy-start(s32[304]{0:T(512)} %plan.1.meta_ref.refs_0_) | copy-start | bytes 3652
  79.6 7.0 %copy-start.11 = (f32[448,256]{1,0:T(8,128)S(1)}, f32[448,256]{1,0:T(8,128)}, u32[]{:S(2)}) copy-start(f32[448,256]{1,0:T(8,128)} %get-tuple-element.94.refs_5_) | copy-start | bytes 1376260
  87.3 7.4 %collective-permute-start.4 = (f32[256,256]{1,0:T(8,128)S(1)}, f32[256,256]{1,0:T(8,128)S(1)}, u32[]{:S(2)}, u32[]{:S(2)}) collective-permute-start(f32[256,256]{1,0:T(8,128)S(1)} %get-tuple-element.109), channel_id=1, source_target_pairs={{0,2},{1,3},{2,0},{3,1},{4,6},{5,7},{6,4},{7,5},{8,10},{9,11},{10,... | collective-permute-start | bytes 786440 | tf_op jit(solution)/shard_map/ppermute | solution.py:845
  89.0 6.8 %copy-start.5 = (s32[304]{0:T(512)S(1)}, s32[304]{0:T(512)}, u32[]{:S(2)}) copy-start(s32[304]{0:T(512)} %plan.1.meta_ref.refs_0_) | copy-start | bytes 3652
  89.0 6.8 %collective-permute-start.5 = (f32[256,256]{1,0:T(8,128)S(1)}, f32[256,256]{1,0:T(8,128)S(1)}, u32[]{:S(2)}, u32[]{:S(2)}) collective-permute-start(f32[256,256]{1,0:T(8,128)S(1)} %get-tuple-element.110), channel_id=1, source_target_pairs={{0,4},{1,5},{2,6},{3,7},{4,0},{5,1},{6,2},{7,3},{8,12},{9,13},{10,... | collective-permute-start | bytes 786440 | tf_op jit(solution)/shard_map/ppermute | solution.py:845
  96.4 5.8 %collective-permute-start.7 = (f32[56,256]{1,0:T(8,128)S(1)}, f32[56,256]{1,0:T(8,128)S(1)}, u32[]{:S(2)}, u32[]{:S(2)}) collective-permute-start(f32[56,256]{1,0:T(8,128)S(1)} %get-tuple-element.119), channel_id=1, source_target_pairs={{0,2},{1,3},{2,0},{3,1},{4,6},{5,7},{6,4},{7,5},{8,10},{9,11},{10,... | collective-permute-start | bytes 172040 | tf_op jit(solution)/shard_map/ppermute | solution.py:845
  97.1 5.1 %collective-permute-start.8 = (f32[56,256]{1,0:T(8,128)S(1)}, f32[56,256]{1,0:T(8,128)S(1)}, u32[]{:S(2)}, u32[]{:S(2)}) collective-permute-start(f32[56,256]{1,0:T(8,128)S(1)} %get-tuple-element.120), channel_id=1, source_target_pairs={{0,4},{1,5},{2,6},{3,7},{4,0},{5,1},{6,2},{7,3},{8,12},{9,13},{10,... | collective-permute-start | bytes 172040 | tf_op jit(solution)/shard_map/ppermute | solution.py:845
  97.8 5.1 %copy-start.6 = (s32[304]{0:T(512)S(1)}, s32[304]{0:T(512)}, u32[]{:S(2)}) copy-start(s32[304]{0:T(512)} %plan.1.meta_ref.refs_0_) | copy-start | bytes 3652
  97.8 5.1 %collective-permute-start.6 = (f32[144,256]{1,0:T(8,128)S(1)}, f32[144,256]{1,0:T(8,128)S(1)}, u32[]{:S(2)}, u32[]{:S(2)}) collective-permute-start(f32[144,256]{1,0:T(8,128)S(1)} %get-tuple-element.118), channel_id=1, source_target_pairs={{0,8},{1,9},{2,10},{3,11},{4,12},{5,13},{6,14},{7,15},{8,0},{9,1},... | collective-permute-start | bytes 442376 | tf_op jit(solution)/shard_map/ppermute | solution.py:845
  103.5 11.9 %copy-start.7 = (s32[304]{0:T(512)S(1)}, s32[304]{0:T(512)}, u32[]{:S(2)}) copy-start(s32[304]{0:T(512)} %plan.1.meta_ref.refs_0_) | copy-start | bytes 3652
  103.5 11.9 %collective-permute-start.9 = (f32[256,256]{1,0:T(8,128)S(1)}, f32[256,256]{1,0:T(8,128)S(1)}, u32[]{:S(2)}, u32[]{:S(2)}) collective-permute-start(f32[256,256]{1,0:T(8,128)S(1)} %combine.11.refs_1_), channel_id=1, source_target_pairs={{0,16},{1,17},{2,18},{3,19},{4,20},{5,21},{6,22},{7,23},{8,24},{9,... | collective-permute-start | bytes 786440 | tf_op jit(solution)/shard_map/ppermute | solution.py:845
  116.1 7.2 %collective-permute-start.10 = (f32[256,256]{1,0:T(8,128)S(1)}, f32[256,256]{1,0:T(8,128)S(1)}, u32[]{:S(2)}, u32[]{:S(2)}) collective-permute-start(f32[256,256]{1,0:T(8,128)S(1)} %combine.12.refs_1_), channel_id=1, source_target_pairs={{0,8},{1,9},{2,10},{3,11},{4,12},{5,13},{6,14},{7,15},{8,0},{9,1},... | collective-permute-start | bytes 786440 | tf_op jit(solution)/shard_map/ppermute | solution.py:845
  116.1 7.1 %copy-start.8 = (s32[304]{0:T(512)S(1)}, s32[304]{0:T(512)}, u32[]{:S(2)}) copy-start(s32[304]{0:T(512)} %plan.1.meta_ref.refs_0_) | copy-start | bytes 3652
  123.8 6.5 %collective-permute-start.11 = (f32[200,256]{1,0:T(8,128)S(1)}, f32[200,256]{1,0:T(8,128)S(1)}, u32[]{:S(2)}, u32[]{:S(2)}) collective-permute-start(f32[200,256]{1,0:T(8,128)S(1)} %get-tuple-element.134.refs_1_), channel_id=1, source_target_pairs={{0,2},{1,3},{2,0},{3,1},{4,6},{5,7},{6,4},{7,5},{8,10},{9,11},{10,... | collective-permute-start | bytes 614408 | tf_op jit(solution)/shard_map/ppermute | solution.py:845
  125.2 5.8 %copy-start.9 = (s32[304]{0:T(512)S(1)}, s32[304]{0:T(512)}, u32[]{:S(2)}) copy-start(s32[304]{0:T(512)} %plan.1.meta_ref.refs_0_) | copy-start | bytes 3652
  125.2 5.8 %collective-permute-start.12 = (f32[200,256]{1,0:T(8,128)S(1)}, f32[200,256]{1,0:T(8,128)S(1)}, u32[]{:S(2)}, u32[]{:S(2)}) collective-permute-start(f32[200,256]{1,0:T(8,128)S(1)} %get-tuple-element.135.refs_3_), channel_id=1, source_target_pairs={{0,4},{1,5},{2,6},{3,7},{4,0},{5,1},{6,2},{7,3},{8,12},{9,13},{10,... | collective-permute-start | bytes 614408 | tf_op jit(solution)/shard_map/ppermute | solution.py:845
  131.6 10.3 %collective-permute-start.13 = (f32[400,256]{1,0:T(8,128)S(1)}, f32[400,256]{1,0:T(8,128)S(1)}, u32[]{:S(2)}, u32[]{:S(2)}) collective-permute-start(f32[400,256]{1,0:T(8,128)S(1)} %get-tuple-element.139.refs_1_), channel_id=1, source_target_pairs={{0,4},{1,5},{2,6},{3,7},{4,0},{5,1},{6,2},{7,3},{8,12},{9,13},{10,... | collective-permute-start | bytes 1228808 | tf_op jit(solution)/shard_map/ppermute | solution.py:845
  133.0 8.9 %copy-start.10 = (s32[304]{0:T(512)S(1)}, s32[304]{0:T(512)}, u32[]{:S(2)}) copy-start(s32[304]{0:T(512)} %plan.1.meta_ref.refs_0_) | copy-start | bytes 3652
  133.0 13.2 %copy-start = (bf16[256,768]{1,0:T(8,128)(2,1)S(1)}, bf16[256,768]{1,0:T(8,128)(2,1)}, u32[]{:S(2)}) copy-start(bf16[256,768]{1,0:T(8,128)(2,1)} %refs_7_.1) | copy-start | bytes 1179652
  133.0 13.2 %copy-start.1 = (bf16[256,1024]{1,0:T(8,128)(2,1)S(1)}, bf16[256,1024]{1,0:T(8,128)(2,1)}, u32[]{:S(2)}) copy-start(bf16[256,1024]{1,0:T(8,128)(2,1)} %refs_8_.1) | copy-start | bytes 1572868
  133.0 13.2 %copy-start.12 = (bf16[256]{0:T(256)(128)(2,1)S(1)}, bf16[256]{0:T(256)(128)(2,1)}, u32[]{:S(2)}) copy-start(bf16[256]{0:T(256)(128)(2,1)} %refs_5_.1) | copy-start | bytes 1540
  133.0 13.2 %copy-start.13 = (bf16[256]{0:T(256)(128)(2,1)S(1)}, bf16[256]{0:T(256)(128)(2,1)}, u32[]{:S(2)}) copy-start(bf16[256]{0:T(256)(128)(2,1)} %refs_6_.1) | copy-start | bytes 1540
  133.0 8.9 %collective-permute-start.14 = (f32[400,256]{1,0:T(8,128)S(1)}, f32[400,256]{1,0:T(8,128)S(1)}, u32[]{:S(2)}, u32[]{:S(2)}) collective-permute-start(f32[400,256]{1,0:T(8,128)S(1)} %get-tuple-element.140.refs_3_), channel_id=1, source_target_pairs={{0,2},{1,3},{2,0},{3,1},{4,6},{5,7},{6,4},{7,5},{8,10},{9,11},{10,... | collective-permute-start | bytes 1228808 | tf_op jit(solution)/shard_map/ppermute | solution.py:845
  142.6 3.6 %collective-permute-start.15 = (f32[1600,256]{1,0:T(8,128)S(1)}, f32[1600,256]{1,0:T(8,128)S(1)}, u32[]{:S(2)}, u32[]{:S(2)}) collective-permute-start(f32[1600,256]{1,0:T(8,128)S(1)} %combine.15.refs_1_.refs_3_), channel_id=1, source_target_pairs={{0,1},{1,0},{2,3},{3,2},{4,5},{5,4},{6,7},{7,6},{8,9},{9,8},{10,11... | collective-permute-start | bytes 4915208 | tf_op jit(solution)/shard_map/ppermute | solution.py:845

commit v2 on v1

--- a/solution.py
+++ b/solution.py
@@ -199,12 +199,6 @@
 
     def stop(self, tiles):
         return lax.shift_right_logical(tiles * self.last, 4)
-
-    def most(self, fewest, most):
-        return max((n * self.last >> 4) - (n * self.first >> 4) for n in range(fewest, most + 1))
-
-    def block(self, tiles_at):
-        return lambda i, meta: jnp.minimum(self.start(meta[tiles_at]) + i, self.stop(meta[tiles_at]) - 1)
 
 
 def shares(*cuts):
@@ -267,7 +261,7 @@
     u_s,
     ga_s,
     gp_s,
-    gb_s,
+    mid_s,
     gs_s,
     acc_s,
     bacc_s,
@@ -372,12 +366,12 @@
 
         def residual(t):
             lanes = pair_lanes(t)
-            mid_ref[0, :, lanes] = mm(wot_s[...], att_s[:, lanes])
+            mid_s[:, lanes] = mm(wot_s[...], att_s[:, lanes])
 
         def second_norm(b):
             lanes = bin_lanes(b)
-            mid = mid_ref[0, :, lanes] + gath_s[:, lanes] + col(5)
-            mid_ref[0, :, lanes] = mid
+            mid = mid_s[:, lanes] + gath_s[:, lanes] + col(5)
+            mid_ref[0, :, lanes] = mid.astype(BF16)
             nhat, rstds[b] = center(mid)
             nhat_s[:, lanes] = nhat
             sec_s[:, lanes] = (nhat * col(6) + col(7)).astype(BF16)
@@ -398,7 +392,7 @@
             gp_s[rows, lanes] = gp.astype(BF16)
             bacc_s[d + rows.start : d + rows.stop, :] += gp[:, 0:BIN] + gp[:, BIN:PAIR]
 
-        def down(t):
+        def grad_second(t):
             lanes = pair_lanes(t)
             gs_s[:, lanes] = mm(wup_ref[...], gp_s[:, lanes])
 
@@ -412,48 +406,43 @@
             m2 = jnp.mean(a * nhat, axis=0, keepdims=True)
             gm = gm_s[:, lanes].astype(F32)
             gmid = gm + rstds[b] * (a - m1 - nhat * m2)
-            gmid_ref[0, :, lanes] = gmid
-            gb_s[:, lanes] = gmid.astype(BF16)
+            gmid_ref[0, :, lanes] = gmid.astype(BF16)
             bacc_s[d + ff : 2 * d + ff, :] += gm
             bacc_s[2 * d + ff : 3 * d + ff, :] += gmid
 
         def grad_attended(t):
             lanes = pair_lanes(t)
-            gatt_ref[0, :, lanes] = mm(wo_ref[...], gb_s[:, lanes]).astype(BF16)
+            gatt_ref[0, :, lanes] = mm(wo_ref[...], gmid_ref[0, :, lanes]).astype(BF16)
 
         def work(count):
             bins, tiles, chunk, lanes = range(count), range(count // 2), 32, slice(0, count * BIN)
+            pairs = [[(b, p) for b in (2 * t, 2 * t + 1) for p in range(HEADS // 2)] for t in tiles]
+            stages = dict(
+                cotangent=lambda t: [cotangent(b) for b in (2 * t, 2 * t + 1)],
+                first_norm=lambda t: [first_norm(b) for b in (2 * t, 2 * t + 1)],
+                project=project,
+                scores=lambda t: [scores(b, p) for b, p in pairs[t]],
+                softmax=lambda t: [softmax(b) for b in (2 * t, 2 * t + 1)],
+                attend=lambda t: [attend(b, p) for b, p in pairs[t]],
+                residual=residual,
+                second_norm=lambda t: [second_norm(b) for b in (2 * t, 2 * t + 1)],
+                up=up,
+                gelu=lambda t: [gelu(t, slice(j, j + chunk)) for j in range(0, ff, chunk)],
+                grad_second=grad_second,
+            )
             for b in bins:
                 gather(b)
-            for b in bins:
-                cotangent(b)
-            for b in bins:
-                first_norm(b)
-            for t in tiles:
-                project(t)
-            pairs = [(b, p) for b in bins for p in range(HEADS // 2)]
-            for b, p in pairs:
-                scores(b, p)
-            for b in bins:
-                softmax(b)
-            for b, p in pairs:
-                attend(b, p)
-            for t in tiles:
-                residual(t)
-            for b in bins:
-                second_norm(b)
-            for t in tiles:
-                up(t)
-            for t in tiles:
-                for j in range(ff // chunk):
-                    gelu(t, slice(j * chunk, (j + 1) * chunk))
+            for when in range(len(tiles) + len(stages) - 1):
+                for n, stage in enumerate(stages.values()):
+                    if 0 <= when - n < len(tiles):
+                        stage(when - n)
             acc_s[0:ff, :] += mm(act_ref[0, :, lanes], gm_s[:, lanes], NT)
+            for b in bins[: count // 2]:
+                second_norm_back(b)
             acc_s[ff : 2 * ff, :] += mm(gp_s[:, lanes], sec_s[:, lanes], NT)
-            for t in tiles:
-                down(t)
-            for b in bins:
+            for b in bins[count // 2 :]:
                 second_norm_back(b)
-            acc_s[2 * ff : 2 * ff + d, :] += mm(att_s[:, lanes], gb_s[:, lanes], NT)
+            acc_s[2 * ff : 2 * ff + d, :] += mm(att_s[:, lanes], gmid_ref[0, :, lanes], NT)
             for t in tiles:
                 grad_attended(t)
 
@@ -551,86 +540,130 @@
         keep_half(meta, acc_s, keep_ref, send_ref)
 
 
-def token_kernel(share, meta_ref, idx_ref, g1_ref, wqkv_ref, nhat1_ref, rstd1_ref, gq_ref, gmid_ref, *refs):
-    tg_ref, idx_s, col_s, gg_s, rows_s, sems = refs[-6:]
-    step = pl.program_id(0)
+def token_kernel(share, meta_ref, g1_ref, idx_ref, wqkv_ref, nhat1_ref, rstd1_ref, gq_ref, gmid_ref, *refs):
+    tg_ref, idx_in, wqkv_s, nhat1_s, rstd1_s, gq_s, gmid_s, sems, idx_s, col_s, gg_s, rows_s, out_sems = refs[-13:]
     traj, slots = idx_ref.shape
     seq, d = tg_ref.shape[1:]
     meta = Meta(meta_ref, traj)
 
-    @pl.when(step == 0)
-    def _():
+    def prepare():
         idx_s[...] = jnp.zeros_like(idx_s)
-        idx_s[:, 0:slots] = idx_ref[...]
+        idx_s[:, 0:slots] = idx_in[...]
         row = jnp.broadcast_to(g1_ref[...].astype(F32).reshape(1, d), (8, d))
         col_s[...] = jnp.broadcast_to(row.T[:, 0:1], (d, BIN))
 
     def rows_of(tile, slot):
-        gfs = [mm(wqkv_ref[...], gq_ref[0, :, pair_lanes(t)]) for t in range(BINS // 2)]
+        for b in range(BINS):
+            gg_s[:, bin_lanes(b)] = bin_onehot(idx_s, *meta.bin(tile * BINS + b), seq)
+        gfs = [mm(wqkv_s[...], gq_s[slot, :, pair_lanes(t)]) for t in range(BINS // 2)]
+        grads = []
         for b in range(BINS):
             lanes = bin_lanes(b)
-            nhat = nhat1_ref[0, :, lanes].astype(F32)
+            nhat = nhat1_s[slot, :, lanes].astype(F32)
             a = gfs[b // 2][:, bin_lanes(b % 2)] * col_s[...]
             m1 = jnp.mean(a, axis=0, keepdims=True)
             m2 = jnp.mean(a * nhat, axis=0, keepdims=True)
-            rstd = rstd1_ref[0, 0:1, lanes]
-            gg_s[:, lanes] = (gmid_ref[0, :, lanes] + rstd * (a - m1 - nhat * m2)).astype(BF16)
+            rstd = rstd1_s[slot, 0:1, lanes]
+            grads.append((gmid_s[slot, :, lanes].astype(F32) + rstd * (a - m1 - nhat * m2)).astype(BF16))
         for b in range(BINS):
-            onehot = bin_onehot(idx_s, *meta.bin(tile * BINS + b), seq)
-            rows_s[slot, b] = mm(onehot, gg_s[:, bin_lanes(b)], NT).astype(BF16)
-
-    store_tiles(share, meta, step, rows_of, rows_s, tg_ref, seq, sems)
-
-
-def store_tiles(share, meta, step, rows_of, rows_s, to_ref, rows, sems):
+            rows_s[slot, b] = mm(gg_s[:, bin_lanes(b)], grads[b], NT).astype(BF16)
+
+    store_tiles(
+        share,
+        meta,
+        [(idx_ref, idx_in), (wqkv_ref, wqkv_s)],
+        [(nhat1_ref, nhat1_s), (rstd1_ref, rstd1_s), (gq_ref, gq_s), (gmid_ref, gmid_s)],
+        sems,
+        prepare,
+        rows_of,
+        rows_s,
+        tg_ref,
+        seq,
+        out_sems,
+    )
+
+
+def store_tiles(share, meta, once, each, sems, prepare, rows_of, rows_s, to_ref, rows, out_sems):
     first, stop = share.start(meta.tiles()), share.stop(meta.tiles())
-    tile = first + step
-    slot = jnp.bitwise_and(step, 1)
-
-    def leave(tile, slot, act):
-        departures(meta, tile, rows_s, slot, to_ref, rows, sems, act)
-
-    @pl.when(tile < stop)
+    done = stop - first
+
+    def constant(act):
+        for k, (ref, place) in enumerate(once):
+            act(pltpu.make_async_copy(ref, place, sems.at[2, k]))
+
+    def come(tile, slot, act):
+        lanes = pl.ds(pl.multiple_of(jnp.bitwise_and(tile, 1) * TILE, TILE), TILE)
+        for k, (ref, place) in enumerate(each):
+            act(
+                pltpu.make_async_copy(
+                    ref.at[lax.shift_right_logical(tile, 1), :, lanes], place.at[slot], sems.at[slot, k]
+                )
+            )
+
+    def leave(i, act):
+        departures(meta, first + i, rows_s, jnp.bitwise_and(i, 1), to_ref, rows, out_sems, act)
+
+    constant(lambda c: c.start())
+    come(first, 0, lambda c: c.start())
+    constant(lambda c: c.wait())
+    prepare()
+
+    def step(i, carry):
+        slot = jnp.bitwise_and(i, 1)
+        come(first + i, slot, lambda c: c.wait())
+
+        @pl.when(i + 1 < done)
+        def _():
+            come(first + i + 1, 1 - slot, lambda c: c.start())
+
+        @pl.when(i >= 2)
+        def _():
+            leave(i - 2, lambda c: c.wait())
+
+        rows_of(first + i, slot)
+        leave(i, lambda c: c.start())
+        return carry
+
+    lax.fori_loop(0, done, step, 0)
+
+    @pl.when(done >= 2)
     def _():
-        @pl.when(step >= 2)
-        def _():
-            leave(tile - 2, slot, lambda c: c.wait())
-
-        rows_of(tile, slot)
-        leave(tile, slot, lambda c: c.start())
-
-    @pl.when(step == pl.num_programs(0) - 1)
-    def _():
-        done = stop - first
-
-        @pl.when(done >= 2)
-        def _():
-            leave(stop - 2, jnp.bitwise_and(done, 1), lambda c: c.wait())
-
-        leave(stop - 1, jnp.bitwise_and(done - 1, 1), lambda c: c.wait())
+        leave(done - 2, lambda c: c.wait())
+
+    leave(done - 1, lambda c: c.wait())
 
 
 def output_kernel(share, traj, meta_ref, bdn_ref, wdnt_ref, act_ref, mid_ref, *refs):
-    lay_ref, col_s, y_s, rows_s, sems = refs[-5:]
-    step = pl.program_id(0)
+    lay_ref, wdnt_s, act_s, mid_s, sems, col_s, y_s, rows_s, out_sems = refs[-9:]
     slots, d = lay_ref.shape[1:]
     meta = Meta(meta_ref, traj)
 
-    @pl.when(step == 0)
-    def _():
+    def prepare():
         row = jnp.broadcast_to(bdn_ref[...].astype(F32).reshape(1, d), (8, d))
         col_s[...] = jnp.broadcast_to(row.T[:, 0:1], (d, BIN))
 
     def rows_of(tile, slot):
         for t in range(BINS // 2):
             lanes = pair_lanes(t)
-            mlp = mm(wdnt_ref[...], act_ref[0, :, lanes])
-            y_s[:, lanes] = (mlp + mid_ref[0, :, lanes] + two(col_s[...])).astype(BF16)
+            mlp = mm(wdnt_s[...], act_s[slot, :, lanes])
+            y_s[:, lanes] = (mlp + mid_s[slot, :, lanes].astype(F32) + two(col_s[...])).astype(BF16)
         for b in range(BINS):
             _, _, ca, cb = meta.bin(tile * BINS + b)
             rows_s[slot, b] = mm(bin_slots(ca, cb), y_s[:, bin_lanes(b)], NT).astype(BF16)
 
-    store_tiles(share, meta, step, rows_of, rows_s, lay_ref, slots, sems)
+    store_tiles(
+        share,
+        meta,
+        [(wdnt_ref, wdnt_s)],
+        [(act_ref, act_s), (mid_ref, mid_s)],
+        sems,
+        prepare,
+        rows_of,
+        rows_s,
+        lay_ref,
+        slots,
+        out_sems,
+    )
 
 
 CORE, Y, X, Z = 0, 1, 2, 3
@@ -942,18 +975,6 @@
     return pl.BlockSpec((1,) + shape, lambda i, meta: (at(i, meta),) + rest)
 
 
-def per_tile(shape, at):
-    axis = 0 if len(shape) == 3 else len(shape) - 1
-
-    def index(i, meta):
-        tile = at(i, meta)
-        place = [0] * len(shape)
-        place[axis] = jnp.bitwise_and(tile, 1)
-        return (lax.shift_right_logical(tile, 1), *place)
-
-    return pl.BlockSpec((1,) + shape, index)
-
-
 def doubled(shape):
     if len(shape) == 3:
         return (2 * shape[0],) + shape[1:]
@@ -1012,9 +1033,9 @@
         qkv=((3 * d, TILE), BF16),
         prob=((BINS, BIN, HEADS * BIN), BF16),
         gatt=((d, TILE), BF16),
-        gmid=((d, TILE), F32),
+        gmid=((d, TILE), BF16),
         act=((ff, TILE), BF16),
-        mid=((d, TILE), F32),
+        mid=((d, TILE), BF16),
     )
 
     def stored(name):
@@ -1060,7 +1081,7 @@
                 pltpu.VMEM((ff, TILE_A), F32),
                 pltpu.VMEM((ff, TILE_A), F32),
                 pltpu.VMEM((ff, TILE_A), BF16),
-                pltpu.VMEM((d, TILE_A), BF16),
+                pltpu.VMEM((d, TILE_A), F32),
                 pltpu.VMEM((d, TILE_A), F32),
                 pltpu.VMEM(late_shape, F32),
                 pltpu.VMEM((3 * d + ff, BIN), F32),
@@ -1103,54 +1124,54 @@
     sums.add("first", first)
     sums.advance(first_keep)
 
-    fewest = -(-traj // (2 * BINS))
-
-    def stores(kernel, share, name, inputs, in_specs, rows, scratch, earlier):
+    smem, vmem = (pl.BlockSpec(memory_space=m) for m in (pltpu.SMEM, pltpu.VMEM))
+
+    def tile_places(*names):
+        shapes_of = dict(shapes, gq=((3 * d, TILE), BF16))
+        return [pltpu.VMEM((2,) + shapes_of[n][0], shapes_of[n][1]) for n in names]
+
+    def stores(kernel, name, vector, inputs, rows, scratch, earlier):
         given = [] if earlier is None else [earlier]
         return pl.pallas_call(
             kernel,
-            grid_spec=pltpu.PrefetchScalarGridSpec(
-                num_scalar_prefetch=1,
-                grid=(share.most(fewest, tiles),),
-                in_specs=in_specs + [HBM] * len(given),
-                out_specs=HBM,
-                scratch_shapes=scratch
-                + [pltpu.VMEM((2, BINS, 2 * BIN, d), BF16), pltpu.SemaphoreType.DMA((2, BINS, 2))],
-            ),
+            in_specs=[smem, vmem] + [HBM] * (len(inputs) + len(given)),
+            out_specs=HBM,
+            scratch_shapes=scratch
+            + [pltpu.VMEM((2, BINS, 2 * BIN, d), BF16), pltpu.SemaphoreType.DMA((2, BINS, 2))],
             out_shape=jax.ShapeDtypeStruct((traj, rows, d), BF16),
-            input_output_aliases={1 + len(inputs): 0} if given else {},
-            compiler_params=params(56),
+            input_output_aliases={2 + len(inputs): 0} if given else {},
+            compiler_params=pltpu.CompilerParams(vmem_limit_bytes=56 * MIB),
             cost_estimate=pl.CostEstimate(flops=2 * 10**9, bytes_accessed=8 * 10**6, transcendentals=0),
             name=name,
-        )(sums.ordered(meta), *inputs, *given)
+        )(sums.ordered(meta), vector, *inputs, *given)
 
     tokens_grad = None
     for share in SHARES_C:
-        at = share.block(tiles_at)
         tokens_grad = stores(
             lambda *refs, share=share: token_kernel(share, *refs),
-            share,
             "tokens_backward",
-            [visible_index, ln1_gain, qkv_weight, nhat, rstd, grad_qkv, gmid],
-            [whole((traj, slots)), whole((d,)), whole((d, 3 * d))]
-            + [per_tile(shapes["nhat"][0], at), per_tile(shapes["rstd"][0], at)]
-            + [per_tile((3 * d, TILE), at), per_tile(shapes["gmid"][0], at)],
+            ln1_gain,
+            [visible_index, qkv_weight, nhat, rstd, grad_qkv, gmid],
             seq,
-            [pltpu.VMEM((traj, BIN), jnp.int32), pltpu.VMEM((d, BIN), F32), pltpu.VMEM((d, TILE), BF16)],
+            [pltpu.VMEM((traj, slots), jnp.int32), pltpu.VMEM((d, 3 * d), BF16)]
+            + tile_places("nhat", "rstd", "gq", "gmid")
+            + [pltpu.SemaphoreType.DMA((3, 4))]
+            + [pltpu.VMEM((traj, BIN), jnp.int32), pltpu.VMEM((d, BIN), F32), pltpu.VMEM((d, TILE), BF16)],
             tokens_grad,
         )
         sums.advance(tokens_grad)
     layer_out = None
     for share in SHARES_D:
-        at = share.block(tiles_at)
         layer_out = stores(
             lambda *refs, share=share: output_kernel(share, traj, *refs),
-            share,
             "layer_output",
-            [down_bias, down_weight_t, act, mid],
-            [whole((d,)), whole((d, ff)), per_tile(shapes["act"][0], at), per_tile(shapes["mid"][0], at)],
+            down_bias,
+            [down_weight_t, act, mid],
             slots,
-            [pltpu.VMEM((d, BIN), F32), pltpu.VMEM((d, TILE), BF16)],
+            [pltpu.VMEM((d, ff), BF16)]
+            + tile_places("act", "mid")
+            + [pltpu.SemaphoreType.DMA((3, 4))]
+            + [pltpu.VMEM((d, BIN), F32), pltpu.VMEM((d, TILE), BF16)],
             layer_out,
         )
         sums.advance(layer_out)

time: 150 us -> 151 us (level); the launches traced: 151 us -> 149 us
  Pallas kernels: 128 us -> 110 us
  starting transfers between devices: 11 us -> 25.7 us
  waiting for transfers between devices: 10.5 us -> 12.5 us
    ppermute x16, starting transfers between devices: 11 us -> 25.7 us  [advance(): received[key] = self.view(lax.ppermute(self.arrays[k], AXES, perm))[0]]
    pallas_call x1, Pallas kernels: 54 us -> 44.2 us  [body(): pl.pallas_call(late_kernel, grid_spec=pltpu.PrefetchScalarGridSpec(num_sc...]
    pallas_call x7, Pallas kernels: 44.8 us -> 39.1 us  [stores(): pl.pallas_call(kernel, in_specs=[smem, vmem] + [HBM] * (len(inputs) + len...]
    pallas_call x1, Pallas kernels: 16.9 us -> 14.4 us  [body(): pl.pallas_call(lambda *refs: attention_kernel(traj, *refs), grid_spec=plt...]
    ppermute x16, waiting for transfers between devices: 10.5 us -> 12.5 us  [advance(): received[key] = self.view(lax.ppermute(self.arrays[k], AXES, perm))[0]]
  transfers between devices with their start and end apart: 16 -> 16, of which waited for: 6 -> 9; matrix products, arithmetic and copies ran while one was open for 0% -> 0% of each run, Pallas kernels for 41% -> 36%
where the time goes in v2:
time: 151 us; the launch traced here: 149 us
  Pallas kernels  110 us (73%)
  starting transfers between devices  25.7 us (17%)
  waiting for transfers between devices  12.5 us (8%)
    pallas_call x1, Pallas kernels, body(): pl.pallas_call(late_kernel, grid_spec=pltpu.PrefetchScalarGridSpec(num_sc...  44.2 us
    pallas_call x7, Pallas kernels, stores(): pl.pallas_call(kernel, in_specs=[smem, vmem] + [HBM] * (len(inputs) + len...  39.1 us
    ppermute x16, starting transfers between devices, advance(): received[key] = self.view(lax.ppermute(self.arrays[k], AXES, perm))[0]  25.7 us
    pallas_call x1, Pallas kernels, body(): pl.pallas_call(lambda *refs: attention_kernel(traj, *refs), grid_spec=plt...  14.4 us
    ppermute x16, waiting for transfers between devices, advance(): received[key] = self.view(lax.ppermute(self.arrays[k], AXES, perm))[0]  12.5 us
    pallas_call x8, Pallas kernels, combine(): pl.pallas_call(lambda *refs: combine_kernel(step, bits_at, *refs), in_spe...  5.05 us
    pallas_call x1, Pallas kernels, body(): pl.pallas_call(lambda *refs: finish_kernel(tiles_at + 1, rows_at, *refs),...  4.33 us
  transfers between devices with their start and end apart: 16, of which 9 were waited for; matrix products, arithmetic and copies ran while one was open for 0% of the time, Pallas kernels for 36%

profile of v2, /device:TPU:0, one launch (start us, length us, event | category | flops | bytes accessed | tf_op | source)
XLA Modules:
  0.0 149.3 jit_solution(18117285046225235739)
XLA Ops:
  0.7 2.8 %plan.1.meta_ref.refs_0_ = s32[304]{0:T(512)} custom-call(s32[64]{0:T(128)} %count_ref.1, s32[1]{0:T(128)} %bitcast.rank_ref), custom_call_target="tpu_custom_call" | custom-call | tf_op jit(solution)/shard_map/plan/pallas_call | solution.py:118
  3.4 44.2 %forward_mlp.1 = (bf16[256,1024]{1,0:T(8,128)(2,1)}, bf16[8,256,1024]{2,1,0:T(8,128)(2,1)}, f32[8,8,1024]{2,1,0:T(8,128)}, bf16[8,768,1024]{2,1,0:T(8,128)(2,1)}...) custom-call(s32[304]{0:T(512)} %plan.1.meta_ref.refs_0_, ...), custom_call_target="tpu_custom_call" | custom-call | tf_op jit(solution)/shard_map/forward_mlp/pallas_call | solution.py:1053
  47.7 5.4 %collective-permute-start = (f32[1152,256]{1,0:T(8,128)}, f32[1152,256]{1,0:T(8,128)S(1)}, u32[]{:S(2)}, u32[]{:S(2)}) collective-permute-start(f32[1152,256]{1,0:T(8,128)} %get-tuple-element.87), channel_id=1, source_target_pairs={{0,1},{1,0},{2,3},{3,2},{4,5},{5,4},{6,7},{7,6},{8,9},{9,8},{10,11... | collective-permute-start | bytes 3538952 | tf_op jit(solution)/shard_map/ppermute | solution.py:878
  53.1 14.4 %attention_backward.1 = (bf16[8,768,1024]{2,1,0:T(8,128)(2,1)}, f32[448,256]{1,0:T(8,128)}, f32[448,256]{1,0:T(8,128)}) custom-call(s32[304]{0:T(512)} %plan.1.meta_ref.refs_0_, bf16[8,256,1024]{2,1,0:T(8,128)(2,1)} %get-tuple-element.89.refs_1_.refs_4_, bf16[8,768,1024]{2,1,0:T(8,128)(2,1)} %get-tuple-element.90.refs_2_, ...), custom_call_target="tpu_custom_call" | custom-call | flops 5000000000 | bytes 16000000 | tf_op jit(solution)/shard_map/attention_backward/pallas_call | solution.py:1103
  67.5 1.5 %collective-permute-start.3 = (f32[448,256]{1,0:T(8,128)}, f32[448,256]{1,0:T(8,128)S(1)}, u32[]{:S(2)}, u32[]{:S(2)}) collective-permute-start(f32[448,256]{1,0:T(8,128)} %get-tuple-element.99), channel_id=1, source_target_pairs={{0,1},{1,0},{2,3},{3,2},{4,5},{5,4},{6,7},{7,6},{8,9},{9,8},{10,11... | collective-permute-start | bytes 1376264 | tf_op jit(solution)/shard_map/ppermute | solution.py:878
  69.0 0.0 collective-permute-done.refs_2_
  69.0 0.0 copy-done.2
  69.0 0.0 copy-done.3
  69.0 0.7 combine.8
  69.7 3.0 %collective-permute-start.1 = (f32[288,256]{1,0:T(8,128)S(1)}, f32[288,256]{1,0:T(8,128)S(1)}, u32[]{:S(2)}, u32[]{:S(2)}) collective-permute-start(f32[288,256]{1,0:T(8,128)S(1)} %get-tuple-element.97), channel_id=1, source_target_pairs={{0,4},{1,5},{2,6},{3,7},{4,0},{5,1},{6,2},{7,3},{8,12},{9,13},{10,... | collective-permute-start | bytes 884744 | tf_op jit(solution)/shard_map/ppermute | solution.py:878
  72.7 0.9 collective-permute-start.2
  73.7 5.4 %tokens_backward.4.refs_8_ = bf16[64,128,256]{2,1,0:T(8,128)(2,1)} custom-call(s32[304]{0:T(512)} %plan.1.meta_ref.refs_0_, bf16[256]{0:T(256)(128)(2,1)} %refs_5_.1, s32[64,112]{1,0:T(8,128)} %refs_2_.7, bf16[256,768]{1,0:T(8,128)(2,1)} %refs_7_.1, bf16[8,256,1024]{2,1,0:T(8,128)(2,1)} %get-tuple-element.89.refs_1_.refs_4_, ...), custom_call_target="tpu_custom_call" | custom-call | flops 2000000000 | bytes 8000000 | tf_op jit(solution)/shard_map/tokens_backward/pallas_call | solution.py:1135
  79.1 0.0 collective-permute-done.3.refs_6_
  79.1 0.9 collective-permute-done.1.refs_2_
  80.0 1.5 collective-permute-done.2.refs_4_
  81.4 0.0 copy-done.4
  81.4 0.0 copy-done.11
  81.4 0.7 combine.9
  82.1 1.0 collective-permute-start.4
  83.1 1.2 collective-permute-start.5
  84.3 5.2 %tokens_backward.5.refs_8_ = bf16[64,128,256]{2,1,0:T(8,128)(2,1)} custom-call(s32[304]{0:T(512)} %plan.1.meta_ref.refs_0_, bf16[256]{0:T(256)(128)(2,1)} %refs_5_.1, s32[64,112]{1,0:T(8,128)} %refs_2_.7, bf16[256,768]{1,0:T(8,128)(2,1)} %refs_7_.1, bf16[8,256,1024]{2,1,0:T(8,128)(2,1)} %get-tuple-element.89.refs_1_.refs_4_, ...), custom_call_target="tpu_custom_call", output_to_operand_aliasing={{}: (8, {})} | custom-call | flops 2000000000 | bytes 8000000 | tf_op jit(solution)/shard_map/tokens_backward/pallas_call | solution.py:1135
  89.5 0.0 collective-permute-done.4.refs_2_
  89.5 0.4 collective-permute-done.5.refs_4_
  89.9 0.0 copy-done.5
  89.9 0.6 combine.10
  90.5 1.2 collective-permute-start.7
  91.7 0.7 collective-permute-start.8
  92.4 5.5 %collective-permute-start.6 = (f32[144,256]{1,0:T(8,128)S(1)}, f32[144,256]{1,0:T(8,128)S(1)}, u32[]{:S(2)}, u32[]{:S(2)}) collective-permute-start(f32[144,256]{1,0:T(8,128)S(1)} %get-tuple-element.118), channel_id=1, source_target_pairs={{0,8},{1,9},{2,10},{3,11},{4,12},{5,13},{6,14},{7,15},{8,0},{9,1},... | collective-permute-start | bytes 442376 | tf_op jit(solution)/shard_map/ppermute | solution.py:878
  97.9 4.0 %tokens_backward.6.refs_8_ = bf16[64,128,256]{2,1,0:T(8,128)(2,1)} custom-call(s32[304]{0:T(512)} %plan.1.meta_ref.refs_0_, bf16[256]{0:T(256)(128)(2,1)} %refs_5_.1, s32[64,112]{1,0:T(8,128)} %refs_2_.7, bf16[256,768]{1,0:T(8,128)(2,1)} %refs_7_.1, bf16[8,256,1024]{2,1,0:T(8,128)(2,1)} %get-tuple-element.89.refs_1_.refs_4_, ...), custom_call_target="tpu_custom_call", output_to_operand_aliasing={{}: (8, {})} | custom-call | flops 2000000000 | bytes 8000000 | tf_op jit(solution)/shard_map/tokens_backward/pallas_call | solution.py:1135
  101.9 0.0 collective-permute-done.7.refs_4_
  101.9 0.0 collective-permute-done.8.refs_6_
  101.9 0.0 collective-permute-done.6.refs_2_
  101.9 0.0 copy-done.6
  101.9 0.6 combine.11.refs_1_
  102.5 0.0 copy-start.7
  102.5 0.1 collective-permute-start.9
  102.6 6.6 %tokens_backward.7 = bf16[64,128,256]{2,1,0:T(8,128)(2,1)} custom-call(s32[304]{0:T(512)} %plan.1.meta_ref.refs_0_, bf16[256]{0:T(256)(128)(2,1)} %refs_5_.1, s32[64,112]{1,0:T(8,128)} %refs_2_.7, bf16[256,768]{1,0:T(8,128)(2,1)} %refs_7_.1, bf16[8,256,1024]{2,1,0:T(8,128)(2,1)} %get-tuple-element.89.refs_1_.refs_4_, ...), custom_call_target="tpu_custom_call", output_to_operand_aliasing={{}: (8, {})} | custom-call | flops 2000000000 | bytes 8000000 | tf_op jit(solution)/shard_map/tokens_backward/pallas_call | solution.py:1135
  109.2 5.1 %collective-permute-done.9.refs_2_ = f32[256,256]{1,0:T(8,128)S(1)} collective-permute-done((f32[256,256]{1,0:T(8,128)S(1)}, f32[256,256]{1,0:T(8,128)S(1)}, u32[]{:S(2)}, u32[]{:S(2)}) %collective-permute-start.9) | collective-permute-done | bytes 262176 | tf_op jit(solution)/shard_map/ppermute | solution.py:878
  114.3 0.0 copy-done.7
  114.3 0.6 combine.12.refs_1_
  114.9 0.1 collective-permute-start.10
  115.0 0.0 copy-start.8
  115.0 6.5 %layer_output.3.refs_5_ = bf16[64,112,256]{2,1,0:T(8,128)(2,1)} custom-call(s32[304]{0:T(512)} %plan.1.meta_ref.refs_0_, bf16[256]{0:T(256)(128)(2,1)} %refs_1_.13, bf16[256,1024]{1,0:T(8,128)(2,1)} %get-tuple-element.130.refs_2_, bf16[8,1024,1024]{2,1,0:T(8,128)(2,1)} %get-tuple-element.131.refs_3_, bf16[8,256,1024]{2,1,0:T(8,128)(2,1)} %get-tuple-element.132.refs_4_), custom_call_target="tpu_custom_call" | custom-call | flops 2000000000 | bytes 8000000 | tf_op jit(solution)/shard_map/layer_output/pallas_call | solution.py:1135
  121.5 0.5 collective-permute-done.10.refs_2_
  122.0 0.0 copy-done.8
  122.0 0.6 combine.13
  122.6 1.1 collective-permute-start.11
  123.8 1.6 %collective-permute-start.12 = (f32[200,256]{1,0:T(8,128)S(1)}, f32[200,256]{1,0:T(8,128)S(1)}, u32[]{:S(2)}, u32[]{:S(2)}) collective-permute-start(f32[200,256]{1,0:T(8,128)S(1)} %get-tuple-element.135.refs_3_), channel_id=1, source_target_pairs={{0,4},{1,5},{2,6},{3,7},{4,0},{5,1},{6,2},{7,3},{8,12},{9,13},{10,... | collective-permute-start | bytes 614408 | tf_op jit(solution)/shard_map/ppermute | solution.py:878
  125.3 3.8 %layer_output.4.refs_5_ = bf16[64,112,256]{2,1,0:T(8,128)(2,1)} custom-call(s32[304]{0:T(512)} %plan.1.meta_ref.refs_0_, bf16[256]{0:T(256)(128)(2,1)} %refs_1_.13, bf16[256,1024]{1,0:T(8,128)(2,1)} %get-tuple-element.130.refs_2_, bf16[8,1024,1024]{2,1,0:T(8,128)(2,1)} %get-tuple-element.131.refs_3_, ...), custom_call_target="tpu_custom_call", output_to_operand_aliasing={{}: (5, {})} | custom-call | flops 2000000000 | bytes 8000000 | tf_op jit(solution)/shard_map/layer_output/pallas_call | solution.py:1135
  129.2 0.0 collective-permute-done.11.refs_2_
  129.2 0.3 collective-permute-done.12.refs_4_
  129.5 0.0 copy-done.9
  129.5 0.6 combine.14
  130.1 1.7 %collective-permute-start.13 = (f32[400,256]{1,0:T(8,128)S(1)}, f32[400,256]{1,0:T(8,128)S(1)}, u32[]{:S(2)}, u32[]{:S(2)}) collective-permute-start(f32[400,256]{1,0:T(8,128)S(1)} %get-tuple-element.139.refs_1_), channel_id=1, source_target_pairs={{0,4},{1,5},{2,6},{3,7},{4,0},{5,1},{6,2},{7,3},{8,12},{9,13},{10,... | collective-permute-start | bytes 1228808 | tf_op jit(solution)/shard_map/ppermute | solution.py:878
  131.8 0.0 copy-start.13
  131.8 0.8 collective-permute-start.14
  132.6 7.6 %layer_output.5 = bf16[64,112,256]{2,1,0:T(8,128)(2,1)} custom-call(s32[304]{0:T(512)} %plan.1.meta_ref.refs_0_, bf16[256]{0:T(256)(128)(2,1)} %refs_1_.13, bf16[256,1024]{1,0:T(8,128)(2,1)} %get-tuple-element.130.refs_2_, bf16[8,1024,1024]{2,1,0:T(8,128)(2,1)} %get-tuple-element.131.refs_3_, ...), custom_call_target="tpu_custom_call", output_to_operand_aliasing={{}: (5, {})} | custom-call | flops 2000000000 | bytes 8000000 | tf_op jit(solution)/shard_map/layer_output/pallas_call | solution.py:1135
  140.2 0.1 collective-permute-done.13.refs_2_
  140.3 0.2 collective-permute-done.14.refs_4_
  140.6 0.7 combine.15.refs_1_.refs_3_
  141.2 0.1 collective-permute-start.15
  141.3 3.5 %collective-permute-done.15.refs_2_.refs_4_ = f32[1600,256]{1,0:T(8,128)S(1)} collective-permute-done((f32[1600,256]{1,0:T(8,128)S(1)}, f32[1600,256]{1,0:T(8,128)S(1)}, u32[]{:S(2)}, u32[]{:S(2)}) %collective-permute-start.15) | collective-permute-done | bytes 1638432 | tf_op jit(solution)/shard_map/ppermute | solution.py:878
  144.8 0.0 copy-done
  144.8 4.3 %finish.1 = (f32[1024,256]{1,0:T(8,128)}, f32[256,1024]{1,0:T(8,128)}, f32[256,256]{1,0:T(8,128)}, f32[256,768]{1,0:T(8,128)}, f32[256]{0:T(256)}, /*index=5*/f3...) custom-call(s32[304]{0:T(512)S(1)} %copy-done.10, ...), custom_call_target="tpu_custom_call" | custom-call | tf_op jit(solution)/shard_map/finish/pallas_call | solution.py:1186
  (15 shorter events, 0.0 us)
Async XLA Ops:
  47.7 21.4 %collective-permute-start = (f32[1152,256]{1,0:T(8,128)}, f32[1152,256]{1,0:T(8,128)S(1)}, u32[]{:S(2)}, u32[]{:S(2)}) collective-permute-start(f32[1152,256]{1,0:T(8,128)} %get-tuple-element.87), channel_id=1, source_target_pairs={{0,1},{1,0},{2,3},{3,2},{4,5},{5,4},{6,7},{7,6},{8,9},{9,8},{10,11... | collective-permute-start | bytes 3538952 | tf_op jit(solution)/shard_map/ppermute | solution.py:878
  53.1 16.0 %copy-start.2 = (f32[1152,256]{1,0:T(8,128)S(1)}, f32[1152,256]{1,0:T(8,128)}, u32[]{:S(2)}) copy-start(f32[1152,256]{1,0:T(8,128)} %get-tuple-element.86.refs_1_) | copy-start | bytes 3538948
  53.1 16.0 %copy-start.3 = (s32[304]{0:T(512)S(1)}, s32[304]{0:T(512)}, u32[]{:S(2)}) copy-start(s32[304]{0:T(512)} %plan.1.meta_ref.refs_0_) | copy-start | bytes 3652
  67.5 11.6 %collective-permute-start.3 = (f32[448,256]{1,0:T(8,128)}, f32[448,256]{1,0:T(8,128)S(1)}, u32[]{:S(2)}, u32[]{:S(2)}) collective-permute-start(f32[448,256]{1,0:T(8,128)} %get-tuple-element.99), channel_id=1, source_target_pairs={{0,1},{1,0},{2,3},{3,2},{4,5},{5,4},{6,7},{7,6},{8,9},{9,8},{10,11... | collective-permute-start | bytes 1376264 | tf_op jit(solution)/shard_map/ppermute | solution.py:878
  69.7 10.2 %collective-permute-start.1 = (f32[288,256]{1,0:T(8,128)S(1)}, f32[288,256]{1,0:T(8,128)S(1)}, u32[]{:S(2)}, u32[]{:S(2)}) collective-permute-start(f32[288,256]{1,0:T(8,128)S(1)} %get-tuple-element.97), channel_id=1, source_target_pairs={{0,4},{1,5},{2,6},{3,7},{4,0},{5,1},{6,2},{7,3},{8,12},{9,13},{10,... | collective-permute-start | bytes 884744 | tf_op jit(solution)/shard_map/ppermute | solution.py:878
  72.7 8.7 %collective-permute-start.2 = (f32[288,256]{1,0:T(8,128)S(1)}, f32[288,256]{1,0:T(8,128)S(1)}, u32[]{:S(2)}, u32[]{:S(2)}) collective-permute-start(f32[288,256]{1,0:T(8,128)S(1)} %get-tuple-element.98), channel_id=1, source_target_pairs={{0,2},{1,3},{2,0},{3,1},{4,6},{5,7},{6,4},{7,5},{8,10},{9,11},{10,... | collective-permute-start | bytes 884744 | tf_op jit(solution)/shard_map/ppermute | solution.py:878
  73.7 7.7 %copy-start.4 = (s32[304]{0:T(512)S(1)}, s32[304]{0:T(512)}, u32[]{:S(2)}) copy-start(s32[304]{0:T(512)} %plan.1.meta_ref.refs_0_) | copy-start | bytes 3652
  73.7 7.7 %copy-start.11 = (f32[448,256]{1,0:T(8,128)S(1)}, f32[448,256]{1,0:T(8,128)}, u32[]{:S(2)}) copy-start(f32[448,256]{1,0:T(8,128)} %get-tuple-element.94.refs_5_) | copy-start | bytes 1376260
  82.1 7.4 %collective-permute-start.4 = (f32[256,256]{1,0:T(8,128)S(1)}, f32[256,256]{1,0:T(8,128)S(1)}, u32[]{:S(2)}, u32[]{:S(2)}) collective-permute-start(f32[256,256]{1,0:T(8,128)S(1)} %get-tuple-element.109), channel_id=1, source_target_pairs={{0,2},{1,3},{2,0},{3,1},{4,6},{5,7},{6,4},{7,5},{8,10},{9,11},{10,... | collective-permute-start | bytes 786440 | tf_op jit(solution)/shard_map/ppermute | solution.py:878
  83.1 6.8 %copy-start.5 = (s32[304]{0:T(512)S(1)}, s32[304]{0:T(512)}, u32[]{:S(2)}) copy-start(s32[304]{0:T(512)} %plan.1.meta_ref.refs_0_) | copy-start | bytes 3652
  83.1 6.8 %collective-permute-start.5 = (f32[256,256]{1,0:T(8,128)S(1)}, f32[256,256]{1,0:T(8,128)S(1)}, u32[]{:S(2)}, u32[]{:S(2)}) collective-permute-start(f32[256,256]{1,0:T(8,128)S(1)} %get-tuple-element.110), channel_id=1, source_target_pairs={{0,4},{1,5},{2,6},{3,7},{4,0},{5,1},{6,2},{7,3},{8,12},{9,13},{10,... | collective-permute-start | bytes 786440 | tf_op jit(solution)/shard_map/ppermute | solution.py:878
  90.5 11.3 %collective-permute-start.7 = (f32[56,256]{1,0:T(8,128)S(1)}, f32[56,256]{1,0:T(8,128)S(1)}, u32[]{:S(2)}, u32[]{:S(2)}) collective-permute-start(f32[56,256]{1,0:T(8,128)S(1)} %get-tuple-element.119), channel_id=1, source_target_pairs={{0,2},{1,3},{2,0},{3,1},{4,6},{5,7},{6,4},{7,5},{8,10},{9,11},{10,... | collective-permute-start | bytes 172040 | tf_op jit(solution)/shard_map/ppermute | solution.py:878
  91.7 10.2 %collective-permute-start.8 = (f32[56,256]{1,0:T(8,128)S(1)}, f32[56,256]{1,0:T(8,128)S(1)}, u32[]{:S(2)}, u32[]{:S(2)}) collective-permute-start(f32[56,256]{1,0:T(8,128)S(1)} %get-tuple-element.120), channel_id=1, source_target_pairs={{0,4},{1,5},{2,6},{3,7},{4,0},{5,1},{6,2},{7,3},{8,12},{9,13},{10,... | collective-permute-start | bytes 172040 | tf_op jit(solution)/shard_map/ppermute | solution.py:878
  92.4 9.5 %copy-start.6 = (s32[304]{0:T(512)S(1)}, s32[304]{0:T(512)}, u32[]{:S(2)}) copy-start(s32[304]{0:T(512)} %plan.1.meta_ref.refs_0_) | copy-start | bytes 3652
  92.4 9.5 %collective-permute-start.6 = (f32[144,256]{1,0:T(8,128)S(1)}, f32[144,256]{1,0:T(8,128)S(1)}, u32[]{:S(2)}, u32[]{:S(2)}) collective-permute-start(f32[144,256]{1,0:T(8,128)S(1)} %get-tuple-element.118), channel_id=1, source_target_pairs={{0,8},{1,9},{2,10},{3,11},{4,12},{5,13},{6,14},{7,15},{8,0},{9,1},... | collective-permute-start | bytes 442376 | tf_op jit(solution)/shard_map/ppermute | solution.py:878
  102.5 11.8 %copy-start.7 = (s32[304]{0:T(512)S(1)}, s32[304]{0:T(512)}, u32[]{:S(2)}) copy-start(s32[304]{0:T(512)} %plan.1.meta_ref.refs_0_) | copy-start | bytes 3652
  102.5 11.8 %collective-permute-start.9 = (f32[256,256]{1,0:T(8,128)S(1)}, f32[256,256]{1,0:T(8,128)S(1)}, u32[]{:S(2)}, u32[]{:S(2)}) collective-permute-start(f32[256,256]{1,0:T(8,128)S(1)} %combine.11.refs_1_), channel_id=1, source_target_pairs={{0,16},{1,17},{2,18},{3,19},{4,20},{5,21},{6,22},{7,23},{8,24},{9,... | collective-permute-start | bytes 786440 | tf_op jit(solution)/shard_map/ppermute | solution.py:878
  114.9 7.1 %collective-permute-start.10 = (f32[256,256]{1,0:T(8,128)S(1)}, f32[256,256]{1,0:T(8,128)S(1)}, u32[]{:S(2)}, u32[]{:S(2)}) collective-permute-start(f32[256,256]{1,0:T(8,128)S(1)} %combine.12.refs_1_), channel_id=1, source_target_pairs={{0,8},{1,9},{2,10},{3,11},{4,12},{5,13},{6,14},{7,15},{8,0},{9,1},... | collective-permute-start | bytes 786440 | tf_op jit(solution)/shard_map/ppermute | solution.py:878
  115.0 7.1 %copy-start.8 = (s32[304]{0:T(512)S(1)}, s32[304]{0:T(512)}, u32[]{:S(2)}) copy-start(s32[304]{0:T(512)} %plan.1.meta_ref.refs_0_) | copy-start | bytes 3652
  122.6 6.6 %collective-permute-start.11 = (f32[200,256]{1,0:T(8,128)S(1)}, f32[200,256]{1,0:T(8,128)S(1)}, u32[]{:S(2)}, u32[]{:S(2)}) collective-permute-start(f32[200,256]{1,0:T(8,128)S(1)} %get-tuple-element.134.refs_1_), channel_id=1, source_target_pairs={{0,2},{1,3},{2,0},{3,1},{4,6},{5,7},{6,4},{7,5},{8,10},{9,11},{10,... | collective-permute-start | bytes 614408 | tf_op jit(solution)/shard_map/ppermute | solution.py:878
  123.8 5.8 %copy-start.9 = (s32[304]{0:T(512)S(1)}, s32[304]{0:T(512)}, u32[]{:S(2)}) copy-start(s32[304]{0:T(512)} %plan.1.meta_ref.refs_0_) | copy-start | bytes 3652
  123.8 5.8 %collective-permute-start.12 = (f32[200,256]{1,0:T(8,128)S(1)}, f32[200,256]{1,0:T(8,128)S(1)}, u32[]{:S(2)}, u32[]{:S(2)}) collective-permute-start(f32[200,256]{1,0:T(8,128)S(1)} %get-tuple-element.135.refs_3_), channel_id=1, source_target_pairs={{0,4},{1,5},{2,6},{3,7},{4,0},{5,1},{6,2},{7,3},{8,12},{9,13},{10,... | collective-permute-start | bytes 614408 | tf_op jit(solution)/shard_map/ppermute | solution.py:878
  130.1 10.2 %collective-permute-start.13 = (f32[400,256]{1,0:T(8,128)S(1)}, f32[400,256]{1,0:T(8,128)S(1)}, u32[]{:S(2)}, u32[]{:S(2)}) collective-permute-start(f32[400,256]{1,0:T(8,128)S(1)} %get-tuple-element.139.refs_1_), channel_id=1, source_target_pairs={{0,4},{1,5},{2,6},{3,7},{4,0},{5,1},{6,2},{7,3},{8,12},{9,13},{10,... | collective-permute-start | bytes 1228808 | tf_op jit(solution)/shard_map/ppermute | solution.py:878
  131.8 8.8 %copy-start.10 = (s32[304]{0:T(512)S(1)}, s32[304]{0:T(512)}, u32[]{:S(2)}) copy-start(s32[304]{0:T(512)} %plan.1.meta_ref.refs_0_) | copy-start | bytes 3652
  131.8 13.0 %copy-start = (bf16[256,768]{1,0:T(8,128)(2,1)S(1)}, bf16[256,768]{1,0:T(8,128)(2,1)}, u32[]{:S(2)}) copy-start(bf16[256,768]{1,0:T(8,128)(2,1)} %refs_7_.1) | copy-start | bytes 1179652
  131.8 13.0 %copy-start.1 = (bf16[256,1024]{1,0:T(8,128)(2,1)S(1)}, bf16[256,1024]{1,0:T(8,128)(2,1)}, u32[]{:S(2)}) copy-start(bf16[256,1024]{1,0:T(8,128)(2,1)} %refs_8_.1) | copy-start | bytes 1572868
  131.8 13.0 %copy-start.12 = (bf16[256]{0:T(256)(128)(2,1)S(1)}, bf16[256]{0:T(256)(128)(2,1)}, u32[]{:S(2)}) copy-start(bf16[256]{0:T(256)(128)(2,1)} %refs_5_.1) | copy-start | bytes 1540
  131.8 13.0 %copy-start.13 = (bf16[256]{0:T(256)(128)(2,1)S(1)}, bf16[256]{0:T(256)(128)(2,1)}, u32[]{:S(2)}) copy-start(bf16[256]{0:T(256)(128)(2,1)} %refs_6_.1) | copy-start | bytes 1540
  131.8 8.7 %collective-permute-start.14 = (f32[400,256]{1,0:T(8,128)S(1)}, f32[400,256]{1,0:T(8,128)S(1)}, u32[]{:S(2)}, u32[]{:S(2)}) collective-permute-start(f32[400,256]{1,0:T(8,128)S(1)} %get-tuple-element.140.refs_3_), channel_id=1, source_target_pairs={{0,2},{1,3},{2,0},{3,1},{4,6},{5,7},{6,4},{7,5},{8,10},{9,11},{10,... | collective-permute-start | bytes 1228808 | tf_op jit(solution)/shard_map/ppermute | solution.py:878
  141.2 3.6 %collective-permute-start.15 = (f32[1600,256]{1,0:T(8,128)S(1)}, f32[1600,256]{1,0:T(8,128)S(1)}, u32[]{:S(2)}, u32[]{:S(2)}) collective-permute-start(f32[1600,256]{1,0:T(8,128)S(1)} %combine.15.refs_1_.refs_3_), channel_id=1, source_target_pairs={{0,1},{1,0},{2,3},{3,2},{4,5},{5,4},{6,7},{7,6},{8,9},{9,8},{10,11... | collective-permute-start | bytes 4915208 | tf_op jit(solution)/shard_map/ppermute | solution.py:878

commit v3 on v2

--- a/solution.py
+++ b/solution.py
@@ -230,20 +230,29 @@
     wup_ref,
     wdn_ref,
     wdnt_s,
-    nhat1_ref,
-    rstd1_ref,
-    qkv_ref,
-    prob_ref,
-    gatt_ref,
-    gmid_ref,
-    act_ref,
-    mid_ref,
+    nhat1_hbm,
+    rstd1_hbm,
+    qkv_hbm,
+    prob_hbm,
+    gatt_hbm,
+    gmid_hbm,
+    act_hbm,
+    mid_hbm,
     keep_ref,
     send_ref,
     dvec_ref,
     tok_s,
     og_s,
     in_sem,
+    nhat1_b,
+    rstd1_b,
+    qkv_b,
+    prob_b,
+    gatt_b,
+    gmid_b,
+    act_b,
+    mid_b,
+    out_sem,
     idx_s,
     vec_s,
     col_s,
@@ -266,7 +275,6 @@
     acc_s,
     bacc_s,
 ):
-    step = pl.program_id(0)
     traj, seq, d = tok_ref.shape
     slots = og_ref.shape[1]
     ff = wup_ref.shape[1]
@@ -275,52 +283,62 @@
     meta = Meta(meta_ref, traj)
     steps = lax.shift_right_logical(meta.tiles() + 1, 1)
 
-    def arrivals(i, act):
-        slot = jnp.bitwise_and(i, 1)
+    def arrivals(i, slot, act):
         for b in range(BINS_A):
             for part, t in enumerate(meta.bin(i * BINS_A + b)[0:2]):
                 sems = in_sem.at[slot, b, part]
                 act(pltpu.make_async_copy(tok_ref.at[t], tok_s.at[slot, b, pl.ds(part * seq, seq)], sems.at[0]))
                 act(pltpu.make_async_copy(og_ref.at[t], og_s.at[slot, b, pl.ds(part * BIN, slots)], sems.at[1]))
 
-    @pl.when(step == 0)
-    def _():
-        for part in range(2):
-            og_s[:, :, part * BIN + slots : (part + 1) * BIN, :] = jnp.zeros((2, BINS_A, BIN - slots, d), BF16)
-        arrivals(0, lambda c: c.start())
-        idx_s[...] = jnp.zeros_like(idx_s)
-        idx_s[:, 0:slots] = idx_ref[...]
-        vec_s[...] = jnp.zeros_like(vec_s)
-        rows = [(0, g1_ref), (1, c1_ref), (2, bq_ref), (4, bv_ref), (5, bo_ref), (6, g2_ref), (7, c2_ref)]
-        for j, ref in rows:
-            vec_s[j : j + 1, :] = ref[...].astype(F32).reshape(1, d)
-        for j in range(ff // d):
-            vec_s[8 + j : 9 + j, :] = bup_ref[j * d : (j + 1) * d].astype(F32).reshape(1, d)
-        vec_s[2:3, :] = vec_s[2:3, :] * scale
-        cols = vec_s[...].T
-        for j in range(12):
-            col_s[j * d : (j + 1) * d, :] = jnp.broadcast_to(cols[:, j : j + 1], (d, BIN))
-        wqkvt_s[...] = wqkv_ref[...].T
-        wqkvt_s[0:d, :] = (wqkvt_s[0:d, :].astype(F32) * scale).astype(BF16)
-        wot_s[...] = wo_ref[...].T
-        wupt_s[...] = wup_ref[...].T
-        wdnt_s[...] = wdn_ref[...].T
-        bd_s[...] = jnp.zeros_like(bd_s)
-        bacc_s[...] = jnp.zeros_like(bacc_s)
-        acc_s[...] = jnp.zeros_like(acc_s)
+    saved = (
+        (nhat1_b, nhat1_hbm), (rstd1_b, rstd1_hbm), (qkv_b, qkv_hbm), (prob_b, prob_hbm),
+        (act_b, act_hbm), (mid_b, mid_hbm), (gatt_b, gatt_hbm), (gmid_b, gmid_hbm),
+    )
+
+    def departures(i, which, act):
+        slot = jnp.bitwise_and(i, 1)
+        for k in which:
+            place, ref = saved[k]
+            act(pltpu.make_async_copy(place.at[slot], ref.at[i], out_sem.at[slot, k]))
+
+    for part in range(2):
+        og_s[:, :, part * BIN + slots : (part + 1) * BIN, :] = jnp.zeros((2, BINS_A, BIN - slots, d), BF16)
+    arrivals(0, 0, lambda c: c.start())
+    idx_s[...] = jnp.zeros_like(idx_s)
+    idx_s[:, 0:slots] = idx_ref[...]
+    vec_s[...] = jnp.zeros_like(vec_s)
+    rows = [(0, g1_ref), (1, c1_ref), (2, bq_ref), (4, bv_ref), (5, bo_ref), (6, g2_ref), (7, c2_ref)]
+    for j, ref in rows:
+        vec_s[j : j + 1, :] = ref[...].astype(F32).reshape(1, d)
+    for j in range(ff // d):
+        vec_s[8 + j : 9 + j, :] = bup_ref[j * d : (j + 1) * d].astype(F32).reshape(1, d)
+    vec_s[2:3, :] = vec_s[2:3, :] * scale
+    cols = vec_s[...].T
+    for j in range(12):
+        col_s[j * d : (j + 1) * d, :] = jnp.broadcast_to(cols[:, j : j + 1], (d, BIN))
+    wqkvt_s[...] = wqkv_ref[...].T
+    wqkvt_s[0:d, :] = (wqkvt_s[0:d, :].astype(F32) * scale).astype(BF16)
+    wot_s[...] = wo_ref[...].T
+    wupt_s[...] = wup_ref[...].T
+    wdnt_s[...] = wdn_ref[...].T
+    bd_s[...] = jnp.zeros_like(bd_s)
+    bacc_s[...] = jnp.zeros_like(bacc_s)
+    acc_s[...] = jnp.zeros_like(acc_s)
 
     def col(j, n=1):
         return col_s[j * d : (j + n) * d, :]
 
-    @pl.when(step < steps)
-    def _():
+    def work_on(step, carry):
         slot = jnp.bitwise_and(step, 1)
-        arrivals(step, lambda c: c.wait())
-
-        @pl.when(step + 1 < steps)
+        arrivals(step, slot, lambda c: c.wait())
+
+        @pl.when(step >= 2)
         def _():
-            arrivals(step + 1, lambda c: c.start())
-
+            departures(step - 2, range(8), lambda c: c.wait())
+
+        nhat1_ref, rstd1_ref, qkv_ref, prob_ref, act_ref, mid_ref, gatt_ref, gmid_ref = (
+            place.at[pl.ds(slot, 1)] for place, _ in saved
+        )
         metas = [meta.bin(step * BINS_A + b) for b in range(BINS_A)]
         rstds = {}
 
@@ -378,19 +396,19 @@
 
         def up(t):
             lanes = pair_lanes(t)
-            u_s[:, lanes] = mm(wupt_s[...], sec_s[:, lanes])
-            ga_s[:, lanes] = mm(wdn_ref[...], gm_s[:, lanes])
+            u_s[:, lanes] = (mm(wupt_s[...], sec_s[:, lanes]) + two(col_s[8 * d : 8 * d + ff, :])).astype(BF16)
+            ga_s[:, lanes] = mm(wdn_ref[...], gm_s[:, lanes]).astype(BF16)
 
         def gelu(t, rows):
             lanes = pair_lanes(t)
-            u = u_s[rows, lanes] + two(col_s[8 * d + rows.start : 8 * d + rows.stop, :])
-            q = u * u * GELU_B + GELU_A
-            sg = 0.5 * jnp.tanh(u * q) + 0.5
+            u = u_s[rows, lanes]
+            u2 = u * u
+            sg = 0.5 * jnp.tanh(u * (u2 * GELU_B + GELU_A)) + 0.5
             act = u * sg
-            gp = (act * (1.0 - sg) * (6.0 * q - 4.0 * GELU_A) + sg) * ga_s[rows, lanes]
-            act_ref[0, rows, lanes] = act.astype(BF16)
-            gp_s[rows, lanes] = gp.astype(BF16)
-            bacc_s[d + rows.start : d + rows.stop, :] += gp[:, 0:BIN] + gp[:, BIN:PAIR]
+            gp = (act * (1.0 - sg) * (u2 * (6.0 * GELU_B) + 2.0 * GELU_A) + sg) * ga_s[rows, lanes]
+            act_ref[0, rows, lanes] = act
+            gp_s[rows, lanes] = gp
+            bacc_s[d + rows.start : d + rows.stop, :] += (gp[:, 0:BIN] + gp[:, BIN:PAIR]).astype(F32)
 
         def grad_second(t):
             lanes = pair_lanes(t)
@@ -415,7 +433,7 @@
             gatt_ref[0, :, lanes] = mm(wo_ref[...], gmid_ref[0, :, lanes]).astype(BF16)
 
         def work(count):
-            bins, tiles, chunk, lanes = range(count), range(count // 2), 32, slice(0, count * BIN)
+            bins, tiles, chunk, lanes = range(count), range(count // 2), 64, slice(0, count * BIN)
             pairs = [[(b, p) for b in (2 * t, 2 * t + 1) for p in range(HEADS // 2)] for t in tiles]
             stages = dict(
                 cotangent=lambda t: [cotangent(b) for b in (2 * t, 2 * t + 1)],
@@ -430,12 +448,14 @@
                 gelu=lambda t: [gelu(t, slice(j, j + chunk)) for j in range(0, ff, chunk)],
                 grad_second=grad_second,
             )
+            arrivals(jnp.minimum(step + 1, steps - 1), 1 - slot, lambda c: c.start())
             for b in bins:
                 gather(b)
             for when in range(len(tiles) + len(stages) - 1):
                 for n, stage in enumerate(stages.values()):
                     if 0 <= when - n < len(tiles):
                         stage(when - n)
+            departures(step, range(6), lambda c: c.start())
             acc_s[0:ff, :] += mm(act_ref[0, :, lanes], gm_s[:, lanes], NT)
             for b in bins[: count // 2]:
                 second_norm_back(b)
@@ -456,25 +476,41 @@
         def _():
             work(BINS)
 
-        @pl.when(step == steps - 1)
-        def _():
-            dvec_ref[...] = jnp.zeros_like(dvec_ref)
-            keep_half(meta, acc_s, keep_ref, send_ref)
-            for j in range(7):
-                dvec_ref[j : j + 1, :] = lanes_into_rows(bacc_s[j * d : (j + 1) * d, :])
+        departures(step, range(6, 8), lambda c: c.start())
+        return carry
+
+    lax.fori_loop(0, steps, work_on, 0)
+    keep_half(meta, acc_s, keep_ref, send_ref)
+    for j in range(7):
+        dvec_ref[j : j + 1, :] = lanes_into_rows(bacc_s[j * d : (j + 1) * d, :])
+    dvec_ref[7:8, :] = jnp.zeros((1, d), F32)
+    arrivals(steps - 1, jnp.bitwise_and(steps, 1), lambda c: c.wait())
+
+    @pl.when(steps >= 2)
+    def _():
+        departures(steps - 2, range(8), lambda c: c.wait())
+
+    departures(steps - 1, range(8), lambda c: c.wait())
 
 
 def attention_kernel(
     traj,
     meta_ref,
-    nhat1_ref,
-    qkv_ref,
-    prob_ref,
-    gatt_ref,
+    nhat1_hbm,
+    qkv_hbm,
+    prob_hbm,
+    gatt_hbm,
     dvec_ref,
-    gq_ref,
+    gq_hbm,
     keep_ref,
     send_ref,
+    nhat1_s,
+    qkv_s,
+    prob_s,
+    gatt_s,
+    gq_s,
+    in_sem,
+    out_sem,
     bd_s,
     bdq_s,
     dp_s,
@@ -482,20 +518,55 @@
     bacc_s,
     acc_s,
 ):
-    step = pl.program_id(0)
-    d = nhat1_ref.shape[1]
+    d = nhat1_hbm.shape[1]
     hs = d // HEADS
     scale = hs**-0.5
     meta = Meta(meta_ref, traj)
-
-    @pl.when(step == 0)
-    def _():
-        bd_s[...] = jnp.zeros_like(bd_s)
-        bdq_s[...] = jnp.zeros_like(bdq_s)
-        bacc_s[...] = jnp.zeros_like(bacc_s)
-        acc_s[...] = jnp.zeros_like(acc_s)
-
-    def work(count):
+    steps = lax.shift_right_logical(meta.tiles() + 1, 1)
+
+    def come(i, act):
+        slot = jnp.bitwise_and(i, 1)
+        for k, (ref, place) in enumerate(
+            ((gatt_hbm, gatt_s), (qkv_hbm, qkv_s), (prob_hbm, prob_s), (nhat1_hbm, nhat1_s))
+        ):
+            act(pltpu.make_async_copy(ref.at[i], place.at[slot], in_sem.at[slot, k]))
+
+    def leave(i, act):
+        slot = jnp.bitwise_and(i, 1)
+        act(pltpu.make_async_copy(gq_s.at[slot], gq_hbm.at[i], out_sem.at[slot]))
+
+    come(0, lambda c: c.start())
+    bd_s[...] = jnp.zeros_like(bd_s)
+    bdq_s[...] = jnp.zeros_like(bdq_s)
+    bacc_s[...] = jnp.zeros_like(bacc_s)
+    acc_s[...] = jnp.zeros_like(acc_s)
+
+    def step(i, carry):
+        slot = jnp.bitwise_and(i, 1)
+        come(i, lambda c: c.wait())
+
+        @pl.when(i + 1 < steps)
+        def _():
+            come(i + 1, lambda c: c.start())
+
+        @pl.when(i >= 2)
+        def _():
+            leave(i - 2, lambda c: c.wait())
+
+        refs = [ref.at[pl.ds(slot, 1)] for ref in (nhat1_s, qkv_s, prob_s, gatt_s, gq_s)]
+
+        @pl.when(2 * i + 1 < meta.tiles())
+        def _():
+            work(BINS_A, *refs)
+
+        @pl.when(2 * i + 1 == meta.tiles())
+        def _():
+            work(BINS, *refs)
+
+        leave(i, lambda c: c.start())
+        return carry
+
+    def work(count, nhat1_ref, qkv_ref, prob_ref, gatt_ref, gq_ref):
         pairs = [(b, p * 2 * hs, b * (HEADS // 2) + p, p) for b in range(count) for p in range(HEADS // 2)]
         for b, f0, at, _ in pairs:
             lanes = bin_lanes(b)
@@ -524,20 +595,17 @@
         lanes = slice(0, count * BIN)
         acc_s[0 : 3 * d, :] += mm(gq_ref[0, :, lanes], nhat1_ref[0, :, lanes], NT)
 
-    @pl.when(2 * step + 1 < meta.tiles())
+    lax.fori_loop(0, steps, step, 0)
+    for j in range(3):
+        acc_s[3 * d + j : 3 * d + j + 1, :] = lanes_into_rows(bacc_s[j * d : (j + 1) * d, :])
+    acc_s[3 * d + 3 : 3 * d + 11, :] = dvec_ref[...]
+    keep_half(meta, acc_s, keep_ref, send_ref)
+
+    @pl.when(steps >= 2)
     def _():
-        work(BINS_A)
-
-    @pl.when(2 * step + 1 == meta.tiles())
-    def _():
-        work(BINS)
-
-    @pl.when(step == pl.num_programs(0) - 1)
-    def _():
-        for j in range(3):
-            acc_s[3 * d + j : 3 * d + j + 1, :] = lanes_into_rows(bacc_s[j * d : (j + 1) * d, :])
-        acc_s[3 * d + 3 : 3 * d + 11, :] = dvec_ref[...]
-        keep_half(meta, acc_s, keep_ref, send_ref)
+        leave(steps - 2, lambda c: c.wait())
+
+    leave(steps - 1, lambda c: c.wait())
 
 
 def token_kernel(share, meta_ref, g1_ref, idx_ref, wqkv_ref, nhat1_ref, rstd1_ref, gq_ref, gmid_ref, *refs):
@@ -722,46 +790,40 @@
 
 
 def bucket_sum(bits, keep, send, half, halve_z):
-    q, e, f = half // 4, half // 8, half // 16
-    _, (got,) = yield Step([send], [], [], {0: CORE})
-    (k0, k1, _, _), (g0, g1) = yield Step(
+    h, e, f = half // 4, half // 8, half // 16
+    _, (got,) = yield Step([send], [], [], {0: (CORE,)})
+
+    def part(x, y):
+        return (0 if x else 2 * h) + (0 if y else h), ((X, 2 * h if x else -2 * h), (Y, h if y else -h))
+
+    (k, _, _, _), got = yield Step(
         [keep, got],
-        [q, q, q, q],
+        [h] * 4,
         [
-            (2 * q, [(0, row_at()), (1, row_at())], [(0, row_at(), mine(X, q), q), (2, row_at(), other(X, q), q)]),
-            (
-                2 * q,
-                [(0, row_at(2 * q)), (1, row_at(2 * q))],
-                [(1, row_at(), mine(Y, q), q), (3, row_at(), other(Y, q), q)],
-            ),
+            (h, [(0, part(x, y)), (1, part(x, y))], [(out, row_at(), 0, h)])
+            for out, (x, y) in enumerate(((True, True), (False, True), (True, False), (False, False)))
         ],
-        {2: X, 3: Y},
+        {1: (X,), 2: (Y,), 3: (X, Y)},
     )
-    (a0, a1, _, _), (g0, g1) = yield Step(
-        [k0, k1, g0, g1],
-        [e, e, e, e],
-        [
-            (q, [(0, row_at()), (2, row_at())], [(0, row_at(), mine(Y, e), e), (2, row_at(), other(Y, e), e)]),
-            (q, [(1, row_at()), (3, row_at())], [(1, row_at(), mine(X, e), e), (3, row_at(), other(X, e), e)]),
-        ],
-        {2: Y, 3: X},
-    )
+    four = [k, *got]
     if halve_z:
         (z, _), (got,) = yield Step(
-            [a0, a1, g0, g1],
+            four,
             [e, e],
             [
                 (
                     e,
-                    [(c, row_at()), (2 + c, row_at())],
+                    [(n, row_at(c * e)) for n in range(4)],
                     [(0, row_at(c * f), mine(Z, f), f), (1, row_at(c * f), other(Z, f), f)],
                 )
                 for c in range(2)
             ],
-            {1: Z},
+            {1: (Z,)},
         )
         for bit in [*range(Z + 1, bits), Z]:
-            (z,), (got,) = yield Step([z, got], [e], [(e, [(0, row_at()), (1, row_at())], [(0, row_at(), 0, e)])], {0: bit})
+            (z,), (got,) = yield Step(
+                [z, got], [e], [(e, [(0, row_at()), (1, row_at())], [(0, row_at(), 0, e)])], {0: (bit,)}
+            )
         (e0, e1), (g0, g1) = yield Step(
             [z, got],
             [e, e],
@@ -770,46 +832,43 @@
                 for ref, side in enumerate((mine, other))
                 for c in range(2)
             ],
-            {0: Y, 1: X},
+            {0: (Y,), 1: (X,)},
         )
     else:
         (z,), (got,) = yield Step(
-            [a0, a1, g0, g1],
-            [2 * e],
-            [(e, [(c, row_at()), (2 + c, row_at())], [(0, row_at(c * e), 0, e)]) for c in range(2)],
-            {0: bits - 1},
+            four, [h], [(h, [(n, row_at()) for n in range(4)], [(0, row_at(), 0, h)])], {0: (bits - 1,)}
         )
         for bit in range(bits - 2, Z - 1, -1):
             (z,), (got,) = yield Step(
-                [z, got], [2 * e], [(2 * e, [(0, row_at()), (1, row_at())], [(0, row_at(), 0, 2 * e)])], {0: bit}
+                [z, got], [h], [(h, [(0, row_at()), (1, row_at())], [(0, row_at(), 0, h)])], {0: (bit,)}
             )
         (e0, e1), (g0, g1) = yield Step(
             [z, got],
             [e, e],
-            [(2 * e, [(0, row_at()), (1, row_at())], [(0, row_at(), 0, e), (1, row_at(), e, e)])],
-            {0: Y, 1: X},
+            [(h, [(0, row_at()), (1, row_at())], [(0, row_at(), 0, e), (1, row_at(), e, e)])],
+            {0: (Y,), 1: (X,)},
         )
     (f0, f1), (g0, g1) = yield Step(
         [e0, e1, g0, g1],
-        [q, q],
+        [h, h],
         [
             (e, [(0, row_at())], [(0, mine(Y, e), 0, e)]),
             (e, [(2, row_at())], [(0, other(Y, e), 0, e)]),
             (e, [(1, row_at())], [(1, mine(X, e), 0, e)]),
             (e, [(3, row_at())], [(1, other(X, e), 0, e)]),
         ],
-        {0: X, 1: Y},
+        {0: (X,), 1: (Y,)},
     )
     (near,), (far,) = yield Step(
         [f0, f1, g0, g1],
         [half],
         [
-            (q, [(0, row_at())], [(0, mine(X, q), 0, q)]),
-            (q, [(2, row_at())], [(0, other(X, q), 0, q)]),
-            (q, [(1, row_at())], [(0, mine(Y, q, 2 * q), 0, q)]),
-            (q, [(3, row_at())], [(0, other(Y, q, 2 * q), 0, q)]),
+            (h, [(0, row_at())], [(0, mine(X, 2 * h, y * h), y * e, e) for y in range(2)]),
+            (h, [(2, row_at())], [(0, other(X, 2 * h, y * h), y * e, e) for y in range(2)]),
+            (h, [(1, row_at())], [(0, mine(Y, h, x * 2 * h + e), x * e, e) for x in range(2)]),
+            (h, [(3, row_at())], [(0, other(Y, h, x * 2 * h + e), x * e, e) for x in range(2)]),
         ],
-        {0: CORE},
+        {0: (CORE,)},
     )
     return near, far
 
@@ -873,8 +932,8 @@
         self.sent = [self.arrays[k] for k in to_send.values()]
         received = {}
         for key, k in to_send.items():
-            bit = key[0] if isinstance(key, tuple) else key
-            perm = [(r, r ^ (1 << bit)) for r in range(self.ranks)]
+            mask = sum(1 << bit for bit in (key[0] if isinstance(key[0], tuple) else key))
+            perm = [(r, r ^ mask) for r in range(self.ranks)]
             received[key] = self.view(lax.ppermute(self.arrays[k], AXES, perm))[0]
         self.arrived = list(received.values())
         for name, (steps, step) in list(self.running.items()):
@@ -965,34 +1024,14 @@
         copy.wait()
 
 
-def whole(shape):
-    zeros = (0,) * len(shape)
-    return pl.BlockSpec(shape, lambda i, *_: zeros, pipeline_mode=pl.Buffered(1))
-
-
-def per_step(shape, at):
-    rest = (0,) * len(shape)
-    return pl.BlockSpec((1,) + shape, lambda i, meta: (at(i, meta),) + rest)
-
-
 def doubled(shape):
     if len(shape) == 3:
         return (2 * shape[0],) + shape[1:]
     return shape[:-1] + (2 * shape[-1],)
 
 
-SHARES_C = shares(0, 5, 8, 10, 16)
+SHARES_C = shares(0, 8, 11, 16)
 SHARES_D = shares(0, 6, 9, 16)
-
-
-def strided(first, pieces, tiles_at, halved=0):
-    def at(i, meta):
-        bits = pieces.bit_length() - 1
-        count = lax.shift_right_logical(meta[tiles_at] + halved, halved)
-        last = first + lax.shift_left(lax.shift_right_logical(count - 1 - first, bits), bits)
-        return jnp.minimum(i * pieces + first, last)
-
-    return at
 
 
 def body(
@@ -1042,55 +1081,50 @@
         shape, kind = shapes[name]
         return jax.ShapeDtypeStruct((steps_a,) + doubled(shape), kind)
 
-    at_a = strided(0, 1, tiles_at, 1)
-
-    def params(mib):
-        return pltpu.CompilerParams(dimension_semantics=("arbitrary",), vmem_limit_bytes=mib * MIB)
+    smem, vmem = (pl.BlockSpec(memory_space=m) for m in (pltpu.SMEM, pltpu.VMEM))
+
+    def step_places(*names):
+        return [pltpu.VMEM((2,) + doubled(shapes[n][0]), shapes[n][1]) for n in names]
 
     late_shape = (2 * ff + d, d)
     vectors = [ln1_gain, ln1_bias, query_bias, value_bias, out_bias, ln2_gain, ln2_bias, up_bias]
     weights = [qkv_weight, out_weight, up_weight, down_weight]
     down_weight_t, nhat, rstd, qkv, prob, gatt, gmid, act, mid, late_keep, late_send, late_vectors = pl.pallas_call(
         late_kernel,
-        grid_spec=pltpu.PrefetchScalarGridSpec(
-            num_scalar_prefetch=1,
-            grid=(steps_a,),
-            in_specs=[whole((traj, slots)), HBM, HBM] + [whole(v.shape) for v in vectors + weights],
-            out_specs=[whole((d, ff))]
-            + [per_step(doubled(shapes[n][0]), at_a) for n in shapes]
-            + [whole((late_shape[0] // 2, d))] * 2
-            + [whole((8, d))],
-            scratch_shapes=[
-                pltpu.VMEM((2, BINS_A, 2 * seq, d), BF16),
-                pltpu.VMEM((2, BINS_A, 2 * BIN, d), BF16),
-                pltpu.SemaphoreType.DMA((2, BINS_A, 2, 2)),
-                pltpu.VMEM((traj, BIN), jnp.int32),
-                pltpu.VMEM((16, d), F32),
-                pltpu.VMEM((12 * d, BIN), F32),
-                pltpu.VMEM((3 * d, d), BF16),
-                pltpu.VMEM((d, d), BF16),
-                pltpu.VMEM((ff, d), BF16),
-                pltpu.VMEM((d, TILE_A), F32),
-                pltpu.VMEM((d, TILE_A), BF16),
-                pltpu.VMEM((BINS_A * HEADS // 2, 2 * hs, PAIR), BF16),
-                pltpu.VMEM((BINS_A * HEADS // 2, BIN, PAIR), F32),
-                pltpu.VMEM((d, TILE_A), BF16),
-                pltpu.VMEM((d, TILE_A), F32),
-                pltpu.VMEM((d, TILE_A), BF16),
-                pltpu.VMEM((d, TILE_A), BF16),
-                pltpu.VMEM((ff, TILE_A), F32),
-                pltpu.VMEM((ff, TILE_A), F32),
-                pltpu.VMEM((ff, TILE_A), BF16),
-                pltpu.VMEM((d, TILE_A), F32),
-                pltpu.VMEM((d, TILE_A), F32),
-                pltpu.VMEM(late_shape, F32),
-                pltpu.VMEM((3 * d + ff, BIN), F32),
-            ],
-        ),
+        in_specs=[smem, vmem, HBM, HBM] + [vmem] * len(vectors + weights),
+        out_specs=[vmem] + [HBM] * len(shapes) + [vmem] * 3,
+        scratch_shapes=[
+            pltpu.VMEM((2, BINS_A, 2 * seq, d), BF16),
+            pltpu.VMEM((2, BINS_A, 2 * BIN, d), BF16),
+            pltpu.SemaphoreType.DMA((2, BINS_A, 2, 2)),
+            *step_places(*shapes),
+            pltpu.SemaphoreType.DMA((2, 8)),
+            pltpu.VMEM((traj, BIN), jnp.int32),
+            pltpu.VMEM((16, d), F32),
+            pltpu.VMEM((12 * d, BIN), F32),
+            pltpu.VMEM((3 * d, d), BF16),
+            pltpu.VMEM((d, d), BF16),
+            pltpu.VMEM((ff, d), BF16),
+            pltpu.VMEM((d, TILE_A), F32),
+            pltpu.VMEM((d, TILE_A), BF16),
+            pltpu.VMEM((BINS_A * HEADS // 2, 2 * hs, PAIR), BF16),
+            pltpu.VMEM((BINS_A * HEADS // 2, BIN, PAIR), F32),
+            pltpu.VMEM((d, TILE_A), BF16),
+            pltpu.VMEM((d, TILE_A), F32),
+            pltpu.VMEM((d, TILE_A), BF16),
+            pltpu.VMEM((d, TILE_A), BF16),
+            pltpu.VMEM((ff, TILE_A), BF16),
+            pltpu.VMEM((ff, TILE_A), BF16),
+            pltpu.VMEM((ff, TILE_A), BF16),
+            pltpu.VMEM((d, TILE_A), F32),
+            pltpu.VMEM((d, TILE_A), F32),
+            pltpu.VMEM(late_shape, F32),
+            pltpu.VMEM((3 * d + ff, BIN), F32),
+        ],
         out_shape=[jax.ShapeDtypeStruct((d, ff), BF16)]
         + [stored(n) for n in shapes]
         + [jax.ShapeDtypeStruct(n, F32) for n in ((late_shape[0] // 2, d), (late_shape[0] // 2, d), (8, d))],
-        compiler_params=params(56),
+        compiler_params=pltpu.CompilerParams(vmem_limit_bytes=58 * MIB),
         name="forward_mlp",
     )(meta, visible_index, tokens, out_grad, *vectors, *weights)
     late = bucket_sum(bits, sums.view(late_keep), sums.view(late_send), late_shape[0] // 2, True)
@@ -1099,32 +1133,27 @@
 
     acc_shape = (-(-(3 * d + 11) // 128) * 128, d)
     send_shape = (acc_shape[0] // 2, d)
-    at = strided(0, 1, tiles_at, 1)
     grad_qkv, first_keep, first_send = pl.pallas_call(
         lambda *refs: attention_kernel(traj, *refs),
-        grid_spec=pltpu.PrefetchScalarGridSpec(
-            num_scalar_prefetch=1,
-            grid=(steps_a,),
-            in_specs=[per_step(doubled(shapes[n][0]), at) for n in ("nhat", "qkv", "prob", "gatt")] + [whole((8, d))],
-            out_specs=[per_step((3 * d, TILE_A), at)] + [whole(send_shape)] * 2,
-            scratch_shapes=[pltpu.VMEM((BINS_A * HEADS // 2, 2 * hs, PAIR), BF16)] * 2
-            + [
-                pltpu.VMEM((BINS_A * HEADS // 2, BIN, PAIR), F32),
-                pltpu.VMEM((BINS_A * HEADS // 2, BIN, PAIR), BF16),
-                pltpu.VMEM((3 * d, BIN), F32),
-                pltpu.VMEM(acc_shape, F32),
-            ],
-        ),
+        in_specs=[smem] + [HBM] * 4 + [vmem],
+        out_specs=[HBM, vmem, vmem],
+        scratch_shapes=step_places("nhat", "qkv", "prob", "gatt")
+        + [pltpu.VMEM((2, 3 * d, TILE_A), BF16), pltpu.SemaphoreType.DMA((2, 4)), pltpu.SemaphoreType.DMA((2,))]
+        + [pltpu.VMEM((BINS_A * HEADS // 2, 2 * hs, PAIR), BF16)] * 2
+        + [
+            pltpu.VMEM((BINS_A * HEADS // 2, BIN, PAIR), F32),
+            pltpu.VMEM((BINS_A * HEADS // 2, BIN, PAIR), BF16),
+            pltpu.VMEM((3 * d, BIN), F32),
+            pltpu.VMEM(acc_shape, F32),
+        ],
         out_shape=[jax.ShapeDtypeStruct((steps_a, 3 * d, TILE_A), BF16)] + [jax.ShapeDtypeStruct(send_shape, F32)] * 2,
-        compiler_params=params(56),
+        compiler_params=pltpu.CompilerParams(vmem_limit_bytes=56 * MIB),
         cost_estimate=pl.CostEstimate(flops=5 * 10**9, bytes_accessed=16 * 10**6, transcendentals=0),
         name="attention_backward",
     )(sums.ordered(meta), nhat, qkv, prob, gatt, late_vectors)
     first = bucket_sum(bits, sums.view(first_keep), sums.view(first_send), send_shape[0], False)
     sums.add("first", first)
     sums.advance(first_keep)
-
-    smem, vmem = (pl.BlockSpec(memory_space=m) for m in (pltpu.SMEM, pltpu.VMEM))
 
     def tile_places(*names):
         shapes_of = dict(shapes, gq=((3 * d, TILE), BF16))

time: 151 us -> 147 us (0.974)
  starting transfers between devices: 25.7 us -> 17.1 us
  Pallas kernels: 110 us -> 115 us
    ppermute x16, starting transfers between devices: 25.7 us -> 17.1 us  [advance(): received[key] = self.view(lax.ppermute(self.arrays[k], AXES, perm))[0]]
    pallas_call x2, Pallas kernels: 58.7 us -> 62 us  [the longest x1 45.7 us: body(): pl.pallas_call(late_kernel, in_specs=[smem, vmem, HBM, HBM] + [vmem] * le...]
    pallas_call x7 -> x6, Pallas kernels: 39.1 us -> 41.3 us  [stores(): pl.pallas_call(kernel, in_specs=[smem, vmem] + [HBM] * (len(inputs) + len...]
    pallas_call x8 -> x7, Pallas kernels: 5.05 us -> 4.46 us  [combine(): pl.pallas_call(lambda *refs: combine_kernel(step, bits_at, *refs), in_spe...]
  transfers between devices with their start and end apart: 16 -> 16, of which waited for: 9 -> 6; matrix products, arithmetic and copies ran while one was open for 0% -> 0% of each run, Pallas kernels for 36% -> 40%
where the time goes in v3:
time: 147 us
  Pallas kernels  115 us (78%)
  starting transfers between devices  17.1 us (12%)
  waiting for transfers between devices  13.5 us (9%)
    pallas_call x1, Pallas kernels, body(): pl.pallas_call(late_kernel, in_specs=[smem, vmem, HBM, HBM] + [vmem] * le...  45.7 us
    pallas_call x6, Pallas kernels, stores(): pl.pallas_call(kernel, in_specs=[smem, vmem] + [HBM] * (len(inputs) + len...  41.3 us
    ppermute x16, starting transfers between devices, advance(): received[key] = self.view(lax.ppermute(self.arrays[k], AXES, perm))[0]  17.1 us
    pallas_call x1, Pallas kernels, body(): pl.pallas_call(lambda *refs: attention_kernel(traj, *refs), in_specs=[sme...  16.3 us
    ppermute x16, waiting for transfers between devices, advance(): received[key] = self.view(lax.ppermute(self.arrays[k], AXES, perm))[0]  13.5 us
    pallas_call x7, Pallas kernels, combine(): pl.pallas_call(lambda *refs: combine_kernel(step, bits_at, *refs), in_spe...  4.46 us
    pallas_call x1, Pallas kernels, body(): pl.pallas_call(lambda *refs: finish_kernel(tiles_at + 1, rows_at, *refs),...  4.33 us
  transfers between devices with their start and end apart: 16, of which 6 were waited for; matrix products, arithmetic and copies ran while one was open for 0% of the time, Pallas kernels for 40%

profile of v3, /device:TPU:0, one launch (start us, length us, event | category | flops | bytes accessed | tf_op | source)
XLA Modules:
  0.0 146.7 jit_solution(11928789095191445598)
XLA Ops:
  0.7 2.9 %plan.1.meta_ref.refs_0_ = s32[304]{0:T(512)} custom-call(s32[64]{0:T(128)} %count_ref.1, s32[1]{0:T(128)} %bitcast.rank_ref), custom_call_target="tpu_custom_call" | custom-call | tf_op jit(solution)/shard_map/plan/pallas_call | solution.py:118
  3.5 45.7 %forward_mlp.1 = (bf16[256,1024]{1,0:T(8,128)(2,1)}, bf16[8,256,1024]{2,1,0:T(8,128)(2,1)}, f32[8,8,1024]{2,1,0:T(8,128)}, bf16[8,768,1024]{2,1,0:T(8,128)(2,1)}...) custom-call(s32[304]{0:T(512)} %plan.1.meta_ref.refs_0_, ...), custom_call_target="tpu_custom_call" | custom-call | tf_op jit(solution)/shard_map/forward_mlp/pallas_call | solution.py:1092
  49.2 0.1 collective-permute-start
  49.3 0.0 copy-start.2
  49.3 0.0 copy-start.3
  49.3 16.3 %attention_backward.1 = (bf16[8,768,1024]{2,1,0:T(8,128)(2,1)}, f32[448,256]{1,0:T(8,128)}, f32[448,256]{1,0:T(8,128)}) custom-call(s32[304]{0:T(512)} %plan.1.meta_ref.refs_0_, bf16[8,256,1024]{2,1,0:T(8,128)(2,1)} %get-tuple-element.82.refs_1_.refs_4_, bf16[8,768,1024]{2,1,0:T(8,128)(2,1)} %get-tuple-element.83.refs_2_, ...), custom_call_target="tpu_custom_call" | custom-call | flops 5000000000 | bytes 16000000 | tf_op jit(solution)/shard_map/attention_backward/pallas_call | solution.py:1136
  65.6 0.1 collective-permute-start.4
  65.7 0.0 collective-permute-done.refs_2_
  65.7 0.0 copy-done.2
  65.7 0.0 copy-done.3
  65.7 0.7 combine.7
  66.4 0.1 collective-permute-start.1
  66.5 1.6 %collective-permute-start.2 = (f32[288,256]{1,0:T(8,128)S(1)}, f32[288,256]{1,0:T(8,128)S(1)}, u32[]{:S(2)}, u32[]{:S(2)}) collective-permute-start(f32[288,256]{1,0:T(8,128)S(1)} %get-tuple-element.91), channel_id=1, source_target_pairs={{0,2},{1,3},{2,0},{3,1},{4,6},{5,7},{6,4},{7,5},{8,10},{9,11},{10,... | collective-permute-start | bytes 884744 | tf_op jit(solution)/shard_map/ppermute | solution.py:937
  68.1 1.9 %collective-permute-start.3 = (f32[288,256]{1,0:T(8,128)S(1)}, f32[288,256]{1,0:T(8,128)S(1)}, u32[]{:S(2)}, u32[]{:S(2)}) collective-permute-start(f32[288,256]{1,0:T(8,128)S(1)} %get-tuple-element.92), channel_id=1, source_target_pairs={{0,6},{1,7},{2,4},{3,5},{4,2},{5,3},{6,0},{7,1},{8,14},{9,15},{10,... | collective-permute-start | bytes 884744 | tf_op jit(solution)/shard_map/ppermute | solution.py:937
  70.0 9.2 %tokens_backward.3.refs_8_ = bf16[64,128,256]{2,1,0:T(8,128)(2,1)} custom-call(s32[304]{0:T(512)} %plan.1.meta_ref.refs_0_, bf16[256]{0:T(256)(128)(2,1)} %refs_5_.1, s32[64,112]{1,0:T(8,128)} %refs_2_.5, bf16[256,768]{1,0:T(8,128)(2,1)} %refs_7_.1, bf16[8,256,1024]{2,1,0:T(8,128)(2,1)} %get-tuple-element.82.refs_1_.refs_4_, ...), custom_call_target="tpu_custom_call" | custom-call | flops 2000000000 | bytes 8000000 | tf_op jit(solution)/shard_map/tokens_backward/pallas_call | solution.py:1164
  79.1 0.0 collective-permute-done.4.refs_6_
  79.2 0.0 collective-permute-done.1.refs_2_
  79.2 3.1 %collective-permute-done.2.refs_3_ = f32[288,256]{1,0:T(8,128)S(1)} collective-permute-done((f32[288,256]{1,0:T(8,128)S(1)}, f32[288,256]{1,0:T(8,128)S(1)}, u32[]{:S(2)}, u32[]{:S(2)}) %collective-permute-start.2) | collective-permute-done | bytes 294944 | tf_op jit(solution)/shard_map/ppermute | solution.py:937
  82.3 0.0 collective-permute-done.3.refs_4_
  82.3 0.0 copy-done.4
  82.3 0.0 copy-done.10
  82.3 0.7 combine.8
  83.0 1.7 %collective-permute-start.6 = (f32[112,256]{1,0:T(8,128)S(1)}, f32[112,256]{1,0:T(8,128)S(1)}, u32[]{:S(2)}, u32[]{:S(2)}) collective-permute-start(f32[112,256]{1,0:T(8,128)S(1)} %get-tuple-element.104), channel_id=1, source_target_pairs={{0,4},{1,5},{2,6},{3,7},{4,0},{5,1},{6,2},{7,3},{8,12},{9,13},{10,... | collective-permute-start | bytes 344072 | tf_op jit(solution)/shard_map/ppermute | solution.py:937
  84.7 0.3 collective-permute-start.7
  85.0 1.5 %collective-permute-start.8 = (f32[112,256]{1,0:T(8,128)S(1)}, f32[112,256]{1,0:T(8,128)S(1)}, u32[]{:S(2)}, u32[]{:S(2)}) collective-permute-start(f32[112,256]{1,0:T(8,128)S(1)} %get-tuple-element.106), channel_id=1, source_target_pairs={{0,6},{1,7},{2,4},{3,5},{4,2},{5,3},{6,0},{7,1},{8,14},{9,15},{10,... | collective-permute-start | bytes 344072 | tf_op jit(solution)/shard_map/ppermute | solution.py:937
  86.5 4.1 %collective-permute-start.5 = (f32[144,256]{1,0:T(8,128)S(1)}, f32[144,256]{1,0:T(8,128)S(1)}, u32[]{:S(2)}, u32[]{:S(2)}) collective-permute-start(f32[144,256]{1,0:T(8,128)S(1)} %get-tuple-element.103), channel_id=1, source_target_pairs={{0,8},{1,9},{2,10},{3,11},{4,12},{5,13},{6,14},{7,15},{8,0},{9,1},... | collective-permute-start | bytes 442376 | tf_op jit(solution)/shard_map/ppermute | solution.py:937
  90.7 4.0 %tokens_backward.4.refs_8_ = bf16[64,128,256]{2,1,0:T(8,128)(2,1)} custom-call(s32[304]{0:T(512)} %plan.1.meta_ref.refs_0_, bf16[256]{0:T(256)(128)(2,1)} %refs_5_.1, s32[64,112]{1,0:T(8,128)} %refs_2_.5, bf16[256,768]{1,0:T(8,128)(2,1)} %refs_7_.1, bf16[8,256,1024]{2,1,0:T(8,128)(2,1)} %get-tuple-element.82.refs_1_.refs_4_, ...), custom_call_target="tpu_custom_call", output_to_operand_aliasing={{}: (8, {})} | custom-call | flops 2000000000 | bytes 8000000 | tf_op jit(solution)/shard_map/tokens_backward/pallas_call | solution.py:1164
  94.6 0.0 collective-permute-done.6.refs_4_
  94.7 0.0 collective-permute-done.7.refs_5_
  94.7 0.0 collective-permute-done.8.refs_6_
  94.7 0.0 collective-permute-done.5.refs_2_
  94.7 0.0 copy-done.5
  94.7 0.6 combine.9.refs_1_
  95.3 0.0 copy-start.6
  95.3 1.6 %collective-permute-start.9 = (f32[256,256]{1,0:T(8,128)S(1)}, f32[256,256]{1,0:T(8,128)S(1)}, u32[]{:S(2)}, u32[]{:S(2)}) collective-permute-start(f32[256,256]{1,0:T(8,128)S(1)} %combine.9.refs_1_), channel_id=1, source_target_pairs={{0,16},{1,17},{2,18},{3,19},{4,20},{5,21},{6,22},{7,23},{8,24},{9,... | collective-permute-start | bytes 786440 | tf_op jit(solution)/shard_map/ppermute | solution.py:937
  96.9 7.8 %tokens_backward.5 = bf16[64,128,256]{2,1,0:T(8,128)(2,1)} custom-call(s32[304]{0:T(512)} %plan.1.meta_ref.refs_0_, bf16[256]{0:T(256)(128)(2,1)} %refs_5_.1, s32[64,112]{1,0:T(8,128)} %refs_2_.5, bf16[256,768]{1,0:T(8,128)(2,1)} %refs_7_.1, bf16[8,256,1024]{2,1,0:T(8,128)(2,1)} %get-tuple-element.82.refs_1_.refs_4_, ...), custom_call_target="tpu_custom_call", output_to_operand_aliasing={{}: (8, {})} | custom-call | flops 2000000000 | bytes 8000000 | tf_op jit(solution)/shard_map/tokens_backward/pallas_call | solution.py:1164
  104.7 4.8 %collective-permute-done.9.refs_2_ = f32[256,256]{1,0:T(8,128)S(1)} collective-permute-done((f32[256,256]{1,0:T(8,128)S(1)}, f32[256,256]{1,0:T(8,128)S(1)}, u32[]{:S(2)}, u32[]{:S(2)}) %collective-permute-start.9) | collective-permute-done | bytes 262176 | tf_op jit(solution)/shard_map/ppermute | solution.py:937
  109.5 0.0 copy-done.6
  109.5 0.6 combine.10.refs_1_
  110.1 0.1 collective-permute-start.10
  110.2 0.0 copy-start.7
  110.2 6.5 %layer_output.3.refs_5_ = bf16[64,112,256]{2,1,0:T(8,128)(2,1)} custom-call(s32[304]{0:T(512)} %plan.1.meta_ref.refs_0_, bf16[256]{0:T(256)(128)(2,1)} %refs_1_.11, bf16[256,1024]{1,0:T(8,128)(2,1)} %get-tuple-element.116.refs_2_, bf16[8,1024,1024]{2,1,0:T(8,128)(2,1)} %get-tuple-element.117.refs_3_, bf16[8,256,1024]{2,1,0:T(8,128)(2,1)} %get-tuple-element.118.refs_4_), custom_call_target="tpu_custom_call" | custom-call | flops 2000000000 | bytes 8000000 | tf_op jit(solution)/shard_map/layer_output/pallas_call | solution.py:1164
  116.7 1.7 %collective-permute-done.10.refs_2_ = f32[256,256]{1,0:T(8,128)S(1)} collective-permute-done((f32[256,256]{1,0:T(8,128)S(1)}, f32[256,256]{1,0:T(8,128)S(1)}, u32[]{:S(2)}, u32[]{:S(2)}) %collective-permute-start.10) | collective-permute-done | bytes 262176 | tf_op jit(solution)/shard_map/ppermute | solution.py:937
  118.4 0.0 copy-done.7
  118.4 0.6 combine.11
  119.0 0.1 collective-permute-start.11
  119.1 0.0 copy-start.8
  119.1 0.8 collective-permute-start.12
  119.9 5.0 %layer_output.4.refs_5_ = bf16[64,112,256]{2,1,0:T(8,128)(2,1)} custom-call(s32[304]{0:T(512)} %plan.1.meta_ref.refs_0_, bf16[256]{0:T(256)(128)(2,1)} %refs_1_.11, bf16[256,1024]{1,0:T(8,128)(2,1)} %get-tuple-element.116.refs_2_, bf16[8,1024,1024]{2,1,0:T(8,128)(2,1)} %get-tuple-element.117.refs_3_, ...), custom_call_target="tpu_custom_call", output_to_operand_aliasing={{}: (5, {})} | custom-call | flops 2000000000 | bytes 8000000 | tf_op jit(solution)/shard_map/layer_output/pallas_call | solution.py:1164
  125.0 0.3 collective-permute-done.11.refs_2_
  125.2 0.1 collective-permute-done.12.refs_4_
  125.3 0.0 copy-done.8
  125.3 0.6 combine.12
  125.9 0.5 collective-permute-start.13
  126.4 0.0 copy-start.12
  126.4 2.6 %collective-permute-start.14 = (f32[400,256]{1,0:T(8,128)S(1)}, f32[400,256]{1,0:T(8,128)S(1)}, u32[]{:S(2)}, u32[]{:S(2)}) collective-permute-start(f32[400,256]{1,0:T(8,128)S(1)} %get-tuple-element.126.refs_3_), channel_id=1, source_target_pairs={{0,2},{1,3},{2,0},{3,1},{4,6},{5,7},{6,4},{7,5},{8,10},{9,11},{10,... | collective-permute-start | bytes 1228808 | tf_op jit(solution)/shard_map/ppermute | solution.py:937
  129.0 8.8 %layer_output.5 = bf16[64,112,256]{2,1,0:T(8,128)(2,1)} custom-call(s32[304]{0:T(512)} %plan.1.meta_ref.refs_0_, bf16[256]{0:T(256)(128)(2,1)} %refs_1_.11, bf16[256,1024]{1,0:T(8,128)(2,1)} %get-tuple-element.116.refs_2_, bf16[8,1024,1024]{2,1,0:T(8,128)(2,1)} %get-tuple-element.117.refs_3_, ...), custom_call_target="tpu_custom_call", output_to_operand_aliasing={{}: (5, {})} | custom-call | flops 2000000000 | bytes 8000000 | tf_op jit(solution)/shard_map/layer_output/pallas_call | solution.py:1164
  137.9 0.0 collective-permute-done.13.refs_2_
  137.9 0.0 collective-permute-done.14.refs_4_
  137.9 0.7 combine.13.refs_1_.refs_3_
  138.6 0.1 collective-permute-start.15
  138.7 3.5 %collective-permute-done.15.refs_2_.refs_4_ = f32[1600,256]{1,0:T(8,128)S(1)} collective-permute-done((f32[1600,256]{1,0:T(8,128)S(1)}, f32[1600,256]{1,0:T(8,128)S(1)}, u32[]{:S(2)}, u32[]{:S(2)}) %collective-permute-start.15) | collective-permute-done | bytes 1638432 | tf_op jit(solution)/shard_map/ppermute | solution.py:937
  142.2 0.0 copy-done.1
  142.2 4.3 %finish.1 = (f32[1024,256]{1,0:T(8,128)}, f32[256,1024]{1,0:T(8,128)}, f32[256,256]{1,0:T(8,128)}, f32[256,768]{1,0:T(8,128)}, f32[256]{0:T(256)}, /*index=5*/f3...) custom-call(s32[304]{0:T(512)S(1)} %copy-done.9, ...), custom_call_target="tpu_custom_call" | custom-call | tf_op jit(solution)/shard_map/finish/pallas_call | solution.py:1215
  (11 shorter events, 0.0 us)
Async XLA Ops:
  49.2 16.5 %collective-permute-start = (f32[1152,256]{1,0:T(8,128)}, f32[1152,256]{1,0:T(8,128)S(1)}, u32[]{:S(2)}, u32[]{:S(2)}) collective-permute-start(f32[1152,256]{1,0:T(8,128)} %get-tuple-element.80), channel_id=1, source_target_pairs={{0,1},{1,0},{2,3},{3,2},{4,5},{5,4},{6,7},{7,6},{8,9},{9,8},{10,11... | collective-permute-start | bytes 3538952 | tf_op jit(solution)/shard_map/ppermute | solution.py:937
  49.3 16.4 %copy-start.2 = (f32[1152,256]{1,0:T(8,128)S(1)}, f32[1152,256]{1,0:T(8,128)}, u32[]{:S(2)}) copy-start(f32[1152,256]{1,0:T(8,128)} %get-tuple-element.79.refs_1_) | copy-start | bytes 3538948
  49.3 16.4 %copy-start.3 = (s32[304]{0:T(512)S(1)}, s32[304]{0:T(512)}, u32[]{:S(2)}) copy-start(s32[304]{0:T(512)} %plan.1.meta_ref.refs_0_) | copy-start | bytes 3652
  65.6 13.5 %collective-permute-start.4 = (f32[448,256]{1,0:T(8,128)}, f32[448,256]{1,0:T(8,128)S(1)}, u32[]{:S(2)}, u32[]{:S(2)}) collective-permute-start(f32[448,256]{1,0:T(8,128)} %get-tuple-element.93), channel_id=1, source_target_pairs={{0,1},{1,0},{2,3},{3,2},{4,5},{5,4},{6,7},{7,6},{8,9},{9,8},{10,11... | collective-permute-start | bytes 1376264 | tf_op jit(solution)/shard_map/ppermute | solution.py:937
  66.4 12.7 %collective-permute-start.1 = (f32[288,256]{1,0:T(8,128)S(1)}, f32[288,256]{1,0:T(8,128)S(1)}, u32[]{:S(2)}, u32[]{:S(2)}) collective-permute-start(f32[288,256]{1,0:T(8,128)S(1)} %get-tuple-element.90), channel_id=1, source_target_pairs={{0,4},{1,5},{2,6},{3,7},{4,0},{5,1},{6,2},{7,3},{8,12},{9,13},{10,... | collective-permute-start | bytes 884744 | tf_op jit(solution)/shard_map/ppermute | solution.py:937
  66.5 15.8 %collective-permute-start.2 = (f32[288,256]{1,0:T(8,128)S(1)}, f32[288,256]{1,0:T(8,128)S(1)}, u32[]{:S(2)}, u32[]{:S(2)}) collective-permute-start(f32[288,256]{1,0:T(8,128)S(1)} %get-tuple-element.91), channel_id=1, source_target_pairs={{0,2},{1,3},{2,0},{3,1},{4,6},{5,7},{6,4},{7,5},{8,10},{9,11},{10,... | collective-permute-start | bytes 884744 | tf_op jit(solution)/shard_map/ppermute | solution.py:937
  68.1 14.2 %collective-permute-start.3 = (f32[288,256]{1,0:T(8,128)S(1)}, f32[288,256]{1,0:T(8,128)S(1)}, u32[]{:S(2)}, u32[]{:S(2)}) collective-permute-start(f32[288,256]{1,0:T(8,128)S(1)} %get-tuple-element.92), channel_id=1, source_target_pairs={{0,6},{1,7},{2,4},{3,5},{4,2},{5,3},{6,0},{7,1},{8,14},{9,15},{10,... | collective-permute-start | bytes 884744 | tf_op jit(solution)/shard_map/ppermute | solution.py:937
  70.0 12.3 %copy-start.4 = (s32[304]{0:T(512)S(1)}, s32[304]{0:T(512)}, u32[]{:S(2)}) copy-start(s32[304]{0:T(512)} %plan.1.meta_ref.refs_0_) | copy-start | bytes 3652
  70.0 12.3 %copy-start.10 = (f32[448,256]{1,0:T(8,128)S(1)}, f32[448,256]{1,0:T(8,128)}, u32[]{:S(2)}) copy-start(f32[448,256]{1,0:T(8,128)} %get-tuple-element.87.refs_5_) | copy-start | bytes 1376260
  83.0 11.7 %collective-permute-start.6 = (f32[112,256]{1,0:T(8,128)S(1)}, f32[112,256]{1,0:T(8,128)S(1)}, u32[]{:S(2)}, u32[]{:S(2)}) collective-permute-start(f32[112,256]{1,0:T(8,128)S(1)} %get-tuple-element.104), channel_id=1, source_target_pairs={{0,4},{1,5},{2,6},{3,7},{4,0},{5,1},{6,2},{7,3},{8,12},{9,13},{10,... | collective-permute-start | bytes 344072 | tf_op jit(solution)/shard_map/ppermute | solution.py:937
  84.7 9.9 %collective-permute-start.7 = (f32[112,256]{1,0:T(8,128)S(1)}, f32[112,256]{1,0:T(8,128)S(1)}, u32[]{:S(2)}, u32[]{:S(2)}) collective-permute-start(f32[112,256]{1,0:T(8,128)S(1)} %get-tuple-element.105), channel_id=1, source_target_pairs={{0,2},{1,3},{2,0},{3,1},{4,6},{5,7},{6,4},{7,5},{8,10},{9,11},{10,... | collective-permute-start | bytes 344072 | tf_op jit(solution)/shard_map/ppermute | solution.py:937
  85.0 9.7 %collective-permute-start.8 = (f32[112,256]{1,0:T(8,128)S(1)}, f32[112,256]{1,0:T(8,128)S(1)}, u32[]{:S(2)}, u32[]{:S(2)}) collective-permute-start(f32[112,256]{1,0:T(8,128)S(1)} %get-tuple-element.106), channel_id=1, source_target_pairs={{0,6},{1,7},{2,4},{3,5},{4,2},{5,3},{6,0},{7,1},{8,14},{9,15},{10,... | collective-permute-start | bytes 344072 | tf_op jit(solution)/shard_map/ppermute | solution.py:937
  86.5 8.2 %copy-start.5 = (s32[304]{0:T(512)S(1)}, s32[304]{0:T(512)}, u32[]{:S(2)}) copy-start(s32[304]{0:T(512)} %plan.1.meta_ref.refs_0_) | copy-start | bytes 3652
  86.5 8.1 %collective-permute-start.5 = (f32[144,256]{1,0:T(8,128)S(1)}, f32[144,256]{1,0:T(8,128)S(1)}, u32[]{:S(2)}, u32[]{:S(2)}) collective-permute-start(f32[144,256]{1,0:T(8,128)S(1)} %get-tuple-element.103), channel_id=1, source_target_pairs={{0,8},{1,9},{2,10},{3,11},{4,12},{5,13},{6,14},{7,15},{8,0},{9,1},... | collective-permute-start | bytes 442376 | tf_op jit(solution)/shard_map/ppermute | solution.py:937
  95.3 14.2 %copy-start.6 = (s32[304]{0:T(512)S(1)}, s32[304]{0:T(512)}, u32[]{:S(2)}) copy-start(s32[304]{0:T(512)} %plan.1.meta_ref.refs_0_) | copy-start | bytes 3652
  95.3 14.2 %collective-permute-start.9 = (f32[256,256]{1,0:T(8,128)S(1)}, f32[256,256]{1,0:T(8,128)S(1)}, u32[]{:S(2)}, u32[]{:S(2)}) collective-permute-start(f32[256,256]{1,0:T(8,128)S(1)} %combine.9.refs_1_), channel_id=1, source_target_pairs={{0,16},{1,17},{2,18},{3,19},{4,20},{5,21},{6,22},{7,23},{8,24},{9,... | collective-permute-start | bytes 786440 | tf_op jit(solution)/shard_map/ppermute | solution.py:937
  110.1 8.3 %collective-permute-start.10 = (f32[256,256]{1,0:T(8,128)S(1)}, f32[256,256]{1,0:T(8,128)S(1)}, u32[]{:S(2)}, u32[]{:S(2)}) collective-permute-start(f32[256,256]{1,0:T(8,128)S(1)} %combine.10.refs_1_), channel_id=1, source_target_pairs={{0,8},{1,9},{2,10},{3,11},{4,12},{5,13},{6,14},{7,15},{8,0},{9,1},... | collective-permute-start | bytes 786440 | tf_op jit(solution)/shard_map/ppermute | solution.py:937
  110.2 8.2 %copy-start.7 = (s32[304]{0:T(512)S(1)}, s32[304]{0:T(512)}, u32[]{:S(2)}) copy-start(s32[304]{0:T(512)} %plan.1.meta_ref.refs_0_) | copy-start | bytes 3652
  119.0 6.2 %collective-permute-start.11 = (f32[200,256]{1,0:T(8,128)S(1)}, f32[200,256]{1,0:T(8,128)S(1)}, u32[]{:S(2)}, u32[]{:S(2)}) collective-permute-start(f32[200,256]{1,0:T(8,128)S(1)} %get-tuple-element.120.refs_1_), channel_id=1, source_target_pairs={{0,2},{1,3},{2,0},{3,1},{4,6},{5,7},{6,4},{7,5},{8,10},{9,11},{10,... | collective-permute-start | bytes 614408 | tf_op jit(solution)/shard_map/ppermute | solution.py:937
  119.1 6.2 %copy-start.8 = (s32[304]{0:T(512)S(1)}, s32[304]{0:T(512)}, u32[]{:S(2)}) copy-start(s32[304]{0:T(512)} %plan.1.meta_ref.refs_0_) | copy-start | bytes 3652
  119.1 6.2 %collective-permute-start.12 = (f32[200,256]{1,0:T(8,128)S(1)}, f32[200,256]{1,0:T(8,128)S(1)}, u32[]{:S(2)}, u32[]{:S(2)}) collective-permute-start(f32[200,256]{1,0:T(8,128)S(1)} %get-tuple-element.121.refs_3_), channel_id=1, source_target_pairs={{0,4},{1,5},{2,6},{3,7},{4,0},{5,1},{6,2},{7,3},{8,12},{9,13},{10,... | collective-permute-start | bytes 614408 | tf_op jit(solution)/shard_map/ppermute | solution.py:937
  125.9 12.0 %collective-permute-start.13 = (f32[400,256]{1,0:T(8,128)S(1)}, f32[400,256]{1,0:T(8,128)S(1)}, u32[]{:S(2)}, u32[]{:S(2)}) collective-permute-start(f32[400,256]{1,0:T(8,128)S(1)} %get-tuple-element.125.refs_1_), channel_id=1, source_target_pairs={{0,4},{1,5},{2,6},{3,7},{4,0},{5,1},{6,2},{7,3},{8,12},{9,13},{10,... | collective-permute-start | bytes 1228808 | tf_op jit(solution)/shard_map/ppermute | solution.py:937
  126.4 11.5 %copy-start.9 = (s32[304]{0:T(512)S(1)}, s32[304]{0:T(512)}, u32[]{:S(2)}) copy-start(s32[304]{0:T(512)} %plan.1.meta_ref.refs_0_) | copy-start | bytes 3652
  126.4 15.8 %copy-start = (bf16[256,768]{1,0:T(8,128)(2,1)S(1)}, bf16[256,768]{1,0:T(8,128)(2,1)}, u32[]{:S(2)}) copy-start(bf16[256,768]{1,0:T(8,128)(2,1)} %refs_7_.1) | copy-start | bytes 1179652
  126.4 15.8 %copy-start.1 = (bf16[256,1024]{1,0:T(8,128)(2,1)S(1)}, bf16[256,1024]{1,0:T(8,128)(2,1)}, u32[]{:S(2)}) copy-start(bf16[256,1024]{1,0:T(8,128)(2,1)} %refs_8_.1) | copy-start | bytes 1572868
  126.4 15.8 %copy-start.11 = (bf16[256]{0:T(256)(128)(2,1)S(1)}, bf16[256]{0:T(256)(128)(2,1)}, u32[]{:S(2)}) copy-start(bf16[256]{0:T(256)(128)(2,1)} %refs_5_.1) | copy-start | bytes 1540
  126.4 15.8 %copy-start.12 = (bf16[256]{0:T(256)(128)(2,1)S(1)}, bf16[256]{0:T(256)(128)(2,1)}, u32[]{:S(2)}) copy-start(bf16[256]{0:T(256)(128)(2,1)} %refs_6_.1) | copy-start | bytes 1540
  126.4 11.5 %collective-permute-start.14 = (f32[400,256]{1,0:T(8,128)S(1)}, f32[400,256]{1,0:T(8,128)S(1)}, u32[]{:S(2)}, u32[]{:S(2)}) collective-permute-start(f32[400,256]{1,0:T(8,128)S(1)} %get-tuple-element.126.refs_3_), channel_id=1, source_target_pairs={{0,2},{1,3},{2,0},{3,1},{4,6},{5,7},{6,4},{7,5},{8,10},{9,11},{10,... | collective-permute-start | bytes 1228808 | tf_op jit(solution)/shard_map/ppermute | solution.py:937
  138.6 3.6 %collective-permute-start.15 = (f32[1600,256]{1,0:T(8,128)S(1)}, f32[1600,256]{1,0:T(8,128)S(1)}, u32[]{:S(2)}, u32[]{:S(2)}) collective-permute-start(f32[1600,256]{1,0:T(8,128)S(1)} %combine.13.refs_1_.refs_3_), channel_id=1, source_target_pairs={{0,1},{1,0},{2,3},{3,2},{4,5},{5,4},{6,7},{7,6},{8,9},{9,8},{10,11... | collective-permute-start | bytes 4915208 | tf_op jit(solution)/shard_map/ppermute | solution.py:937

commit v4 on v3

--- a/solution.py
+++ b/solution.py
@@ -54,6 +54,9 @@
     def tiles(self):
         return self.ref[self.tiles_at]
 
+    def bins(self):
+        return self.ref[self.tiles_at + 15]
+
     def bit(self, b):
         return self.ref[self.tiles_at + 1 + b]
 
@@ -108,7 +111,8 @@
     for j in range(BINS_A - 1):
         meta.put(n + j, last, last, 0, 0)
     meta_ref[meta.tiles_at] = lax.shift_right_logical(n + BINS - 1, BINS.bit_length() - 1)
-    for b in range(15):
+    meta_ref[meta.tiles_at + 15] = n
+    for b in range(14):
         meta_ref[meta.tiles_at + 1 + b] = jnp.bitwise_and(lax.shift_right_logical(rank_ref[0], b), 1)
 
 
@@ -177,17 +181,13 @@
 
 def departures(meta, tile, rows_s, slot, to_ref, rows, sems, act):
     half = rows_s.shape[2] // 2
+    last = jnp.bitwise_and(meta.bins() - 1, BINS - 1)
     for b in range(BINS):
         ta, tb, ca, cb = meta.bin(tile * BINS + b)
-        for part, (t, c) in enumerate(((ta, ca), (tb, cb))):
-
-            @pl.when(c > 0)
-            def _():
-                act(
-                    pltpu.make_async_copy(
-                        rows_s.at[slot, b, pl.ds(part * half, rows)], to_ref.at[t], sems.at[slot, b, part]
-                    )
-                )
+        source = jnp.where(ca > 0, b, last)
+        for part, (t, row) in enumerate(((ta, 0), (tb, jnp.where(cb > 0, half, 0)))):
+            rows_of_t = pl.ds(pl.multiple_of(row, half) if part else 0, rows)
+            act(pltpu.make_async_copy(rows_s.at[slot, source, rows_of_t], to_ref.at[t], sems.at[slot, b, part]))
 
 
 class Share:
@@ -702,7 +702,7 @@
 
 
 def output_kernel(share, traj, meta_ref, bdn_ref, wdnt_ref, act_ref, mid_ref, *refs):
-    lay_ref, wdnt_s, act_s, mid_s, sems, col_s, y_s, rows_s, out_sems = refs[-9:]
+    lay_ref, wdnt_s, act_s, mid_s, sems, col_s, y_s, sel_s, rows_s, out_sems = refs[-10:]
     slots, d = lay_ref.shape[1:]
     meta = Meta(meta_ref, traj)
 
@@ -711,13 +711,14 @@
         col_s[...] = jnp.broadcast_to(row.T[:, 0:1], (d, BIN))
 
     def rows_of(tile, slot):
+        mlps = [mm(wdnt_s[...], act_s[slot, :, pair_lanes(t)]) for t in range(BINS // 2)]
+        for b in range(BINS):
+            sel_s[b] = bin_slots(*meta.bin(tile * BINS + b)[2:])
         for t in range(BINS // 2):
             lanes = pair_lanes(t)
-            mlp = mm(wdnt_s[...], act_s[slot, :, lanes])
-            y_s[:, lanes] = (mlp + mid_s[slot, :, lanes].astype(F32) + two(col_s[...])).astype(BF16)
+            y_s[:, lanes] = (mlps[t] + mid_s[slot, :, lanes].astype(F32) + two(col_s[...])).astype(BF16)
         for b in range(BINS):
-            _, _, ca, cb = meta.bin(tile * BINS + b)
-            rows_s[slot, b] = mm(bin_slots(ca, cb), y_s[:, bin_lanes(b)], NT).astype(BF16)
+            rows_s[slot, b] = mm(sel_s[b], y_s[:, bin_lanes(b)], NT).astype(BF16)
 
     store_tiles(
         share,
@@ -1030,8 +1031,8 @@
     return shape[:-1] + (2 * shape[-1],)
 
 
-SHARES_C = shares(0, 8, 11, 16)
-SHARES_D = shares(0, 6, 9, 16)
+SHARES_C = shares(0, 10, 16)
+SHARES_D = shares(0, 5, 8, 16)
 
 
 def body(
@@ -1189,6 +1190,8 @@
             tokens_grad,
         )
         sums.advance(tokens_grad)
+        if share is SHARES_C[0]:
+            sums.advance()
     layer_out = None
     for share in SHARES_D:
         layer_out = stores(
@@ -1200,7 +1203,7 @@
             [pltpu.VMEM((d, ff), BF16)]
             + tile_places("act", "mid")
             + [pltpu.SemaphoreType.DMA((3, 4))]
-            + [pltpu.VMEM((d, BIN), F32), pltpu.VMEM((d, TILE), BF16)],
+            + [pltpu.VMEM((d, BIN), F32), pltpu.VMEM((d, TILE), BF16), pltpu.VMEM((BINS, 2 * BIN, BIN), BF16)],
             layer_out,
         )
         sums.advance(layer_out)

time: 147 us -> 152 us (1.034)
  Pallas kernels: 115 us -> 96.9 us
  starting transfers between devices: 17.1 us -> 33.3 us
  waiting for transfers between devices: 13.5 us -> 19.8 us
    ppermute x16, starting transfers between devices: 17.1 us -> 33.3 us  [advance(): received[key] = self.view(lax.ppermute(self.arrays[k], AXES, perm))[0]]
    pallas_call x1, Pallas kernels: 45.7 us -> 37.8 us  [body(): pl.pallas_call(late_kernel, in_specs=[smem, vmem, HBM, HBM] + [vmem] * le...]
    pallas_call x6 -> x5, Pallas kernels: 41.3 us -> 33.8 us  [stores(): pl.pallas_call(kernel, in_specs=[smem, vmem] + [HBM] * (len(inputs) + len...]
    ppermute x16, waiting for transfers between devices: 13.5 us -> 19.8 us  [advance(): received[key] = self.view(lax.ppermute(self.arrays[k], AXES, perm))[0]]
    pallas_call x1, Pallas kernels: 16.3 us -> 13.7 us  [body(): pl.pallas_call(lambda *refs: attention_kernel(traj, *refs), in_specs=[sme...]
  transfers between devices with their start and end apart: 16 -> 16, of which waited for: 6 -> 8; matrix products, arithmetic and copies ran while one was open for 0% -> 0% of each run, Pallas kernels for 40% -> 32%
where the time goes in v4:
time: 152 us; the launch traced here: 151 us
  Pallas kernels  96.9 us (64%)
  starting transfers between devices  33.3 us (22%)
  waiting for transfers between devices  19.8 us (13%)
    pallas_call x1, Pallas kernels, body(): pl.pallas_call(late_kernel, in_specs=[smem, vmem, HBM, HBM] + [vmem] * le...  37.8 us
    pallas_call x5, Pallas kernels, stores(): pl.pallas_call(kernel, in_specs=[smem, vmem] + [HBM] * (len(inputs) + len...  33.8 us
    ppermute x16, starting transfers between devices, advance(): received[key] = self.view(lax.ppermute(self.arrays[k], AXES, perm))[0]  33.3 us
    ppermute x16, waiting for transfers between devices, advance(): received[key] = self.view(lax.ppermute(self.arrays[k], AXES, perm))[0]  19.8 us
    pallas_call x1, Pallas kernels, body(): pl.pallas_call(lambda *refs: attention_kernel(traj, *refs), in_specs=[sme...  13.7 us
    pallas_call x7, Pallas kernels, combine(): pl.pallas_call(lambda *refs: combine_kernel(step, bits_at, *refs), in_spe...  4.44 us
    pallas_call x1, Pallas kernels, body(): pl.pallas_call(lambda *refs: finish_kernel(tiles_at + 1, rows_at, *refs),...  4.33 us
  transfers between devices with their start and end apart: 16, of which 8 were waited for; matrix products, arithmetic and copies ran while one was open for 0% of the time, Pallas kernels for 32%

profile of v4, /device:TPU:0, one launch (start us, length us, event | category | flops | bytes accessed | tf_op | source)
XLA Modules:
  0.0 151.1 jit_solution(3560391423009868336)
XLA Ops:
  0.7 2.8 %plan.1.meta_ref.refs_0_ = s32[304]{0:T(512)} custom-call(s32[64]{0:T(128)} %count_ref.1, s32[1]{0:T(128)} %bitcast.rank_ref), custom_call_target="tpu_custom_call" | custom-call | tf_op jit(solution)/shard_map/plan/pallas_call | solution.py:122
  3.4 37.8 %forward_mlp.1 = (bf16[256,1024]{1,0:T(8,128)(2,1)}, bf16[8,256,1024]{2,1,0:T(8,128)(2,1)}, f32[8,8,1024]{2,1,0:T(8,128)}, bf16[8,768,1024]{2,1,0:T(8,128)(2,1)}...) custom-call(s32[304]{0:T(512)} %plan.1.meta_ref.refs_0_, ...), custom_call_target="tpu_custom_call" | custom-call | tf_op jit(solution)/shard_map/forward_mlp/pallas_call | solution.py:1093
  41.2 0.5 collective-permute-start
  41.8 0.0 copy-start.2
  41.8 13.7 %attention_backward.1 = (bf16[8,768,1024]{2,1,0:T(8,128)(2,1)}, f32[448,256]{1,0:T(8,128)}, f32[448,256]{1,0:T(8,128)}) custom-call(s32[304]{0:T(512)} %plan.1.meta_ref.refs_0_, bf16[8,256,1024]{2,1,0:T(8,128)(2,1)} %get-tuple-element.77.refs_1_.refs_4_, bf16[8,768,1024]{2,1,0:T(8,128)(2,1)} %get-tuple-element.78.refs_2_, ...), custom_call_target="tpu_custom_call" | custom-call | flops 5000000000 | bytes 16000000 | tf_op jit(solution)/shard_map/attention_backward/pallas_call | solution.py:1137
  55.5 0.1 collective-permute-start.4
  55.6 0.0 collective-permute-done.refs_2_
  55.6 0.0 copy-done.2
  55.6 0.0 copy-done.3
  55.6 0.7 combine.7
  56.3 13.1 %collective-permute-start.1 = (f32[288,256]{1,0:T(8,128)S(1)}, f32[288,256]{1,0:T(8,128)S(1)}, u32[]{:S(2)}, u32[]{:S(2)}) collective-permute-start(f32[288,256]{1,0:T(8,128)S(1)} %get-tuple-element.85), channel_id=1, source_target_pairs={{0,4},{1,5},{2,6},{3,7},{4,0},{5,1},{6,2},{7,3},{8,12},{9,13},{10,... | collective-permute-start | bytes 884744 | tf_op jit(solution)/shard_map/ppermute | solution.py:938
  69.4 0.0 collective-permute-start.2
  69.4 1.5 %collective-permute-start.3 = (f32[288,256]{1,0:T(8,128)S(1)}, f32[288,256]{1,0:T(8,128)S(1)}, u32[]{:S(2)}, u32[]{:S(2)}) collective-permute-start(f32[288,256]{1,0:T(8,128)S(1)} %get-tuple-element.87), channel_id=1, source_target_pairs={{0,6},{1,7},{2,4},{3,5},{4,2},{5,3},{6,0},{7,1},{8,14},{9,15},{10,... | collective-permute-start | bytes 884744 | tf_op jit(solution)/shard_map/ppermute | solution.py:938
  71.0 9.2 %tokens_backward.2.refs_8_ = bf16[64,128,256]{2,1,0:T(8,128)(2,1)} custom-call(s32[304]{0:T(512)} %plan.1.meta_ref.refs_0_, bf16[256]{0:T(256)(128)(2,1)} %refs_5_.1, s32[64,112]{1,0:T(8,128)} %refs_2_.3, bf16[256,768]{1,0:T(8,128)(2,1)} %refs_7_.1, bf16[8,256,1024]{2,1,0:T(8,128)(2,1)} %get-tuple-element.77.refs_1_.refs_4_, ...), custom_call_target="tpu_custom_call" | custom-call | flops 2000000000 | bytes 8000000 | tf_op jit(solution)/shard_map/tokens_backward/pallas_call | solution.py:1165
  80.2 0.0 collective-permute-done.4.refs_6_
  80.2 0.0 collective-permute-done.1.refs_2_
  80.2 4.6 %collective-permute-done.2.refs_3_ = f32[288,256]{1,0:T(8,128)S(1)} collective-permute-done((f32[288,256]{1,0:T(8,128)S(1)}, f32[288,256]{1,0:T(8,128)S(1)}, u32[]{:S(2)}, u32[]{:S(2)}) %collective-permute-start.2) | collective-permute-done | bytes 294944 | tf_op jit(solution)/shard_map/ppermute | solution.py:938
  84.8 0.0 collective-permute-done.3.refs_4_
  84.9 0.0 copy-done.4
  84.9 0.0 copy-done.9
  84.9 0.7 combine.8
  85.6 0.6 collective-permute-start.5
  86.1 1.7 %collective-permute-start.6 = (f32[112,256]{1,0:T(8,128)S(1)}, f32[112,256]{1,0:T(8,128)S(1)}, u32[]{:S(2)}, u32[]{:S(2)}) collective-permute-start(f32[112,256]{1,0:T(8,128)S(1)} %get-tuple-element.100), channel_id=1, source_target_pairs={{0,4},{1,5},{2,6},{3,7},{4,0},{5,1},{6,2},{7,3},{8,12},{9,13},{10,... | collective-permute-start | bytes 344072 | tf_op jit(solution)/shard_map/ppermute | solution.py:938
  87.8 0.3 collective-permute-start.7
  88.1 1.5 %collective-permute-start.8 = (f32[112,256]{1,0:T(8,128)S(1)}, f32[112,256]{1,0:T(8,128)S(1)}, u32[]{:S(2)}, u32[]{:S(2)}) collective-permute-start(f32[112,256]{1,0:T(8,128)S(1)} %get-tuple-element.102), channel_id=1, source_target_pairs={{0,6},{1,7},{2,4},{3,5},{4,2},{5,3},{6,0},{7,1},{8,14},{9,15},{10,... | collective-permute-start | bytes 344072 | tf_op jit(solution)/shard_map/ppermute | solution.py:938
  89.6 1.9 %collective-permute-done.6.refs_4_ = f32[112,256]{1,0:T(8,128)S(1)} collective-permute-done((f32[112,256]{1,0:T(8,128)S(1)}, f32[112,256]{1,0:T(8,128)S(1)}, u32[]{:S(2)}, u32[]{:S(2)}) %collective-permute-start.6) | collective-permute-done | bytes 114720 | tf_op jit(solution)/shard_map/ppermute | solution.py:938
  91.5 3.0 %collective-permute-done.7.refs_5_ = f32[112,256]{1,0:T(8,128)S(1)} collective-permute-done((f32[112,256]{1,0:T(8,128)S(1)}, f32[112,256]{1,0:T(8,128)S(1)}, u32[]{:S(2)}, u32[]{:S(2)}) %collective-permute-start.7) | collective-permute-done | bytes 114720 | tf_op jit(solution)/shard_map/ppermute | solution.py:938
  94.5 0.0 collective-permute-done.8.refs_6_
  94.5 0.0 collective-permute-done.5.refs_2_
  94.5 0.6 combine.9.refs_1_
  95.1 0.0 copy-start.5
  95.1 9.6 %collective-permute-start.9 = (f32[256,256]{1,0:T(8,128)S(1)}, f32[256,256]{1,0:T(8,128)S(1)}, u32[]{:S(2)}, u32[]{:S(2)}) collective-permute-start(f32[256,256]{1,0:T(8,128)S(1)} %combine.9.refs_1_), channel_id=1, source_target_pairs={{0,16},{1,17},{2,18},{3,19},{4,20},{5,21},{6,22},{7,23},{8,24},{9,... | collective-permute-start | bytes 786440 | tf_op jit(solution)/shard_map/ppermute | solution.py:938
  104.7 6.6 %tokens_backward.3 = bf16[64,128,256]{2,1,0:T(8,128)(2,1)} custom-call(s32[304]{0:T(512)} %plan.1.meta_ref.refs_0_, bf16[256]{0:T(256)(128)(2,1)} %refs_5_.1, s32[64,112]{1,0:T(8,128)} %refs_2_.3, bf16[256,768]{1,0:T(8,128)(2,1)} %refs_7_.1, bf16[8,256,1024]{2,1,0:T(8,128)(2,1)} %get-tuple-element.77.refs_1_.refs_4_, ...), custom_call_target="tpu_custom_call", output_to_operand_aliasing={{}: (8, {})} | custom-call | flops 2000000000 | bytes 8000000 | tf_op jit(solution)/shard_map/tokens_backward/pallas_call | solution.py:1165
  111.3 3.0 %collective-permute-done.9.refs_2_ = f32[256,256]{1,0:T(8,128)S(1)} collective-permute-done((f32[256,256]{1,0:T(8,128)S(1)}, f32[256,256]{1,0:T(8,128)S(1)}, u32[]{:S(2)}, u32[]{:S(2)}) %collective-permute-start.9) | collective-permute-done | bytes 262176 | tf_op jit(solution)/shard_map/ppermute | solution.py:938
  114.3 0.0 copy-done.5
  114.3 0.6 combine.10.refs_1_
  114.9 0.1 collective-permute-start.10
  115.0 0.0 copy-start.6
  115.0 5.3 %layer_output.3.refs_5_ = bf16[64,112,256]{2,1,0:T(8,128)(2,1)} custom-call(s32[304]{0:T(512)} %plan.1.meta_ref.refs_0_, bf16[256]{0:T(256)(128)(2,1)} %refs_1_.9, bf16[256,1024]{1,0:T(8,128)(2,1)} %get-tuple-element.106.refs_2_, bf16[8,1024,1024]{2,1,0:T(8,128)(2,1)} %get-tuple-element.107.refs_3_, bf16[8,256,1024]{2,1,0:T(8,128)(2,1)} %get-tuple-element.108.refs_4_), custom_call_target="tpu_custom_call" | custom-call | flops 2000000000 | bytes 8000000 | tf_op jit(solution)/shard_map/layer_output/pallas_call | solution.py:1165
  120.3 2.9 %collective-permute-done.10.refs_2_ = f32[256,256]{1,0:T(8,128)S(1)} collective-permute-done((f32[256,256]{1,0:T(8,128)S(1)}, f32[256,256]{1,0:T(8,128)S(1)}, u32[]{:S(2)}, u32[]{:S(2)}) %collective-permute-start.10) | collective-permute-done | bytes 262176 | tf_op jit(solution)/shard_map/ppermute | solution.py:938
  123.2 0.0 copy-done.6
  123.2 0.6 combine.11
  123.8 0.9 collective-permute-start.11
  124.7 1.1 collective-permute-start.12
  125.9 5.1 %layer_output.4.refs_5_ = bf16[64,112,256]{2,1,0:T(8,128)(2,1)} custom-call(s32[304]{0:T(512)} %plan.1.meta_ref.refs_0_, bf16[256]{0:T(256)(128)(2,1)} %refs_1_.9, bf16[256,1024]{1,0:T(8,128)(2,1)} %get-tuple-element.106.refs_2_, bf16[8,1024,1024]{2,1,0:T(8,128)(2,1)} %get-tuple-element.107.refs_3_, ...), custom_call_target="tpu_custom_call", output_to_operand_aliasing={{}: (5, {})} | custom-call | flops 2000000000 | bytes 8000000 | tf_op jit(solution)/shard_map/layer_output/pallas_call | solution.py:1165
  131.0 0.0 collective-permute-done.11.refs_2_
  131.0 0.0 collective-permute-done.12.refs_4_
  131.0 0.0 copy-done.7
  131.0 0.6 combine.12
  131.7 0.9 collective-permute-start.13
  132.6 0.0 copy-start.11
  132.6 1.2 collective-permute-start.14
  133.9 7.7 %layer_output.5 = bf16[64,112,256]{2,1,0:T(8,128)(2,1)} custom-call(s32[304]{0:T(512)} %plan.1.meta_ref.refs_0_, bf16[256]{0:T(256)(128)(2,1)} %refs_1_.9, bf16[256,1024]{1,0:T(8,128)(2,1)} %get-tuple-element.106.refs_2_, bf16[8,1024,1024]{2,1,0:T(8,128)(2,1)} %get-tuple-element.107.refs_3_, ...), custom_call_target="tpu_custom_call", output_to_operand_aliasing={{}: (5, {})} | custom-call | flops 2000000000 | bytes 8000000 | tf_op jit(solution)/shard_map/layer_output/pallas_call | solution.py:1165
  141.5 0.2 collective-permute-done.13.refs_2_
  141.7 0.7 collective-permute-done.14.refs_4_
  142.4 0.0 copy-done.8
  142.4 0.7 combine.13.refs_1_.refs_3_
  143.1 0.1 collective-permute-start.15
  143.1 3.5 %collective-permute-done.15.refs_2_.refs_4_ = f32[1600,256]{1,0:T(8,128)S(1)} collective-permute-done((f32[1600,256]{1,0:T(8,128)S(1)}, f32[1600,256]{1,0:T(8,128)S(1)}, u32[]{:S(2)}, u32[]{:S(2)}) %collective-permute-start.15) | collective-permute-done | bytes 1638432 | tf_op jit(solution)/shard_map/ppermute | solution.py:938
  146.6 0.0 copy-done
  146.6 0.0 copy-done.1
  146.6 0.0 copy-done.10
  146.6 0.0 copy-done.11
  146.6 4.3 %finish.1 = (f32[1024,256]{1,0:T(8,128)}, f32[256,1024]{1,0:T(8,128)}, f32[256,256]{1,0:T(8,128)}, f32[256,768]{1,0:T(8,128)}, f32[256]{0:T(256)}, /*index=5*/f3...) custom-call(s32[304]{0:T(512)S(1)} %copy-done.8, ...), custom_call_target="tpu_custom_call" | custom-call | tf_op jit(solution)/shard_map/finish/pallas_call | solution.py:1218
  (8 shorter events, 0.0 us)
Async XLA Ops:
  41.2 14.4 %collective-permute-start = (f32[1152,256]{1,0:T(8,128)}, f32[1152,256]{1,0:T(8,128)S(1)}, u32[]{:S(2)}, u32[]{:S(2)}) collective-permute-start(f32[1152,256]{1,0:T(8,128)} %get-tuple-element.75), channel_id=1, source_target_pairs={{0,1},{1,0},{2,3},{3,2},{4,5},{5,4},{6,7},{7,6},{8,9},{9,8},{10,11... | collective-permute-start | bytes 3538952 | tf_op jit(solution)/shard_map/ppermute | solution.py:938
  41.8 13.9 %copy-start.2 = (f32[1152,256]{1,0:T(8,128)S(1)}, f32[1152,256]{1,0:T(8,128)}, u32[]{:S(2)}) copy-start(f32[1152,256]{1,0:T(8,128)} %get-tuple-element.74.refs_1_) | copy-start | bytes 3538948
  41.8 13.9 %copy-start.3 = (s32[304]{0:T(512)S(1)}, s32[304]{0:T(512)}, u32[]{:S(2)}) copy-start(s32[304]{0:T(512)} %plan.1.meta_ref.refs_0_) | copy-start | bytes 3652
  55.5 24.7 %collective-permute-start.4 = (f32[448,256]{1,0:T(8,128)}, f32[448,256]{1,0:T(8,128)S(1)}, u32[]{:S(2)}, u32[]{:S(2)}) collective-permute-start(f32[448,256]{1,0:T(8,128)} %get-tuple-element.88), channel_id=1, source_target_pairs={{0,1},{1,0},{2,3},{3,2},{4,5},{5,4},{6,7},{7,6},{8,9},{9,8},{10,11... | collective-permute-start | bytes 1376264 | tf_op jit(solution)/shard_map/ppermute | solution.py:938
  56.3 23.9 %collective-permute-start.1 = (f32[288,256]{1,0:T(8,128)S(1)}, f32[288,256]{1,0:T(8,128)S(1)}, u32[]{:S(2)}, u32[]{:S(2)}) collective-permute-start(f32[288,256]{1,0:T(8,128)S(1)} %get-tuple-element.85), channel_id=1, source_target_pairs={{0,4},{1,5},{2,6},{3,7},{4,0},{5,1},{6,2},{7,3},{8,12},{9,13},{10,... | collective-permute-start | bytes 884744 | tf_op jit(solution)/shard_map/ppermute | solution.py:938
  69.4 15.4 %collective-permute-start.2 = (f32[288,256]{1,0:T(8,128)S(1)}, f32[288,256]{1,0:T(8,128)S(1)}, u32[]{:S(2)}, u32[]{:S(2)}) collective-permute-start(f32[288,256]{1,0:T(8,128)S(1)} %get-tuple-element.86), channel_id=1, source_target_pairs={{0,2},{1,3},{2,0},{3,1},{4,6},{5,7},{6,4},{7,5},{8,10},{9,11},{10,... | collective-permute-start | bytes 884744 | tf_op jit(solution)/shard_map/ppermute | solution.py:938
  69.4 15.4 %collective-permute-start.3 = (f32[288,256]{1,0:T(8,128)S(1)}, f32[288,256]{1,0:T(8,128)S(1)}, u32[]{:S(2)}, u32[]{:S(2)}) collective-permute-start(f32[288,256]{1,0:T(8,128)S(1)} %get-tuple-element.87), channel_id=1, source_target_pairs={{0,6},{1,7},{2,4},{3,5},{4,2},{5,3},{6,0},{7,1},{8,14},{9,15},{10,... | collective-permute-start | bytes 884744 | tf_op jit(solution)/shard_map/ppermute | solution.py:938
  71.0 13.9 %copy-start.4 = (s32[304]{0:T(512)S(1)}, s32[304]{0:T(512)}, u32[]{:S(2)}) copy-start(s32[304]{0:T(512)} %plan.1.meta_ref.refs_0_) | copy-start | bytes 3652
  71.0 13.9 %copy-start.9 = (f32[448,256]{1,0:T(8,128)S(1)}, f32[448,256]{1,0:T(8,128)}, u32[]{:S(2)}) copy-start(f32[448,256]{1,0:T(8,128)} %get-tuple-element.82.refs_5_) | copy-start | bytes 1376260
  85.6 9.0 %collective-permute-start.5 = (f32[144,256]{1,0:T(8,128)S(1)}, f32[144,256]{1,0:T(8,128)S(1)}, u32[]{:S(2)}, u32[]{:S(2)}) collective-permute-start(f32[144,256]{1,0:T(8,128)S(1)} %get-tuple-element.98), channel_id=1, source_target_pairs={{0,8},{1,9},{2,10},{3,11},{4,12},{5,13},{6,14},{7,15},{8,0},{9,1},... | collective-permute-start | bytes 442376 | tf_op jit(solution)/shard_map/ppermute | solution.py:938
  86.1 5.4 %collective-permute-start.6 = (f32[112,256]{1,0:T(8,128)S(1)}, f32[112,256]{1,0:T(8,128)S(1)}, u32[]{:S(2)}, u32[]{:S(2)}) collective-permute-start(f32[112,256]{1,0:T(8,128)S(1)} %get-tuple-element.100), channel_id=1, source_target_pairs={{0,4},{1,5},{2,6},{3,7},{4,0},{5,1},{6,2},{7,3},{8,12},{9,13},{10,... | collective-permute-start | bytes 344072 | tf_op jit(solution)/shard_map/ppermute | solution.py:938
  87.8 6.7 %collective-permute-start.7 = (f32[112,256]{1,0:T(8,128)S(1)}, f32[112,256]{1,0:T(8,128)S(1)}, u32[]{:S(2)}, u32[]{:S(2)}) collective-permute-start(f32[112,256]{1,0:T(8,128)S(1)} %get-tuple-element.101), channel_id=1, source_target_pairs={{0,2},{1,3},{2,0},{3,1},{4,6},{5,7},{6,4},{7,5},{8,10},{9,11},{10,... | collective-permute-start | bytes 344072 | tf_op jit(solution)/shard_map/ppermute | solution.py:938
  88.1 6.4 %collective-permute-start.8 = (f32[112,256]{1,0:T(8,128)S(1)}, f32[112,256]{1,0:T(8,128)S(1)}, u32[]{:S(2)}, u32[]{:S(2)}) collective-permute-start(f32[112,256]{1,0:T(8,128)S(1)} %get-tuple-element.102), channel_id=1, source_target_pairs={{0,6},{1,7},{2,4},{3,5},{4,2},{5,3},{6,0},{7,1},{8,14},{9,15},{10,... | collective-permute-start | bytes 344072 | tf_op jit(solution)/shard_map/ppermute | solution.py:938
  95.1 19.2 %copy-start.5 = (s32[304]{0:T(512)S(1)}, s32[304]{0:T(512)}, u32[]{:S(2)}) copy-start(s32[304]{0:T(512)} %plan.1.meta_ref.refs_0_) | copy-start | bytes 3652
  95.1 19.2 %collective-permute-start.9 = (f32[256,256]{1,0:T(8,128)S(1)}, f32[256,256]{1,0:T(8,128)S(1)}, u32[]{:S(2)}, u32[]{:S(2)}) collective-permute-start(f32[256,256]{1,0:T(8,128)S(1)} %combine.9.refs_1_), channel_id=1, source_target_pairs={{0,16},{1,17},{2,18},{3,19},{4,20},{5,21},{6,22},{7,23},{8,24},{9,... | collective-permute-start | bytes 786440 | tf_op jit(solution)/shard_map/ppermute | solution.py:938
  114.9 8.3 %collective-permute-start.10 = (f32[256,256]{1,0:T(8,128)S(1)}, f32[256,256]{1,0:T(8,128)S(1)}, u32[]{:S(2)}, u32[]{:S(2)}) collective-permute-start(f32[256,256]{1,0:T(8,128)S(1)} %combine.10.refs_1_), channel_id=1, source_target_pairs={{0,8},{1,9},{2,10},{3,11},{4,12},{5,13},{6,14},{7,15},{8,0},{9,1},... | collective-permute-start | bytes 786440 | tf_op jit(solution)/shard_map/ppermute | solution.py:938
  115.0 8.2 %copy-start.6 = (s32[304]{0:T(512)S(1)}, s32[304]{0:T(512)}, u32[]{:S(2)}) copy-start(s32[304]{0:T(512)} %plan.1.meta_ref.refs_0_) | copy-start | bytes 3652
  123.8 7.2 %collective-permute-start.11 = (f32[200,256]{1,0:T(8,128)S(1)}, f32[200,256]{1,0:T(8,128)S(1)}, u32[]{:S(2)}, u32[]{:S(2)}) collective-permute-start(f32[200,256]{1,0:T(8,128)S(1)} %get-tuple-element.110.refs_1_), channel_id=1, source_target_pairs={{0,2},{1,3},{2,0},{3,1},{4,6},{5,7},{6,4},{7,5},{8,10},{9,11},{10,... | collective-permute-start | bytes 614408 | tf_op jit(solution)/shard_map/ppermute | solution.py:938
  124.7 6.3 %copy-start.7 = (s32[304]{0:T(512)S(1)}, s32[304]{0:T(512)}, u32[]{:S(2)}) copy-start(s32[304]{0:T(512)} %plan.1.meta_ref.refs_0_) | copy-start | bytes 3652
  124.7 6.3 %collective-permute-start.12 = (f32[200,256]{1,0:T(8,128)S(1)}, f32[200,256]{1,0:T(8,128)S(1)}, u32[]{:S(2)}, u32[]{:S(2)}) collective-permute-start(f32[200,256]{1,0:T(8,128)S(1)} %get-tuple-element.111.refs_3_), channel_id=1, source_target_pairs={{0,4},{1,5},{2,6},{3,7},{4,0},{5,1},{6,2},{7,3},{8,12},{9,13},{10,... | collective-permute-start | bytes 614408 | tf_op jit(solution)/shard_map/ppermute | solution.py:938
  131.7 10.1 %collective-permute-start.13 = (f32[400,256]{1,0:T(8,128)S(1)}, f32[400,256]{1,0:T(8,128)S(1)}, u32[]{:S(2)}, u32[]{:S(2)}) collective-permute-start(f32[400,256]{1,0:T(8,128)S(1)} %get-tuple-element.115.refs_1_), channel_id=1, source_target_pairs={{0,4},{1,5},{2,6},{3,7},{4,0},{5,1},{6,2},{7,3},{8,12},{9,13},{10,... | collective-permute-start | bytes 1228808 | tf_op jit(solution)/shard_map/ppermute | solution.py:938
  132.6 9.8 %copy-start.8 = (s32[304]{0:T(512)S(1)}, s32[304]{0:T(512)}, u32[]{:S(2)}) copy-start(s32[304]{0:T(512)} %plan.1.meta_ref.refs_0_) | copy-start | bytes 3652
  132.6 14.0 %copy-start = (bf16[256,768]{1,0:T(8,128)(2,1)S(1)}, bf16[256,768]{1,0:T(8,128)(2,1)}, u32[]{:S(2)}) copy-start(bf16[256,768]{1,0:T(8,128)(2,1)} %refs_7_.1) | copy-start | bytes 1179652
  132.6 14.0 %copy-start.1 = (bf16[256,1024]{1,0:T(8,128)(2,1)S(1)}, bf16[256,1024]{1,0:T(8,128)(2,1)}, u32[]{:S(2)}) copy-start(bf16[256,1024]{1,0:T(8,128)(2,1)} %refs_8_.1) | copy-start | bytes 1572868
  132.6 14.0 %copy-start.10 = (bf16[256]{0:T(256)(128)(2,1)S(1)}, bf16[256]{0:T(256)(128)(2,1)}, u32[]{:S(2)}) copy-start(bf16[256]{0:T(256)(128)(2,1)} %refs_5_.1) | copy-start | bytes 1540
  132.6 14.0 %copy-start.11 = (bf16[256]{0:T(256)(128)(2,1)S(1)}, bf16[256]{0:T(256)(128)(2,1)}, u32[]{:S(2)}) copy-start(bf16[256]{0:T(256)(128)(2,1)} %refs_6_.1) | copy-start | bytes 1540
  132.6 9.8 %collective-permute-start.14 = (f32[400,256]{1,0:T(8,128)S(1)}, f32[400,256]{1,0:T(8,128)S(1)}, u32[]{:S(2)}, u32[]{:S(2)}) collective-permute-start(f32[400,256]{1,0:T(8,128)S(1)} %get-tuple-element.116.refs_3_), channel_id=1, source_target_pairs={{0,2},{1,3},{2,0},{3,1},{4,6},{5,7},{6,4},{7,5},{8,10},{9,11},{10,... | collective-permute-start | bytes 1228808 | tf_op jit(solution)/shard_map/ppermute | solution.py:938
  143.1 3.6 %collective-permute-start.15 = (f32[1600,256]{1,0:T(8,128)S(1)}, f32[1600,256]{1,0:T(8,128)S(1)}, u32[]{:S(2)}, u32[]{:S(2)}) collective-permute-start(f32[1600,256]{1,0:T(8,128)S(1)} %combine.13.refs_1_.refs_3_), channel_id=1, source_target_pairs={{0,1},{1,0},{2,3},{3,2},{4,5},{5,4},{6,7},{7,6},{8,9},{9,8},{10,11... | collective-permute-start | bytes 4915208 | tf_op jit(solution)/shard_map/ppermute | solution.py:938

commit v5 on v4

--- a/solution.py
+++ b/solution.py
@@ -179,7 +179,16 @@
     return slice(t * PAIR, (t + 1) * PAIR)
 
 
-def departures(meta, tile, rows_s, slot, to_ref, rows, sems, act):
+def wait_rows(place, rows, sem):
+    _, m, _ = place.shape
+    parts = [place.at[pl.ds(0, rows // m)]] if rows >= m else []
+    if rows % m:
+        parts.append(place.at[pl.ds(0, 1), pl.ds(0, rows % m)])
+    for part in parts:
+        pltpu.make_async_copy(part, part, sem).wait()
+
+
+def departures(meta, tile, rows_s, slot, to_ref, rows, sems):
     half = rows_s.shape[2] // 2
     last = jnp.bitwise_and(meta.bins() - 1, BINS - 1)
     for b in range(BINS):
@@ -187,7 +196,7 @@
         source = jnp.where(ca > 0, b, last)
         for part, (t, row) in enumerate(((ta, 0), (tb, jnp.where(cb > 0, half, 0)))):
             rows_of_t = pl.ds(pl.multiple_of(row, half) if part else 0, rows)
-            act(pltpu.make_async_copy(rows_s.at[slot, source, rows_of_t], to_ref.at[t], sems.at[slot, b, part]))
+            pltpu.make_async_copy(rows_s.at[slot, source, rows_of_t], to_ref.at[t], sems.at[slot]).start()
 
 
 class Share:
@@ -283,12 +292,17 @@
     meta = Meta(meta_ref, traj)
     steps = lax.shift_right_logical(meta.tiles() + 1, 1)
 
-    def arrivals(i, slot, act):
+    def arrivals(i, slot):
         for b in range(BINS_A):
             for part, t in enumerate(meta.bin(i * BINS_A + b)[0:2]):
-                sems = in_sem.at[slot, b, part]
-                act(pltpu.make_async_copy(tok_ref.at[t], tok_s.at[slot, b, pl.ds(part * seq, seq)], sems.at[0]))
-                act(pltpu.make_async_copy(og_ref.at[t], og_s.at[slot, b, pl.ds(part * BIN, slots)], sems.at[1]))
+                to_tok = tok_s.at[slot, b, pl.ds(part * seq, seq)]
+                to_og = og_s.at[slot, b, pl.ds(part * BIN, slots)]
+                pltpu.make_async_copy(tok_ref.at[t], to_tok, in_sem.at[slot, 0]).start()
+                pltpu.make_async_copy(og_ref.at[t], to_og, in_sem.at[slot, 1]).start()
+
+    def wait_arrivals(slot):
+        wait_rows(tok_s.at[slot], 2 * BINS_A * seq, in_sem.at[slot, 0])
+        wait_rows(og_s.at[slot], 2 * BINS_A * slots, in_sem.at[slot, 1])
 
     saved = (
         (nhat1_b, nhat1_hbm), (rstd1_b, rstd1_hbm), (qkv_b, qkv_hbm), (prob_b, prob_hbm),
@@ -303,7 +317,7 @@
 
     for part in range(2):
         og_s[:, :, part * BIN + slots : (part + 1) * BIN, :] = jnp.zeros((2, BINS_A, BIN - slots, d), BF16)
-    arrivals(0, 0, lambda c: c.start())
+    arrivals(0, 0)
     idx_s[...] = jnp.zeros_like(idx_s)
     idx_s[:, 0:slots] = idx_ref[...]
     vec_s[...] = jnp.zeros_like(vec_s)
@@ -330,7 +344,7 @@
 
     def work_on(step, carry):
         slot = jnp.bitwise_and(step, 1)
-        arrivals(step, slot, lambda c: c.wait())
+        wait_arrivals(slot)
 
         @pl.when(step >= 2)
         def _():
@@ -448,7 +462,7 @@
                 gelu=lambda t: [gelu(t, slice(j, j + chunk)) for j in range(0, ff, chunk)],
                 grad_second=grad_second,
             )
-            arrivals(jnp.minimum(step + 1, steps - 1), 1 - slot, lambda c: c.start())
+            arrivals(jnp.minimum(step + 1, steps - 1), 1 - slot)
             for b in bins:
                 gather(b)
             for when in range(len(tiles) + len(stages) - 1):
@@ -484,7 +498,7 @@
     for j in range(7):
         dvec_ref[j : j + 1, :] = lanes_into_rows(bacc_s[j * d : (j + 1) * d, :])
     dvec_ref[7:8, :] = jnp.zeros((1, d), F32)
-    arrivals(steps - 1, jnp.bitwise_and(steps, 1), lambda c: c.wait())
+    wait_arrivals(jnp.bitwise_and(steps, 1))
 
     @pl.when(steps >= 2)
     def _():
@@ -668,8 +682,9 @@
                 )
             )
 
-    def leave(i, act):
-        departures(meta, first + i, rows_s, jnp.bitwise_and(i, 1), to_ref, rows, out_sems, act)
+    def wait_left(i):
+        slot = jnp.bitwise_and(i, 1)
+        wait_rows(rows_s.at[slot], 2 * BINS * rows, out_sems.at[slot])
 
     constant(lambda c: c.start())
     come(first, 0, lambda c: c.start())
@@ -686,19 +701,19 @@
 
         @pl.when(i >= 2)
         def _():
-            leave(i - 2, lambda c: c.wait())
+            wait_left(i - 2)
 
         rows_of(first + i, slot)
-        leave(i, lambda c: c.start())
+        departures(meta, first + i, rows_s, slot, to_ref, rows, out_sems)
         return carry
 
     lax.fori_loop(0, done, step, 0)
 
     @pl.when(done >= 2)
     def _():
-        leave(done - 2, lambda c: c.wait())
-
-    leave(done - 1, lambda c: c.wait())
+        wait_left(done - 2)
+
+    wait_left(done - 1)
 
 
 def output_kernel(share, traj, meta_ref, bdn_ref, wdnt_ref, act_ref, mid_ref, *refs):
@@ -1097,7 +1112,7 @@
         scratch_shapes=[
             pltpu.VMEM((2, BINS_A, 2 * seq, d), BF16),
             pltpu.VMEM((2, BINS_A, 2 * BIN, d), BF16),
-            pltpu.SemaphoreType.DMA((2, BINS_A, 2, 2)),
+            pltpu.SemaphoreType.DMA((2, 2)),
             *step_places(*shapes),
             pltpu.SemaphoreType.DMA((2, 8)),
             pltpu.VMEM((traj, BIN), jnp.int32),
@@ -1167,7 +1182,7 @@
             in_specs=[smem, vmem] + [HBM] * (len(inputs) + len(given)),
             out_specs=HBM,
             scratch_shapes=scratch
-            + [pltpu.VMEM((2, BINS, 2 * BIN, d), BF16), pltpu.SemaphoreType.DMA((2, BINS, 2))],
+            + [pltpu.VMEM((2, BINS, 2 * BIN, d), BF16), pltpu.SemaphoreType.DMA((2,))],
             out_shape=jax.ShapeDtypeStruct((traj, rows, d), BF16),
             input_output_aliases={2 + len(inputs): 0} if given else {},
             compiler_params=pltpu.CompilerParams(vmem_limit_bytes=56 * MIB),

time: 152 us -> 150 us (0.987); the launches traced: 151 us -> 151 us
  transfers between devices with their start and end apart: 16 -> 16, of which waited for: 8 -> 7; matrix products, arithmetic and copies ran while one was open for 0% -> 0% of each run, Pallas kernels for 32% -> 31%
where the time goes in v5:
time: 150 us; the launch traced here: 151 us
  Pallas kernels  97 us (65%)
  starting transfers between devices  32.3 us (22%)
  waiting for transfers between devices  21.1 us (14%)
    pallas_call x1, Pallas kernels, body(): pl.pallas_call(late_kernel, in_specs=[smem, vmem, HBM, HBM] + [vmem] * le...  38.5 us
    pallas_call x5, Pallas kernels, stores(): pl.pallas_call(kernel, in_specs=[smem, vmem] + [HBM] * (len(inputs) + len...  33.2 us
    ppermute x16, starting transfers between devices, advance(): received[key] = self.view(lax.ppermute(self.arrays[k], AXES, perm))[0]  32.3 us
    ppermute x16, waiting for transfers between devices, advance(): received[key] = self.view(lax.ppermute(self.arrays[k], AXES, perm))[0]  21.1 us
    pallas_call x1, Pallas kernels, body(): pl.pallas_call(lambda *refs: attention_kernel(traj, *refs), in_specs=[sme...  13.7 us
    pallas_call x7, Pallas kernels, combine(): pl.pallas_call(lambda *refs: combine_kernel(step, bits_at, *refs), in_spe...  4.44 us
    pallas_call x1, Pallas kernels, body(): pl.pallas_call(lambda *refs: finish_kernel(tiles_at + 1, rows_at, *refs),...  4.33 us
  transfers between devices with their start and end apart: 16, of which 7 were waited for; matrix products, arithmetic and copies ran while one was open for 0% of the time, Pallas kernels for 31%

profile of v5, /device:TPU:0, one launch (start us, length us, event | category | flops | bytes accessed | tf_op | source)
XLA Modules:
  0.0 151.5 jit_solution(17004983476079374930)
XLA Ops:
  0.7 2.8 %plan.1.meta_ref.refs_0_ = s32[304]{0:T(512)} custom-call(s32[64]{0:T(128)} %count_ref.1, s32[1]{0:T(128)} %bitcast.rank_ref), custom_call_target="tpu_custom_call" | custom-call | tf_op jit(solution)/shard_map/plan/pallas_call | solution.py:122
  3.4 38.5 %forward_mlp.1 = (bf16[256,1024]{1,0:T(8,128)(2,1)}, bf16[8,256,1024]{2,1,0:T(8,128)(2,1)}, f32[8,8,1024]{2,1,0:T(8,128)}, bf16[8,768,1024]{2,1,0:T(8,128)(2,1)}...) custom-call(s32[304]{0:T(512)} %plan.1.meta_ref.refs_0_, ...), custom_call_target="tpu_custom_call" | custom-call | tf_op jit(solution)/shard_map/forward_mlp/pallas_call | solution.py:1108
  42.0 8.4 %collective-permute-start = (f32[1152,256]{1,0:T(8,128)}, f32[1152,256]{1,0:T(8,128)S(1)}, u32[]{:S(2)}, u32[]{:S(2)}) collective-permute-start(f32[1152,256]{1,0:T(8,128)} %get-tuple-element.75), channel_id=1, source_target_pairs={{0,1},{1,0},{2,3},{3,2},{4,5},{5,4},{6,7},{7,6},{8,9},{9,8},{10,11... | collective-permute-start | bytes 3538952 | tf_op jit(solution)/shard_map/ppermute | solution.py:953
  50.4 0.0 copy-start.2
  50.4 13.7 %attention_backward.1 = (bf16[8,768,1024]{2,1,0:T(8,128)(2,1)}, f32[448,256]{1,0:T(8,128)}, f32[448,256]{1,0:T(8,128)}) custom-call(s32[304]{0:T(512)} %plan.1.meta_ref.refs_0_, bf16[8,256,1024]{2,1,0:T(8,128)(2,1)} %get-tuple-element.77.refs_1_.refs_4_, bf16[8,768,1024]{2,1,0:T(8,128)(2,1)} %get-tuple-element.78.refs_2_, ...), custom_call_target="tpu_custom_call" | custom-call | flops 5000000000 | bytes 16000000 | tf_op jit(solution)/shard_map/attention_backward/pallas_call | solution.py:1152
  64.1 2.7 %collective-permute-start.4 = (f32[448,256]{1,0:T(8,128)}, f32[448,256]{1,0:T(8,128)S(1)}, u32[]{:S(2)}, u32[]{:S(2)}) collective-permute-start(f32[448,256]{1,0:T(8,128)} %get-tuple-element.88), channel_id=1, source_target_pairs={{0,1},{1,0},{2,3},{3,2},{4,5},{5,4},{6,7},{7,6},{8,9},{9,8},{10,11... | collective-permute-start | bytes 1376264 | tf_op jit(solution)/shard_map/ppermute | solution.py:953
  66.8 0.0 collective-permute-done.refs_2_
  66.8 0.0 copy-done.2
  66.8 0.0 copy-done.3
  66.8 0.7 combine.7
  67.5 0.1 collective-permute-start.1
  67.5 0.1 collective-permute-start.2
  67.6 3.4 %collective-permute-start.3 = (f32[288,256]{1,0:T(8,128)S(1)}, f32[288,256]{1,0:T(8,128)S(1)}, u32[]{:S(2)}, u32[]{:S(2)}) collective-permute-start(f32[288,256]{1,0:T(8,128)S(1)} %get-tuple-element.87), channel_id=1, source_target_pairs={{0,6},{1,7},{2,4},{3,5},{4,2},{5,3},{6,0},{7,1},{8,14},{9,15},{10,... | collective-permute-start | bytes 884744 | tf_op jit(solution)/shard_map/ppermute | solution.py:953
  71.0 9.1 %tokens_backward.2.refs_8_ = bf16[64,128,256]{2,1,0:T(8,128)(2,1)} custom-call(s32[304]{0:T(512)} %plan.1.meta_ref.refs_0_, bf16[256]{0:T(256)(128)(2,1)} %refs_5_.1, s32[64,112]{1,0:T(8,128)} %refs_2_.3, bf16[256,768]{1,0:T(8,128)(2,1)} %refs_7_.1, bf16[8,256,1024]{2,1,0:T(8,128)(2,1)} %get-tuple-element.77.refs_1_.refs_4_, ...), custom_call_target="tpu_custom_call" | custom-call | flops 2000000000 | bytes 8000000 | tf_op jit(solution)/shard_map/tokens_backward/pallas_call | solution.py:1180
  80.1 0.0 collective-permute-done.4.refs_6_
  80.1 0.0 collective-permute-done.1.refs_2_
  80.1 2.7 %collective-permute-done.2.refs_3_ = f32[288,256]{1,0:T(8,128)S(1)} collective-permute-done((f32[288,256]{1,0:T(8,128)S(1)}, f32[288,256]{1,0:T(8,128)S(1)}, u32[]{:S(2)}, u32[]{:S(2)}) %collective-permute-start.2) | collective-permute-done | bytes 294944 | tf_op jit(solution)/shard_map/ppermute | solution.py:953
  82.9 0.0 collective-permute-done.3.refs_4_
  82.9 0.0 copy-done.4
  82.9 0.0 copy-done.9
  82.9 0.7 combine.8
  83.6 9.7 %collective-permute-start.5 = (f32[144,256]{1,0:T(8,128)S(1)}, f32[144,256]{1,0:T(8,128)S(1)}, u32[]{:S(2)}, u32[]{:S(2)}) collective-permute-start(f32[144,256]{1,0:T(8,128)S(1)} %get-tuple-element.98), channel_id=1, source_target_pairs={{0,8},{1,9},{2,10},{3,11},{4,12},{5,13},{6,14},{7,15},{8,0},{9,1},... | collective-permute-start | bytes 442376 | tf_op jit(solution)/shard_map/ppermute | solution.py:953
  93.3 1.5 collective-permute-start.6
  94.8 0.7 collective-permute-start.7
  95.4 1.4 collective-permute-start.8
  96.8 1.8 %collective-permute-done.6.refs_4_ = f32[112,256]{1,0:T(8,128)S(1)} collective-permute-done((f32[112,256]{1,0:T(8,128)S(1)}, f32[112,256]{1,0:T(8,128)S(1)}, u32[]{:S(2)}, u32[]{:S(2)}) %collective-permute-start.6) | collective-permute-done | bytes 114720 | tf_op jit(solution)/shard_map/ppermute | solution.py:953
  98.6 3.0 %collective-permute-done.7.refs_5_ = f32[112,256]{1,0:T(8,128)S(1)} collective-permute-done((f32[112,256]{1,0:T(8,128)S(1)}, f32[112,256]{1,0:T(8,128)S(1)}, u32[]{:S(2)}, u32[]{:S(2)}) %collective-permute-start.7) | collective-permute-done | bytes 114720 | tf_op jit(solution)/shard_map/ppermute | solution.py:953
  101.6 0.0 collective-permute-done.8.refs_6_
  101.6 0.0 collective-permute-done.5.refs_2_
  101.6 0.6 combine.9.refs_1_
  102.2 0.0 copy-start.5
  102.2 0.1 collective-permute-start.9
  102.3 6.4 %tokens_backward.3 = bf16[64,128,256]{2,1,0:T(8,128)(2,1)} custom-call(s32[304]{0:T(512)} %plan.1.meta_ref.refs_0_, bf16[256]{0:T(256)(128)(2,1)} %refs_5_.1, s32[64,112]{1,0:T(8,128)} %refs_2_.3, bf16[256,768]{1,0:T(8,128)(2,1)} %refs_7_.1, bf16[8,256,1024]{2,1,0:T(8,128)(2,1)} %get-tuple-element.77.refs_1_.refs_4_, ...), custom_call_target="tpu_custom_call", output_to_operand_aliasing={{}: (8, {})} | custom-call | flops 2000000000 | bytes 8000000 | tf_op jit(solution)/shard_map/tokens_backward/pallas_call | solution.py:1180
  108.7 6.4 %collective-permute-done.9.refs_2_ = f32[256,256]{1,0:T(8,128)S(1)} collective-permute-done((f32[256,256]{1,0:T(8,128)S(1)}, f32[256,256]{1,0:T(8,128)S(1)}, u32[]{:S(2)}, u32[]{:S(2)}) %collective-permute-start.9) | collective-permute-done | bytes 262176 | tf_op jit(solution)/shard_map/ppermute | solution.py:953
  115.1 0.0 copy-done.5
  115.2 0.6 combine.10.refs_1_
  115.7 0.1 collective-permute-start.10
  115.8 0.0 copy-start.6
  115.8 5.1 %layer_output.3.refs_5_ = bf16[64,112,256]{2,1,0:T(8,128)(2,1)} custom-call(s32[304]{0:T(512)} %plan.1.meta_ref.refs_0_, bf16[256]{0:T(256)(128)(2,1)} %refs_1_.9, bf16[256,1024]{1,0:T(8,128)(2,1)} %get-tuple-element.106.refs_2_, bf16[8,1024,1024]{2,1,0:T(8,128)(2,1)} %get-tuple-element.107.refs_3_, bf16[8,256,1024]{2,1,0:T(8,128)(2,1)} %get-tuple-element.108.refs_4_), custom_call_target="tpu_custom_call" | custom-call | flops 2000000000 | bytes 8000000 | tf_op jit(solution)/shard_map/layer_output/pallas_call | solution.py:1180
  121.0 3.0 %collective-permute-done.10.refs_2_ = f32[256,256]{1,0:T(8,128)S(1)} collective-permute-done((f32[256,256]{1,0:T(8,128)S(1)}, f32[256,256]{1,0:T(8,128)S(1)}, u32[]{:S(2)}, u32[]{:S(2)}) %collective-permute-start.10) | collective-permute-done | bytes 262176 | tf_op jit(solution)/shard_map/ppermute | solution.py:953
  124.0 0.0 copy-done.6
  124.0 0.6 combine.11
  124.6 0.6 collective-permute-start.11
  125.2 1.4 collective-permute-start.12
  126.6 5.0 %layer_output.4.refs_5_ = bf16[64,112,256]{2,1,0:T(8,128)(2,1)} custom-call(s32[304]{0:T(512)} %plan.1.meta_ref.refs_0_, bf16[256]{0:T(256)(128)(2,1)} %refs_1_.9, bf16[256,1024]{1,0:T(8,128)(2,1)} %get-tuple-element.106.refs_2_, bf16[8,1024,1024]{2,1,0:T(8,128)(2,1)} %get-tuple-element.107.refs_3_, ...), custom_call_target="tpu_custom_call", output_to_operand_aliasing={{}: (5, {})} | custom-call | flops 2000000000 | bytes 8000000 | tf_op jit(solution)/shard_map/layer_output/pallas_call | solution.py:1180
  131.6 0.0 collective-permute-done.11.refs_2_
  131.6 0.0 collective-permute-done.12.refs_4_
  131.6 0.0 copy-done.7
  131.6 0.6 combine.12
  132.3 0.8 collective-permute-start.13
  133.0 0.0 copy-start.11
  133.1 1.4 collective-permute-start.14
  134.5 7.5 %layer_output.5 = bf16[64,112,256]{2,1,0:T(8,128)(2,1)} custom-call(s32[304]{0:T(512)} %plan.1.meta_ref.refs_0_, bf16[256]{0:T(256)(128)(2,1)} %refs_1_.9, bf16[256,1024]{1,0:T(8,128)(2,1)} %get-tuple-element.106.refs_2_, bf16[8,1024,1024]{2,1,0:T(8,128)(2,1)} %get-tuple-element.107.refs_3_, ...), custom_call_target="tpu_custom_call", output_to_operand_aliasing={{}: (5, {})} | custom-call | flops 2000000000 | bytes 8000000 | tf_op jit(solution)/shard_map/layer_output/pallas_call | solution.py:1180
  142.0 0.0 collective-permute-done.13.refs_2_
  142.1 0.7 collective-permute-done.14.refs_4_
  142.7 0.0 copy-done.8
  142.7 0.7 combine.13.refs_1_.refs_3_
  143.4 0.1 collective-permute-start.15
  143.5 3.5 %collective-permute-done.15.refs_2_.refs_4_ = f32[1600,256]{1,0:T(8,128)S(1)} collective-permute-done((f32[1600,256]{1,0:T(8,128)S(1)}, f32[1600,256]{1,0:T(8,128)S(1)}, u32[]{:S(2)}, u32[]{:S(2)}) %collective-permute-start.15) | collective-permute-done | bytes 1638432 | tf_op jit(solution)/shard_map/ppermute | solution.py:953
  147.0 0.0 copy-done
  147.0 0.0 copy-done.1
  147.0 0.0 copy-done.10
  147.0 0.0 copy-done.11
  147.0 4.3 %finish.1 = (f32[1024,256]{1,0:T(8,128)}, f32[256,1024]{1,0:T(8,128)}, f32[256,256]{1,0:T(8,128)}, f32[256,768]{1,0:T(8,128)}, f32[256]{0:T(256)}, /*index=5*/f3...) custom-call(s32[304]{0:T(512)S(1)} %copy-done.8, ...), custom_call_target="tpu_custom_call" | custom-call | tf_op jit(solution)/shard_map/finish/pallas_call | solution.py:1233
  (8 shorter events, 0.0 us)
Async XLA Ops:
  42.0 24.8 %collective-permute-start = (f32[1152,256]{1,0:T(8,128)}, f32[1152,256]{1,0:T(8,128)S(1)}, u32[]{:S(2)}, u32[]{:S(2)}) collective-permute-start(f32[1152,256]{1,0:T(8,128)} %get-tuple-element.75), channel_id=1, source_target_pairs={{0,1},{1,0},{2,3},{3,2},{4,5},{5,4},{6,7},{7,6},{8,9},{9,8},{10,11... | collective-permute-start | bytes 3538952 | tf_op jit(solution)/shard_map/ppermute | solution.py:953
  50.4 16.4 %copy-start.2 = (f32[1152,256]{1,0:T(8,128)S(1)}, f32[1152,256]{1,0:T(8,128)}, u32[]{:S(2)}) copy-start(f32[1152,256]{1,0:T(8,128)} %get-tuple-element.74.refs_1_) | copy-start | bytes 3538948
  50.4 16.4 %copy-start.3 = (s32[304]{0:T(512)S(1)}, s32[304]{0:T(512)}, u32[]{:S(2)}) copy-start(s32[304]{0:T(512)} %plan.1.meta_ref.refs_0_) | copy-start | bytes 3652
  64.1 16.1 %collective-permute-start.4 = (f32[448,256]{1,0:T(8,128)}, f32[448,256]{1,0:T(8,128)S(1)}, u32[]{:S(2)}, u32[]{:S(2)}) collective-permute-start(f32[448,256]{1,0:T(8,128)} %get-tuple-element.88), channel_id=1, source_target_pairs={{0,1},{1,0},{2,3},{3,2},{4,5},{5,4},{6,7},{7,6},{8,9},{9,8},{10,11... | collective-permute-start | bytes 1376264 | tf_op jit(solution)/shard_map/ppermute | solution.py:953
  67.5 12.7 %collective-permute-start.1 = (f32[288,256]{1,0:T(8,128)S(1)}, f32[288,256]{1,0:T(8,128)S(1)}, u32[]{:S(2)}, u32[]{:S(2)}) collective-permute-start(f32[288,256]{1,0:T(8,128)S(1)} %get-tuple-element.85), channel_id=1, source_target_pairs={{0,4},{1,5},{2,6},{3,7},{4,0},{5,1},{6,2},{7,3},{8,12},{9,13},{10,... | collective-permute-start | bytes 884744 | tf_op jit(solution)/shard_map/ppermute | solution.py:953
  67.5 15.3 %collective-permute-start.2 = (f32[288,256]{1,0:T(8,128)S(1)}, f32[288,256]{1,0:T(8,128)S(1)}, u32[]{:S(2)}, u32[]{:S(2)}) collective-permute-start(f32[288,256]{1,0:T(8,128)S(1)} %get-tuple-element.86), channel_id=1, source_target_pairs={{0,2},{1,3},{2,0},{3,1},{4,6},{5,7},{6,4},{7,5},{8,10},{9,11},{10,... | collective-permute-start | bytes 884744 | tf_op jit(solution)/shard_map/ppermute | solution.py:953
  67.6 15.3 %collective-permute-start.3 = (f32[288,256]{1,0:T(8,128)S(1)}, f32[288,256]{1,0:T(8,128)S(1)}, u32[]{:S(2)}, u32[]{:S(2)}) collective-permute-start(f32[288,256]{1,0:T(8,128)S(1)} %get-tuple-element.87), channel_id=1, source_target_pairs={{0,6},{1,7},{2,4},{3,5},{4,2},{5,3},{6,0},{7,1},{8,14},{9,15},{10,... | collective-permute-start | bytes 884744 | tf_op jit(solution)/shard_map/ppermute | solution.py:953
  71.0 11.9 %copy-start.4 = (s32[304]{0:T(512)S(1)}, s32[304]{0:T(512)}, u32[]{:S(2)}) copy-start(s32[304]{0:T(512)} %plan.1.meta_ref.refs_0_) | copy-start | bytes 3652
  71.0 11.9 %copy-start.9 = (f32[448,256]{1,0:T(8,128)S(1)}, f32[448,256]{1,0:T(8,128)}, u32[]{:S(2)}) copy-start(f32[448,256]{1,0:T(8,128)} %get-tuple-element.82.refs_5_) | copy-start | bytes 1376260
  83.6 18.0 %collective-permute-start.5 = (f32[144,256]{1,0:T(8,128)S(1)}, f32[144,256]{1,0:T(8,128)S(1)}, u32[]{:S(2)}, u32[]{:S(2)}) collective-permute-start(f32[144,256]{1,0:T(8,128)S(1)} %get-tuple-element.98), channel_id=1, source_target_pairs={{0,8},{1,9},{2,10},{3,11},{4,12},{5,13},{6,14},{7,15},{8,0},{9,1},... | collective-permute-start | bytes 442376 | tf_op jit(solution)/shard_map/ppermute | solution.py:953
  93.3 5.3 %collective-permute-start.6 = (f32[112,256]{1,0:T(8,128)S(1)}, f32[112,256]{1,0:T(8,128)S(1)}, u32[]{:S(2)}, u32[]{:S(2)}) collective-permute-start(f32[112,256]{1,0:T(8,128)S(1)} %get-tuple-element.100), channel_id=1, source_target_pairs={{0,4},{1,5},{2,6},{3,7},{4,0},{5,1},{6,2},{7,3},{8,12},{9,13},{10,... | collective-permute-start | bytes 344072 | tf_op jit(solution)/shard_map/ppermute | solution.py:953
  94.8 6.8 %collective-permute-start.7 = (f32[112,256]{1,0:T(8,128)S(1)}, f32[112,256]{1,0:T(8,128)S(1)}, u32[]{:S(2)}, u32[]{:S(2)}) collective-permute-start(f32[112,256]{1,0:T(8,128)S(1)} %get-tuple-element.101), channel_id=1, source_target_pairs={{0,2},{1,3},{2,0},{3,1},{4,6},{5,7},{6,4},{7,5},{8,10},{9,11},{10,... | collective-permute-start | bytes 344072 | tf_op jit(solution)/shard_map/ppermute | solution.py:953
  95.4 6.2 %collective-permute-start.8 = (f32[112,256]{1,0:T(8,128)S(1)}, f32[112,256]{1,0:T(8,128)S(1)}, u32[]{:S(2)}, u32[]{:S(2)}) collective-permute-start(f32[112,256]{1,0:T(8,128)S(1)} %get-tuple-element.102), channel_id=1, source_target_pairs={{0,6},{1,7},{2,4},{3,5},{4,2},{5,3},{6,0},{7,1},{8,14},{9,15},{10,... | collective-permute-start | bytes 344072 | tf_op jit(solution)/shard_map/ppermute | solution.py:953
  102.2 13.0 %copy-start.5 = (s32[304]{0:T(512)S(1)}, s32[304]{0:T(512)}, u32[]{:S(2)}) copy-start(s32[304]{0:T(512)} %plan.1.meta_ref.refs_0_) | copy-start | bytes 3652
  102.2 12.9 %collective-permute-start.9 = (f32[256,256]{1,0:T(8,128)S(1)}, f32[256,256]{1,0:T(8,128)S(1)}, u32[]{:S(2)}, u32[]{:S(2)}) collective-permute-start(f32[256,256]{1,0:T(8,128)S(1)} %combine.9.refs_1_), channel_id=1, source_target_pairs={{0,16},{1,17},{2,18},{3,19},{4,20},{5,21},{6,22},{7,23},{8,24},{9,... | collective-permute-start | bytes 786440 | tf_op jit(solution)/shard_map/ppermute | solution.py:953
  115.7 8.2 %collective-permute-start.10 = (f32[256,256]{1,0:T(8,128)S(1)}, f32[256,256]{1,0:T(8,128)S(1)}, u32[]{:S(2)}, u32[]{:S(2)}) collective-permute-start(f32[256,256]{1,0:T(8,128)S(1)} %combine.10.refs_1_), channel_id=1, source_target_pairs={{0,8},{1,9},{2,10},{3,11},{4,12},{5,13},{6,14},{7,15},{8,0},{9,1},... | collective-permute-start | bytes 786440 | tf_op jit(solution)/shard_map/ppermute | solution.py:953
  115.8 8.1 %copy-start.6 = (s32[304]{0:T(512)S(1)}, s32[304]{0:T(512)}, u32[]{:S(2)}) copy-start(s32[304]{0:T(512)} %plan.1.meta_ref.refs_0_) | copy-start | bytes 3652
  124.6 7.0 %collective-permute-start.11 = (f32[200,256]{1,0:T(8,128)S(1)}, f32[200,256]{1,0:T(8,128)S(1)}, u32[]{:S(2)}, u32[]{:S(2)}) collective-permute-start(f32[200,256]{1,0:T(8,128)S(1)} %get-tuple-element.110.refs_1_), channel_id=1, source_target_pairs={{0,2},{1,3},{2,0},{3,1},{4,6},{5,7},{6,4},{7,5},{8,10},{9,11},{10,... | collective-permute-start | bytes 614408 | tf_op jit(solution)/shard_map/ppermute | solution.py:953
  125.2 6.4 %copy-start.7 = (s32[304]{0:T(512)S(1)}, s32[304]{0:T(512)}, u32[]{:S(2)}) copy-start(s32[304]{0:T(512)} %plan.1.meta_ref.refs_0_) | copy-start | bytes 3652
  125.2 6.4 %collective-permute-start.12 = (f32[200,256]{1,0:T(8,128)S(1)}, f32[200,256]{1,0:T(8,128)S(1)}, u32[]{:S(2)}, u32[]{:S(2)}) collective-permute-start(f32[200,256]{1,0:T(8,128)S(1)} %get-tuple-element.111.refs_3_), channel_id=1, source_target_pairs={{0,4},{1,5},{2,6},{3,7},{4,0},{5,1},{6,2},{7,3},{8,12},{9,13},{10,... | collective-permute-start | bytes 614408 | tf_op jit(solution)/shard_map/ppermute | solution.py:953
  132.3 9.8 %collective-permute-start.13 = (f32[400,256]{1,0:T(8,128)S(1)}, f32[400,256]{1,0:T(8,128)S(1)}, u32[]{:S(2)}, u32[]{:S(2)}) collective-permute-start(f32[400,256]{1,0:T(8,128)S(1)} %get-tuple-element.115.refs_1_), channel_id=1, source_target_pairs={{0,4},{1,5},{2,6},{3,7},{4,0},{5,1},{6,2},{7,3},{8,12},{9,13},{10,... | collective-permute-start | bytes 1228808 | tf_op jit(solution)/shard_map/ppermute | solution.py:953
  133.0 9.7 %copy-start.8 = (s32[304]{0:T(512)S(1)}, s32[304]{0:T(512)}, u32[]{:S(2)}) copy-start(s32[304]{0:T(512)} %plan.1.meta_ref.refs_0_) | copy-start | bytes 3652
  133.0 13.9 %copy-start = (bf16[256,768]{1,0:T(8,128)(2,1)S(1)}, bf16[256,768]{1,0:T(8,128)(2,1)}, u32[]{:S(2)}) copy-start(bf16[256,768]{1,0:T(8,128)(2,1)} %refs_7_.1) | copy-start | bytes 1179652
  133.0 13.9 %copy-start.1 = (bf16[256,1024]{1,0:T(8,128)(2,1)S(1)}, bf16[256,1024]{1,0:T(8,128)(2,1)}, u32[]{:S(2)}) copy-start(bf16[256,1024]{1,0:T(8,128)(2,1)} %refs_8_.1) | copy-start | bytes 1572868
  133.0 13.9 %copy-start.10 = (bf16[256]{0:T(256)(128)(2,1)S(1)}, bf16[256]{0:T(256)(128)(2,1)}, u32[]{:S(2)}) copy-start(bf16[256]{0:T(256)(128)(2,1)} %refs_5_.1) | copy-start | bytes 1540
  133.0 13.9 %copy-start.11 = (bf16[256]{0:T(256)(128)(2,1)S(1)}, bf16[256]{0:T(256)(128)(2,1)}, u32[]{:S(2)}) copy-start(bf16[256]{0:T(256)(128)(2,1)} %refs_6_.1) | copy-start | bytes 1540
  133.1 9.7 %collective-permute-start.14 = (f32[400,256]{1,0:T(8,128)S(1)}, f32[400,256]{1,0:T(8,128)S(1)}, u32[]{:S(2)}, u32[]{:S(2)}) collective-permute-start(f32[400,256]{1,0:T(8,128)S(1)} %get-tuple-element.116.refs_3_), channel_id=1, source_target_pairs={{0,2},{1,3},{2,0},{3,1},{4,6},{5,7},{6,4},{7,5},{8,10},{9,11},{10,... | collective-permute-start | bytes 1228808 | tf_op jit(solution)/shard_map/ppermute | solution.py:953
  143.4 3.6 %collective-permute-start.15 = (f32[1600,256]{1,0:T(8,128)S(1)}, f32[1600,256]{1,0:T(8,128)S(1)}, u32[]{:S(2)}, u32[]{:S(2)}) collective-permute-start(f32[1600,256]{1,0:T(8,128)S(1)} %combine.13.refs_1_.refs_3_), channel_id=1, source_target_pairs={{0,1},{1,0},{2,3},{3,2},{4,5},{5,4},{6,7},{7,6},{8,9},{9,8},{10,11... | collective-permute-start | bytes 4915208 | tf_op jit(solution)/shard_map/ppermute | solution.py:953

commit v6 on v5

--- a/solution.py
+++ b/solution.py
@@ -1047,7 +1047,7 @@
 
 
 SHARES_C = shares(0, 10, 16)
-SHARES_D = shares(0, 5, 8, 16)
+SHARES_D = shares(0, 4, 7, 10, 16)
 
 
 def body(
@@ -1190,9 +1190,8 @@
             name=name,
         )(sums.ordered(meta), vector, *inputs, *given)
 
-    tokens_grad = None
-    for share in SHARES_C:
-        tokens_grad = stores(
+    def tokens_piece(share, earlier):
+        return stores(
             lambda *refs, share=share: token_kernel(share, *refs),
             "tokens_backward",
             ln1_gain,
@@ -1202,14 +1201,11 @@
             + tile_places("nhat", "rstd", "gq", "gmid")
             + [pltpu.SemaphoreType.DMA((3, 4))]
             + [pltpu.VMEM((traj, BIN), jnp.int32), pltpu.VMEM((d, BIN), F32), pltpu.VMEM((d, TILE), BF16)],
-            tokens_grad,
+            earlier,
         )
-        sums.advance(tokens_grad)
-        if share is SHARES_C[0]:
-            sums.advance()
-    layer_out = None
-    for share in SHARES_D:
-        layer_out = stores(
+
+    def output_piece(share, earlier):
+        return stores(
             lambda *refs, share=share: output_kernel(share, traj, *refs),
             "layer_output",
             down_bias,
@@ -1219,9 +1215,18 @@
             + tile_places("act", "mid")
             + [pltpu.SemaphoreType.DMA((3, 4))]
             + [pltpu.VMEM((d, BIN), F32), pltpu.VMEM((d, TILE), BF16), pltpu.VMEM((BINS, 2 * BIN, BIN), BF16)],
-            layer_out,
+            earlier,
         )
-        sums.advance(layer_out)
+
+    tokens_grad = layer_out = None
+    pieces = [(tokens_piece, SHARES_C[0]), (output_piece, SHARES_D[0]), (tokens_piece, SHARES_C[1])]
+    for piece, share in pieces + [(output_piece, share) for share in SHARES_D[1:]]:
+        if piece is tokens_piece:
+            tokens_grad = piece(share, tokens_grad)
+            sums.advance(tokens_grad)
+        else:
+            layer_out = piece(share, layer_out)
+            sums.advance(layer_out)
     while sums.running:
         sums.advance()
     views = sums.results["late"] + sums.results["first"]

time: 150 us -> 146 us (0.973)
  starting transfers between devices: 32.3 us -> 28 us
  waiting for transfers between devices: 21.1 us -> 17.6 us
  Pallas kernels: 97 us -> 99.5 us
    ppermute x16, starting transfers between devices: 32.3 us -> 28 us  [advance(): received[key] = self.view(lax.ppermute(self.arrays[k], AXES, perm))[0]]
    ppermute x16, waiting for transfers between devices: 21.1 us -> 17.6 us  [advance(): received[key] = self.view(lax.ppermute(self.arrays[k], AXES, perm))[0]]
    pallas_call x5 -> x6, Pallas kernels: 33.2 us -> 35.7 us  [stores(): pl.pallas_call(kernel, in_specs=[smem, vmem] + [HBM] * (len(inputs) + len...]
  transfers between devices with their start and end apart: 16 -> 16, of which waited for: 7 -> 7; matrix products, arithmetic and copies ran while one was open for 0% -> 0% of each run, Pallas kernels for 31% -> 34%
where the time goes in v6:
time: 146 us
  Pallas kernels  99.5 us (68%)
  starting transfers between devices  28 us (19%)
  waiting for transfers between devices  17.6 us (12%)
    pallas_call x1, Pallas kernels, body(): pl.pallas_call(late_kernel, in_specs=[smem, vmem, HBM, HBM] + [vmem] * le...  38.5 us
    pallas_call x6, Pallas kernels, stores(): pl.pallas_call(kernel, in_specs=[smem, vmem] + [HBM] * (len(inputs) + len...  35.7 us
    ppermute x16, starting transfers between devices, advance(): received[key] = self.view(lax.ppermute(self.arrays[k], AXES, perm))[0]  28 us
    ppermute x16, waiting for transfers between devices, advance(): received[key] = self.view(lax.ppermute(self.arrays[k], AXES, perm))[0]  17.6 us
    pallas_call x1, Pallas kernels, body(): pl.pallas_call(lambda *refs: attention_kernel(traj, *refs), in_specs=[sme...  13.7 us
    pallas_call x7, Pallas kernels, combine(): pl.pallas_call(lambda *refs: combine_kernel(step, bits_at, *refs), in_spe...  4.46 us
    pallas_call x1, Pallas kernels, body(): pl.pallas_call(lambda *refs: finish_kernel(tiles_at + 1, rows_at, *refs),...  4.33 us
  transfers between devices with their start and end apart: 16, of which 7 were waited for; matrix products, arithmetic and copies ran while one was open for 0% of the time, Pallas kernels for 34%

profile of v6, /device:TPU:0, one launch (start us, length us, event | category | flops | bytes accessed | tf_op | source)
XLA Modules:
  0.0 146.3 jit_solution(15732293652895338381)
XLA Ops:
  0.7 2.8 %plan.1.meta_ref.refs_0_ = s32[304]{0:T(512)} custom-call(s32[64]{0:T(128)} %count_ref.1, s32[1]{0:T(128)} %bitcast.rank_ref), custom_call_target="tpu_custom_call" | custom-call | tf_op jit(solution)/shard_map/plan/pallas_call | solution.py:122
  3.4 38.5 %forward_mlp.1 = (bf16[256,1024]{1,0:T(8,128)(2,1)}, bf16[8,256,1024]{2,1,0:T(8,128)(2,1)}, f32[8,8,1024]{2,1,0:T(8,128)}, bf16[8,768,1024]{2,1,0:T(8,128)(2,1)}...) custom-call(s32[304]{0:T(512)} %plan.1.meta_ref.refs_0_, ...), custom_call_target="tpu_custom_call" | custom-call | tf_op jit(solution)/shard_map/forward_mlp/pallas_call | solution.py:1108
  42.0 5.0 %collective-permute-start = (f32[1152,256]{1,0:T(8,128)}, f32[1152,256]{1,0:T(8,128)S(1)}, u32[]{:S(2)}, u32[]{:S(2)}) collective-permute-start(f32[1152,256]{1,0:T(8,128)} %get-tuple-element.80), channel_id=1, source_target_pairs={{0,1},{1,0},{2,3},{3,2},{4,5},{5,4},{6,7},{7,6},{8,9},{9,8},{10,11... | collective-permute-start | bytes 3538952 | tf_op jit(solution)/shard_map/ppermute | solution.py:953
  47.0 13.7 %attention_backward.1 = (bf16[8,768,1024]{2,1,0:T(8,128)(2,1)}, f32[448,256]{1,0:T(8,128)}, f32[448,256]{1,0:T(8,128)}) custom-call(s32[304]{0:T(512)} %plan.1.meta_ref.refs_0_, bf16[8,256,1024]{2,1,0:T(8,128)(2,1)} %get-tuple-element.82.refs_1_.refs_4_, bf16[8,768,1024]{2,1,0:T(8,128)(2,1)} %get-tuple-element.83.refs_2_, ...), custom_call_target="tpu_custom_call" | custom-call | flops 5000000000 | bytes 16000000 | tf_op jit(solution)/shard_map/attention_backward/pallas_call | solution.py:1152
  60.7 1.8 %collective-permute-start.4 = (f32[448,256]{1,0:T(8,128)}, f32[448,256]{1,0:T(8,128)S(1)}, u32[]{:S(2)}, u32[]{:S(2)}) collective-permute-start(f32[448,256]{1,0:T(8,128)} %get-tuple-element.93), channel_id=1, source_target_pairs={{0,1},{1,0},{2,3},{3,2},{4,5},{5,4},{6,7},{7,6},{8,9},{9,8},{10,11... | collective-permute-start | bytes 1376264 | tf_op jit(solution)/shard_map/ppermute | solution.py:953
  62.5 0.0 collective-permute-done.refs_2_
  62.5 0.0 copy-done.2
  62.5 0.0 copy-done.3
  62.5 0.7 combine.7
  63.2 3.1 %collective-permute-start.1 = (f32[288,256]{1,0:T(8,128)S(1)}, f32[288,256]{1,0:T(8,128)S(1)}, u32[]{:S(2)}, u32[]{:S(2)}) collective-permute-start(f32[288,256]{1,0:T(8,128)S(1)} %get-tuple-element.90), channel_id=1, source_target_pairs={{0,4},{1,5},{2,6},{3,7},{4,0},{5,1},{6,2},{7,3},{8,12},{9,13},{10,... | collective-permute-start | bytes 884744 | tf_op jit(solution)/shard_map/ppermute | solution.py:953
  66.3 3.7 %collective-permute-start.2 = (f32[288,256]{1,0:T(8,128)S(1)}, f32[288,256]{1,0:T(8,128)S(1)}, u32[]{:S(2)}, u32[]{:S(2)}) collective-permute-start(f32[288,256]{1,0:T(8,128)S(1)} %get-tuple-element.91), channel_id=1, source_target_pairs={{0,2},{1,3},{2,0},{3,1},{4,6},{5,7},{6,4},{7,5},{8,10},{9,11},{10,... | collective-permute-start | bytes 884744 | tf_op jit(solution)/shard_map/ppermute | solution.py:953
  70.0 1.4 collective-permute-start.3
  71.3 9.1 %tokens_backward.2.refs_8_ = bf16[64,128,256]{2,1,0:T(8,128)(2,1)} custom-call(s32[304]{0:T(512)} %plan.1.meta_ref.refs_0_, bf16[256]{0:T(256)(128)(2,1)} %refs_5_.1, s32[64,112]{1,0:T(8,128)} %refs_2_.3, bf16[256,768]{1,0:T(8,128)(2,1)} %refs_7_.1, bf16[8,256,1024]{2,1,0:T(8,128)(2,1)} %get-tuple-element.82.refs_1_.refs_4_, ...), custom_call_target="tpu_custom_call" | custom-call | flops 2000000000 | bytes 8000000 | tf_op jit(solution)/shard_map/tokens_backward/pallas_call | solution.py:1180
  80.4 0.0 collective-permute-done.4.refs_6_
  80.5 0.0 collective-permute-done.1.refs_2_
  80.5 2.3 %collective-permute-done.2.refs_3_ = f32[288,256]{1,0:T(8,128)S(1)} collective-permute-done((f32[288,256]{1,0:T(8,128)S(1)}, f32[288,256]{1,0:T(8,128)S(1)}, u32[]{:S(2)}, u32[]{:S(2)}) %collective-permute-start.2) | collective-permute-done | bytes 294944 | tf_op jit(solution)/shard_map/ppermute | solution.py:953
  82.7 1.8 %collective-permute-done.3.refs_4_ = f32[288,256]{1,0:T(8,128)S(1)} collective-permute-done((f32[288,256]{1,0:T(8,128)S(1)}, f32[288,256]{1,0:T(8,128)S(1)}, u32[]{:S(2)}, u32[]{:S(2)}) %collective-permute-start.3) | collective-permute-done | bytes 294944 | tf_op jit(solution)/shard_map/ppermute | solution.py:953
  84.6 0.0 copy-done.4
  84.6 0.0 copy-done.10
  84.6 0.7 combine.8
  85.3 0.6 collective-permute-start.6
  85.9 1.7 %collective-permute-start.7 = (f32[112,256]{1,0:T(8,128)S(1)}, f32[112,256]{1,0:T(8,128)S(1)}, u32[]{:S(2)}, u32[]{:S(2)}) collective-permute-start(f32[112,256]{1,0:T(8,128)S(1)} %get-tuple-element.105), channel_id=1, source_target_pairs={{0,2},{1,3},{2,0},{3,1},{4,6},{5,7},{6,4},{7,5},{8,10},{9,11},{10,... | collective-permute-start | bytes 344072 | tf_op jit(solution)/shard_map/ppermute | solution.py:953
  87.7 1.2 collective-permute-start.8
  88.8 0.0 collective-permute-start.5
  88.8 5.1 %layer_output.4.refs_5_ = bf16[64,112,256]{2,1,0:T(8,128)(2,1)} custom-call(s32[304]{0:T(512)} %plan.1.meta_ref.refs_0_, bf16[256]{0:T(256)(128)(2,1)} %refs_1_.11, bf16[256,1024]{1,0:T(8,128)(2,1)} %get-tuple-element.108.refs_2_, bf16[8,1024,1024]{2,1,0:T(8,128)(2,1)} %get-tuple-element.109.refs_3_, bf16[8,256,1024]{2,1,0:T(8,128)(2,1)} %get-tuple-element.110.refs_4_), custom_call_target="tpu_custom_call" | custom-call | flops 2000000000 | bytes 8000000 | tf_op jit(solution)/shard_map/layer_output/pallas_call | solution.py:1180
  94.0 0.0 collective-permute-done.6.refs_4_
  94.0 0.0 collective-permute-done.7.refs_5_
  94.0 0.0 collective-permute-done.8.refs_6_
  94.0 0.0 collective-permute-done.5.refs_2_
  94.0 0.0 copy-done.5
  94.0 0.6 combine.9.refs_1_
  94.6 0.0 copy-start.6
  94.7 5.2 %collective-permute-start.9 = (f32[256,256]{1,0:T(8,128)S(1)}, f32[256,256]{1,0:T(8,128)S(1)}, u32[]{:S(2)}, u32[]{:S(2)}) collective-permute-start(f32[256,256]{1,0:T(8,128)S(1)} %combine.9.refs_1_), channel_id=1, source_target_pairs={{0,16},{1,17},{2,18},{3,19},{4,20},{5,21},{6,22},{7,23},{8,24},{9,... | collective-permute-start | bytes 786440 | tf_op jit(solution)/shard_map/ppermute | solution.py:953
  99.8 6.5 %tokens_backward.3 = bf16[64,128,256]{2,1,0:T(8,128)(2,1)} custom-call(s32[304]{0:T(512)} %plan.1.meta_ref.refs_0_, bf16[256]{0:T(256)(128)(2,1)} %refs_5_.1, s32[64,112]{1,0:T(8,128)} %refs_2_.3, bf16[256,768]{1,0:T(8,128)(2,1)} %refs_7_.1, bf16[8,256,1024]{2,1,0:T(8,128)(2,1)} %get-tuple-element.82.refs_1_.refs_4_, ...), custom_call_target="tpu_custom_call", output_to_operand_aliasing={{}: (8, {})} | custom-call | flops 2000000000 | bytes 8000000 | tf_op jit(solution)/shard_map/tokens_backward/pallas_call | solution.py:1180
  106.3 3.6 %collective-permute-done.9.refs_2_ = f32[256,256]{1,0:T(8,128)S(1)} collective-permute-done((f32[256,256]{1,0:T(8,128)S(1)}, f32[256,256]{1,0:T(8,128)S(1)}, u32[]{:S(2)}, u32[]{:S(2)}) %collective-permute-start.9) | collective-permute-done | bytes 262176 | tf_op jit(solution)/shard_map/ppermute | solution.py:953
  109.9 0.0 copy-done.6
  109.9 0.6 combine.10.refs_1_
  110.5 0.0 copy-start.7
  110.5 0.1 collective-permute-start.10
  110.6 3.7 %layer_output.5.refs_5_ = bf16[64,112,256]{2,1,0:T(8,128)(2,1)} custom-call(s32[304]{0:T(512)} %plan.1.meta_ref.refs_0_, bf16[256]{0:T(256)(128)(2,1)} %refs_1_.11, bf16[256,1024]{1,0:T(8,128)(2,1)} %get-tuple-element.108.refs_2_, bf16[8,1024,1024]{2,1,0:T(8,128)(2,1)} %get-tuple-element.109.refs_3_, ...), custom_call_target="tpu_custom_call", output_to_operand_aliasing={{}: (5, {})} | custom-call | flops 2000000000 | bytes 8000000 | tf_op jit(solution)/shard_map/layer_output/pallas_call | solution.py:1180
  114.3 4.5 %collective-permute-done.10.refs_2_ = f32[256,256]{1,0:T(8,128)S(1)} collective-permute-done((f32[256,256]{1,0:T(8,128)S(1)}, f32[256,256]{1,0:T(8,128)S(1)}, u32[]{:S(2)}, u32[]{:S(2)}) %collective-permute-start.10) | collective-permute-done | bytes 262176 | tf_op jit(solution)/shard_map/ppermute | solution.py:953
  118.8 0.0 copy-done.7
  118.8 0.6 combine.11
  119.4 0.6 collective-permute-start.11
  120.0 1.5 %collective-permute-start.12 = (f32[200,256]{1,0:T(8,128)S(1)}, f32[200,256]{1,0:T(8,128)S(1)}, u32[]{:S(2)}, u32[]{:S(2)}) collective-permute-start(f32[200,256]{1,0:T(8,128)S(1)} %get-tuple-element.121.refs_3_), channel_id=1, source_target_pairs={{0,4},{1,5},{2,6},{3,7},{4,0},{5,1},{6,2},{7,3},{8,12},{9,13},{10,... | collective-permute-start | bytes 614408 | tf_op jit(solution)/shard_map/ppermute | solution.py:953
  121.5 5.0 %layer_output.6.refs_5_ = bf16[64,112,256]{2,1,0:T(8,128)(2,1)} custom-call(s32[304]{0:T(512)} %plan.1.meta_ref.refs_0_, bf16[256]{0:T(256)(128)(2,1)} %refs_1_.11, bf16[256,1024]{1,0:T(8,128)(2,1)} %get-tuple-element.108.refs_2_, bf16[8,1024,1024]{2,1,0:T(8,128)(2,1)} %get-tuple-element.109.refs_3_, ...), custom_call_target="tpu_custom_call", output_to_operand_aliasing={{}: (5, {})} | custom-call | flops 2000000000 | bytes 8000000 | tf_op jit(solution)/shard_map/layer_output/pallas_call | solution.py:1180
  126.5 0.0 collective-permute-done.11.refs_2_
  126.5 0.0 collective-permute-done.12.refs_4_
  126.5 0.0 copy-done.8
  126.5 0.6 combine.12
  127.2 0.9 collective-permute-start.13
  128.1 0.0 copy-start.12
  128.1 1.2 collective-permute-start.14
  129.3 6.3 %layer_output.7 = bf16[64,112,256]{2,1,0:T(8,128)(2,1)} custom-call(s32[304]{0:T(512)} %plan.1.meta_ref.refs_0_, bf16[256]{0:T(256)(128)(2,1)} %refs_1_.11, bf16[256,1024]{1,0:T(8,128)(2,1)} %get-tuple-element.108.refs_2_, bf16[8,1024,1024]{2,1,0:T(8,128)(2,1)} %get-tuple-element.109.refs_3_, ...), custom_call_target="tpu_custom_call", output_to_operand_aliasing={{}: (5, {})} | custom-call | flops 2000000000 | bytes 8000000 | tf_op jit(solution)/shard_map/layer_output/pallas_call | solution.py:1180
  135.6 1.6 %collective-permute-done.13.refs_2_ = f32[400,256]{1,0:T(8,128)S(1)} collective-permute-done((f32[400,256]{1,0:T(8,128)S(1)}, f32[400,256]{1,0:T(8,128)S(1)}, u32[]{:S(2)}, u32[]{:S(2)}) %collective-permute-start.13) | collective-permute-done | bytes 409632 | tf_op jit(solution)/shard_map/ppermute | solution.py:953
  137.2 0.3 collective-permute-done.14.refs_4_
  137.5 0.0 copy-done.9
  137.5 0.7 combine.13.refs_1_.refs_3_
  138.2 0.1 collective-permute-start.15
  138.3 3.5 %collective-permute-done.15.refs_2_.refs_4_ = f32[1600,256]{1,0:T(8,128)S(1)} collective-permute-done((f32[1600,256]{1,0:T(8,128)S(1)}, f32[1600,256]{1,0:T(8,128)S(1)}, u32[]{:S(2)}, u32[]{:S(2)}) %collective-permute-start.15) | collective-permute-done | bytes 1638432 | tf_op jit(solution)/shard_map/ppermute | solution.py:953
  141.8 0.0 copy-done
  141.8 0.0 copy-done.11
  141.8 0.0 copy-done.12
  141.8 4.3 %finish.1 = (f32[1024,256]{1,0:T(8,128)}, f32[256,1024]{1,0:T(8,128)}, f32[256,256]{1,0:T(8,128)}, f32[256,768]{1,0:T(8,128)}, f32[256]{0:T(256)}, /*index=5*/f3...) custom-call(s32[304]{0:T(512)S(1)} %copy-done.9, ...), custom_call_target="tpu_custom_call" | custom-call | tf_op jit(solution)/shard_map/finish/pallas_call | solution.py:1238
  (11 shorter events, 0.0 us)
Async XLA Ops:
  42.0 20.5 %collective-permute-start = (f32[1152,256]{1,0:T(8,128)}, f32[1152,256]{1,0:T(8,128)S(1)}, u32[]{:S(2)}, u32[]{:S(2)}) collective-permute-start(f32[1152,256]{1,0:T(8,128)} %get-tuple-element.80), channel_id=1, source_target_pairs={{0,1},{1,0},{2,3},{3,2},{4,5},{5,4},{6,7},{7,6},{8,9},{9,8},{10,11... | collective-permute-start | bytes 3538952 | tf_op jit(solution)/shard_map/ppermute | solution.py:953
  47.0 15.5 %copy-start.2 = (f32[1152,256]{1,0:T(8,128)S(1)}, f32[1152,256]{1,0:T(8,128)}, u32[]{:S(2)}) copy-start(f32[1152,256]{1,0:T(8,128)} %get-tuple-element.79.refs_1_) | copy-start | bytes 3538948
  47.0 15.5 %copy-start.3 = (s32[304]{0:T(512)S(1)}, s32[304]{0:T(512)}, u32[]{:S(2)}) copy-start(s32[304]{0:T(512)} %plan.1.meta_ref.refs_0_) | copy-start | bytes 3652
  60.7 19.7 %collective-permute-start.4 = (f32[448,256]{1,0:T(8,128)}, f32[448,256]{1,0:T(8,128)S(1)}, u32[]{:S(2)}, u32[]{:S(2)}) collective-permute-start(f32[448,256]{1,0:T(8,128)} %get-tuple-element.93), channel_id=1, source_target_pairs={{0,1},{1,0},{2,3},{3,2},{4,5},{5,4},{6,7},{7,6},{8,9},{9,8},{10,11... | collective-permute-start | bytes 1376264 | tf_op jit(solution)/shard_map/ppermute | solution.py:953
  63.2 17.3 %collective-permute-start.1 = (f32[288,256]{1,0:T(8,128)S(1)}, f32[288,256]{1,0:T(8,128)S(1)}, u32[]{:S(2)}, u32[]{:S(2)}) collective-permute-start(f32[288,256]{1,0:T(8,128)S(1)} %get-tuple-element.90), channel_id=1, source_target_pairs={{0,4},{1,5},{2,6},{3,7},{4,0},{5,1},{6,2},{7,3},{8,12},{9,13},{10,... | collective-permute-start | bytes 884744 | tf_op jit(solution)/shard_map/ppermute | solution.py:953
  66.3 16.5 %collective-permute-start.2 = (f32[288,256]{1,0:T(8,128)S(1)}, f32[288,256]{1,0:T(8,128)S(1)}, u32[]{:S(2)}, u32[]{:S(2)}) collective-permute-start(f32[288,256]{1,0:T(8,128)S(1)} %get-tuple-element.91), channel_id=1, source_target_pairs={{0,2},{1,3},{2,0},{3,1},{4,6},{5,7},{6,4},{7,5},{8,10},{9,11},{10,... | collective-permute-start | bytes 884744 | tf_op jit(solution)/shard_map/ppermute | solution.py:953
  70.0 14.6 %collective-permute-start.3 = (f32[288,256]{1,0:T(8,128)S(1)}, f32[288,256]{1,0:T(8,128)S(1)}, u32[]{:S(2)}, u32[]{:S(2)}) collective-permute-start(f32[288,256]{1,0:T(8,128)S(1)} %get-tuple-element.92), channel_id=1, source_target_pairs={{0,6},{1,7},{2,4},{3,5},{4,2},{5,3},{6,0},{7,1},{8,14},{9,15},{10,... | collective-permute-start | bytes 884744 | tf_op jit(solution)/shard_map/ppermute | solution.py:953
  71.3 13.2 %copy-start.4 = (s32[304]{0:T(512)S(1)}, s32[304]{0:T(512)}, u32[]{:S(2)}) copy-start(s32[304]{0:T(512)} %plan.1.meta_ref.refs_0_) | copy-start | bytes 3652
  71.3 13.2 %copy-start.10 = (f32[448,256]{1,0:T(8,128)S(1)}, f32[448,256]{1,0:T(8,128)}, u32[]{:S(2)}) copy-start(f32[448,256]{1,0:T(8,128)} %get-tuple-element.87.refs_5_) | copy-start | bytes 1376260
  85.3 8.7 %collective-permute-start.6 = (f32[112,256]{1,0:T(8,128)S(1)}, f32[112,256]{1,0:T(8,128)S(1)}, u32[]{:S(2)}, u32[]{:S(2)}) collective-permute-start(f32[112,256]{1,0:T(8,128)S(1)} %get-tuple-element.104), channel_id=1, source_target_pairs={{0,4},{1,5},{2,6},{3,7},{4,0},{5,1},{6,2},{7,3},{8,12},{9,13},{10,... | collective-permute-start | bytes 344072 | tf_op jit(solution)/shard_map/ppermute | solution.py:953
  85.9 8.1 %collective-permute-start.7 = (f32[112,256]{1,0:T(8,128)S(1)}, f32[112,256]{1,0:T(8,128)S(1)}, u32[]{:S(2)}, u32[]{:S(2)}) collective-permute-start(f32[112,256]{1,0:T(8,128)S(1)} %get-tuple-element.105), channel_id=1, source_target_pairs={{0,2},{1,3},{2,0},{3,1},{4,6},{5,7},{6,4},{7,5},{8,10},{9,11},{10,... | collective-permute-start | bytes 344072 | tf_op jit(solution)/shard_map/ppermute | solution.py:953
  87.7 6.3 %collective-permute-start.8 = (f32[112,256]{1,0:T(8,128)S(1)}, f32[112,256]{1,0:T(8,128)S(1)}, u32[]{:S(2)}, u32[]{:S(2)}) collective-permute-start(f32[112,256]{1,0:T(8,128)S(1)} %get-tuple-element.106), channel_id=1, source_target_pairs={{0,6},{1,7},{2,4},{3,5},{4,2},{5,3},{6,0},{7,1},{8,14},{9,15},{10,... | collective-permute-start | bytes 344072 | tf_op jit(solution)/shard_map/ppermute | solution.py:953
  88.8 5.2 %collective-permute-start.5 = (f32[144,256]{1,0:T(8,128)S(1)}, f32[144,256]{1,0:T(8,128)S(1)}, u32[]{:S(2)}, u32[]{:S(2)}) collective-permute-start(f32[144,256]{1,0:T(8,128)S(1)} %get-tuple-element.103), channel_id=1, source_target_pairs={{0,8},{1,9},{2,10},{3,11},{4,12},{5,13},{6,14},{7,15},{8,0},{9,1},... | collective-permute-start | bytes 442376 | tf_op jit(solution)/shard_map/ppermute | solution.py:953
  88.8 5.2 %copy-start.5 = (s32[304]{0:T(512)S(1)}, s32[304]{0:T(512)}, u32[]{:S(2)}) copy-start(s32[304]{0:T(512)} %plan.1.meta_ref.refs_0_) | copy-start | bytes 3652
  94.6 15.2 %copy-start.6 = (s32[304]{0:T(512)S(1)}, s32[304]{0:T(512)}, u32[]{:S(2)}) copy-start(s32[304]{0:T(512)} %plan.1.meta_ref.refs_0_) | copy-start | bytes 3652
  94.7 15.2 %collective-permute-start.9 = (f32[256,256]{1,0:T(8,128)S(1)}, f32[256,256]{1,0:T(8,128)S(1)}, u32[]{:S(2)}, u32[]{:S(2)}) collective-permute-start(f32[256,256]{1,0:T(8,128)S(1)} %combine.9.refs_1_), channel_id=1, source_target_pairs={{0,16},{1,17},{2,18},{3,19},{4,20},{5,21},{6,22},{7,23},{8,24},{9,... | collective-permute-start | bytes 786440 | tf_op jit(solution)/shard_map/ppermute | solution.py:953
  110.5 8.3 %copy-start.7 = (s32[304]{0:T(512)S(1)}, s32[304]{0:T(512)}, u32[]{:S(2)}) copy-start(s32[304]{0:T(512)} %plan.1.meta_ref.refs_0_) | copy-start | bytes 3652
  110.5 8.3 %collective-permute-start.10 = (f32[256,256]{1,0:T(8,128)S(1)}, f32[256,256]{1,0:T(8,128)S(1)}, u32[]{:S(2)}, u32[]{:S(2)}) collective-permute-start(f32[256,256]{1,0:T(8,128)S(1)} %combine.10.refs_1_), channel_id=1, source_target_pairs={{0,8},{1,9},{2,10},{3,11},{4,12},{5,13},{6,14},{7,15},{8,0},{9,1},... | collective-permute-start | bytes 786440 | tf_op jit(solution)/shard_map/ppermute | solution.py:953
  119.4 7.1 %collective-permute-start.11 = (f32[200,256]{1,0:T(8,128)S(1)}, f32[200,256]{1,0:T(8,128)S(1)}, u32[]{:S(2)}, u32[]{:S(2)}) collective-permute-start(f32[200,256]{1,0:T(8,128)S(1)} %get-tuple-element.120.refs_1_), channel_id=1, source_target_pairs={{0,2},{1,3},{2,0},{3,1},{4,6},{5,7},{6,4},{7,5},{8,10},{9,11},{10,... | collective-permute-start | bytes 614408 | tf_op jit(solution)/shard_map/ppermute | solution.py:953
  120.0 6.5 %copy-start.8 = (s32[304]{0:T(512)S(1)}, s32[304]{0:T(512)}, u32[]{:S(2)}) copy-start(s32[304]{0:T(512)} %plan.1.meta_ref.refs_0_) | copy-start | bytes 3652
  120.0 6.5 %collective-permute-start.12 = (f32[200,256]{1,0:T(8,128)S(1)}, f32[200,256]{1,0:T(8,128)S(1)}, u32[]{:S(2)}, u32[]{:S(2)}) collective-permute-start(f32[200,256]{1,0:T(8,128)S(1)} %get-tuple-element.121.refs_3_), channel_id=1, source_target_pairs={{0,4},{1,5},{2,6},{3,7},{4,0},{5,1},{6,2},{7,3},{8,12},{9,13},{10,... | collective-permute-start | bytes 614408 | tf_op jit(solution)/shard_map/ppermute | solution.py:953
  127.2 10.1 %collective-permute-start.13 = (f32[400,256]{1,0:T(8,128)S(1)}, f32[400,256]{1,0:T(8,128)S(1)}, u32[]{:S(2)}, u32[]{:S(2)}) collective-permute-start(f32[400,256]{1,0:T(8,128)S(1)} %get-tuple-element.125.refs_1_), channel_id=1, source_target_pairs={{0,4},{1,5},{2,6},{3,7},{4,0},{5,1},{6,2},{7,3},{8,12},{9,13},{10,... | collective-permute-start | bytes 1228808 | tf_op jit(solution)/shard_map/ppermute | solution.py:953
  128.1 9.5 %copy-start.9 = (s32[304]{0:T(512)S(1)}, s32[304]{0:T(512)}, u32[]{:S(2)}) copy-start(s32[304]{0:T(512)} %plan.1.meta_ref.refs_0_) | copy-start | bytes 3652
  128.1 13.7 %copy-start = (bf16[256,768]{1,0:T(8,128)(2,1)S(1)}, bf16[256,768]{1,0:T(8,128)(2,1)}, u32[]{:S(2)}) copy-start(bf16[256,768]{1,0:T(8,128)(2,1)} %refs_7_.1) | copy-start | bytes 1179652
  128.1 13.7 %copy-start.1 = (bf16[256,1024]{1,0:T(8,128)(2,1)S(1)}, bf16[256,1024]{1,0:T(8,128)(2,1)}, u32[]{:S(2)}) copy-start(bf16[256,1024]{1,0:T(8,128)(2,1)} %refs_8_.1) | copy-start | bytes 1572868
  128.1 13.7 %copy-start.11 = (bf16[256]{0:T(256)(128)(2,1)S(1)}, bf16[256]{0:T(256)(128)(2,1)}, u32[]{:S(2)}) copy-start(bf16[256]{0:T(256)(128)(2,1)} %refs_5_.1) | copy-start | bytes 1540
  128.1 13.7 %copy-start.12 = (bf16[256]{0:T(256)(128)(2,1)S(1)}, bf16[256]{0:T(256)(128)(2,1)}, u32[]{:S(2)}) copy-start(bf16[256]{0:T(256)(128)(2,1)} %refs_6_.1) | copy-start | bytes 1540
  128.1 9.4 %collective-permute-start.14 = (f32[400,256]{1,0:T(8,128)S(1)}, f32[400,256]{1,0:T(8,128)S(1)}, u32[]{:S(2)}, u32[]{:S(2)}) collective-permute-start(f32[400,256]{1,0:T(8,128)S(1)} %get-tuple-element.126.refs_3_), channel_id=1, source_target_pairs={{0,2},{1,3},{2,0},{3,1},{4,6},{5,7},{6,4},{7,5},{8,10},{9,11},{10,... | collective-permute-start | bytes 1228808 | tf_op jit(solution)/shard_map/ppermute | solution.py:953
  138.2 3.6 %collective-permute-start.15 = (f32[1600,256]{1,0:T(8,128)S(1)}, f32[1600,256]{1,0:T(8,128)S(1)}, u32[]{:S(2)}, u32[]{:S(2)}) collective-permute-start(f32[1600,256]{1,0:T(8,128)S(1)} %combine.13.refs_1_.refs_3_), channel_id=1, source_target_pairs={{0,1},{1,0},{2,3},{3,2},{4,5},{5,4},{6,7},{7,6},{8,9},{9,8},{10,11... | collective-permute-start | bytes 4915208 | tf_op jit(solution)/shard_map/ppermute | solution.py:953
